TPU v7x, 32 devices: a whole 2x2x4 slice. The times are simulated.
32 devices in a mesh: order: 8 (over z, x), blk: 4 (over y, core).
Axes of the slice: x: 2, y: 2, z: 4, core: 2. Of those that a mesh axis runs over, the one named last changes fastest.
Arguments:
- fourier_cycles: float32 [16, 128, 128], P('order', 'blk'), parts along dimension 0, may hold values from -6 to 6
- legendre: float32 [16, 128, 12288], P('order', 'blk'), parts along dimension 0, may hold values from -0.5 to 0.5
- cycle_weight: float32 [128], P('blk'), may hold values from 0.5 to 2
- matched_filter_weights: float32 [12288, 8, 8], P('blk'), may hold values from -2 to 2
- cluster_cycles: int32 [16, 64], P('order'), parts along dimension 0, may hold values from 0 to 127
- cluster_flux: float32 [16, 64, 128], P('order'), parts along dimension 0, may hold values from -18 to 18
- order_per_slot: int32 [16], P('order'), parts along dimension 0, may hold values from 0 to 6143
Outputs:
- synthesized: float32 [16, 128, 128], P('order', 'blk'), parts along dimension 0
There are 8 independent parts, one for each index of `order`. A program takes and returns all parts, laid end to end along the dimension named above; an argument that names none is the same for every part. Nothing has to cross between parts.
Inputs may be any that keep to these rules, and one draw needn't show every extreme that they name: `cluster_cycles`: cycle indices; several clusters may share a cycle, and their coefficients add. `order_per_slot`: order of each slot; degrees below it carry no coefficients.
All inputs are finite; a program needn't handle non-finite values.
Results may differ from a plain program's by a relative error of at most 0.00011.
Values sent between devices are 32-bit elements; how exact they have to be, the bound alone decides.
No kernel may reach another device: no remote copies, remote signals or barrier semaphores. Data moves between devices by JAX's collectives and lax.ppermute only.
A program may use at most 192 MiB of HBM per device.

v0:
```python
import jax
import jax.numpy as jnp
from jax import lax
from jax.sharding import PartitionSpec as P

L = 12288
F = 8
S = 8
SIMS = 8
M = 2


highest_degree = lax.Precision.HIGHEST


def inject(fourier_cycles, cycle_weight, cluster_cycles, cluster_flux):
    local = fourier_cycles.shape[1]
    cycle_ids = lax.axis_index("blk") * local + lax.iota(jnp.int32, local)
    cycle_hits = (cycle_ids[None, :, None] == cluster_cycles[:, None, :]).astype(jnp.float32)
    added = jnp.einsum("krj,kjc->krc", cycle_hits, cluster_flux, precision=highest_degree)
    return cycle_weight[None, :, None] * (fourier_cycles + added)


def finish(owned, matched_filter_weights, order_per_slot):
    blocks = owned.shape[0]
    degrees = lax.axis_index("blk") * blocks + lax.iota(jnp.int32, blocks)
    harmonics = owned.reshape(blocks, M, 2 * F * SIMS)
    kept_mask = (degrees[:, None] >= order_per_slot[None, :]).astype(jnp.float32)
    masked_values = (harmonics * kept_mask[:, :, None]).reshape(blocks, M, 2, F, SIMS)
    matched_output = jnp.einsum(
        "dvr,dotrq->dotvq", matched_filter_weights, masked_values, precision=highest_degree
    )
    squares = jnp.sum(matched_filter_weights * matched_filter_weights, axis=2)
    weights = kept_mask * (2.0 * degrees.astype(jnp.float32) + 1.0)[:, None]
    response = jnp.einsum("lk,ls->ks", weights, squares, precision=highest_degree)
    response = lax.psum(response, "blk")
    scaled = matched_output * (L / jnp.sqrt(response))[None, :, None, :, None]
    return scaled.reshape(blocks, M, 2 * S * SIMS)


def body(
    fourier_cycles,
    legendre,
    cycle_weight,
    matched_filter_weights,
    cluster_cycles,
    cluster_flux,
    order_per_slot,
):
    injected = inject(fourier_cycles, cycle_weight, cluster_cycles, cluster_flux)
    orders_here = legendre.shape[0]
    local = legendre.shape[1]
    width = injected.shape[2]
    out_width = 2 * S * SIMS
    blocks = legendre.shape[2] // lax.axis_size("blk")
    owned_table = lax.all_to_all(legendre, "blk", split_axis=2, concat_axis=1, tiled=True)
    all_cycles = lax.all_gather(injected, "blk", axis=1, tiled=True)
    harmonics = jnp.einsum("krl,krc->lkc", owned_table, all_cycles, precision=highest_degree)
    scaled = finish(
        harmonics.reshape(blocks, orders_here * width), matched_filter_weights, order_per_slot
    )
    partial_running_sum = jnp.einsum("krl,lkc->rkc", owned_table, scaled, precision=highest_degree)
    flat = lax.psum_scatter(
        partial_running_sum.reshape(local * lax.axis_size("blk"), orders_here * out_width),
        "blk",
        scatter_dimension=0,
        tiled=True,
    )
    result = jnp.transpose(flat.reshape(local, orders_here, out_width), (1, 0, 2))
    return result


def solution(mesh):
    return jax.shard_map(
        body,
        mesh=mesh,
        in_specs=(
            P("order", "blk", None),
            P("order", "blk", None),
            P("blk"),
            P("blk", None, None),
            P("order", None),
            P("order", None, None),
            P("order"),
        ),
        out_specs=P("order", "blk", None),
        check_vma=False,
    )
```

profile of v0, /device:TPU:1, one launch (start us, length us, event | category | flops | bytes accessed | tf_op | source)
XLA Modules:
  0.0 274.9 jit_solution(2757774311156553836)
XLA Ops:
  6.5 0.0 copy-start
  6.5 14.9 %copy.17 = f32[2,32,12288]{1,0,2:T(2,128)} copy(f32[2,32,12288]{2,1,0:T(8,128)} %param.8) | data formatting | bytes 6291456 | tf_op args[1]
  21.4 15.0 %reshape.60 = f32[4,1,196608]{2,1,0:T(1,128)} reshape(f32[12288,2,32]{2,1,0:T(2,128)} %bitcast.28) | data formatting | bytes 6291456
  36.4 4.3 %all-to-all-start = ((f32[4,1,196608]{2,1,0:T(1,128)}), f32[4,1,196608]{2,1,0:T(1,128)S(1)}, u32[]{:S(2)}, u32[]{:S(2)}) async-start(f32[4,1,196608]{2,1,0:T(1,128)} %reshape.60), calls=%async_computation | async-start | bytes 6291456 | tf_op jit(solution)/shard_map/all_to_all | solution.py:56
  40.7 0.0 reduce-scatter.2.cloned.1.call-start
  40.7 0.0 copy-start.5
  40.7 7.5 %copy.24 = f32[3072,8,8,1,1]{2,1,4,3,0:T(8,128)} copy(f32[3072,8,8,1,1]{0,2,1,4,3:T(8,128)} %bitcast.33) | data formatting | bytes 1572864 | tf_op args[3]
  48.2 1.4 multiply_reduce_fusion
  49.6 0.0 copy-done.3
  49.6 0.3 fusion.3
  49.9 28.2 %psum.7 = f32[2,8]{1,0:T(2,128)S(1)} all-reduce(f32[2,8]{1,0:T(2,128)S(1)} %fusion.3), channel_id=1, replica_groups=mesh['order'=8,'blk'=4] {'blk'}, use_global_device_ids=true, to_apply=%region_1.0 | all-reduce | flops 16 | bytes 128 | tf_op jit(solution)/shard_map/psum | solution.py:36
  78.1 0.0 copy-done
  78.1 0.0 copy-done.2
  78.1 0.0 copy-done.4
  78.2 0.2 fusion.1
  78.4 6.2 %all_gather.3 = f32[2,128,128]{2,1,0:T(8,128)S(1)} all-gather(f32[2,32,128]{2,1,0:T(8,128)S(1)} %fusion.1), channel_id=1, replica_groups=mesh['order'=8,'blk'=4] {'blk'}, dimensions={1}, use_global_device_ids=true | all-gather | bytes 163840 | tf_op jit(solution)/shard_map/all_gather | solution.py:57
  84.6 0.1 compare_convert_fusion
  84.6 0.0 all-to-all-done
  84.7 0.5 broadcast.54
  85.2 10.8 %reduce = f32[4,196608]{1,0:T(4,128)} reduce(f32[4,1,196608]{2,1,0:T(1,128)S(1)} %all-to-all-done, f32[]{:T(128)} %broadcast.54), dimensions={1}, to_apply=%all_to_all.13.reduce_sub_computation | reduce | bytes 6291460 | tf_op jit(solution)/shard_map/all_to_all | solution.py:56
  96.0 20.8 %reshape.61 = f32[12288,2,32]{2,1,0:T(2,128)} reshape(f32[4,196608]{1,0:T(4,128)} %reduce) | data formatting | bytes 6291456
  116.8 13.9 %copy.18 = f32[2,32,4,3072]{3,1,2,0:T(8,128)S(1)} copy(f32[2,32,4,3072]{1,0,3,2:T(2,128)} %bitcast.27) | data formatting | bytes 6291456 | tf_op jit(solution)/shard_map/all_to_all | solution.py:56
  130.7 4.5 %fusion = f32[3072,2,128]{0,2,1:T(8,128)} fusion(f32[2,128,128]{2,1,0:T(8,128)S(1)} %all_gather.3, f32[2,128,3072]{2,1,0:T(8,128)S(1)} %bitcast.29, f32[3072,2]{0,1:T(2,128)S(1)} %compare_convert_fusion), kind=kOutput, calls=%fused_computation.2 | convolution fusion | flops 1208745984 | bytes 6447104 | tf_op jit(solution)/shard_map/krl,krc->lkc/dot_general | solution.py:58
  135.2 25.3 %copy.19 = f32[3072,2,2,8,8]{3,4,2,1,0:T(8,128)} copy(f32[3072,2,2,8,8]{0,4,3,2,1:T(8,128)} %bitcast.31) | data formatting | bytes 6291456 | tf_op jit(solution)/shard_map/reshape | solution.py:29
  160.5 51.6 %multiply_bitcast_fusion = f32[3072,2,2,8,8]{3,4,2,1,0:T(8,128)} fusion(f32[2,8]{1,0:T(2,128)S(1)} %rsqrt_multiply_fusion, f32[3072,2,2,8,8]{3,4,2,1,0:T(8,128)} %copy.19, f32[3072,8,8,1,1]{2,1,4,3,0:T(8,128)} %copy.24), kind=kOutput, calls=%fused_computation | convolution fusion | flops 76283904 | bytes 7077952 | tf_op jit(solution)/shard_map/dvr,dotrq->dotvq/dot_general | solution.py:30
  212.1 27.8 %copy.21 = f32[3072,2,2,8,8]{0,4,3,2,1:T(8,128)} copy(f32[3072,2,2,8,8]{3,4,2,1,0:T(8,128)} %multiply_bitcast_fusion) | data formatting | bytes 6291456 | tf_op jit(solution)/shard_map/mul | solution.py:37
  239.9 4.9 %fusion.11 = f32[2,128,128]{2,1,0:T(8,128)S(1)} fusion(f32[3072,2,128]{0,2,1:T(8,128)} %bitcast.32, f32[2,128,3072]{2,1,0:T(8,128)S(1)} %bitcast.30), kind=kOutput, calls=%fused_computation.21 | convolution fusion | flops 1207959552 | bytes 6422528 | tf_op jit(solution)/shard_map/krl,lkc->rkc/dot_general | solution.py:62
  244.8 0.7 copy.22
  245.5 0.0 reduce-scatter.2.cloned.1.call-update
  245.5 21.1 %reduce-scatter.2.cloned.1.call-done = f32[32,256]{1,0:T(8,128)} async-done(((f32[128,256]{1,0:T(8,128)}), f32[32,256]{1,0:T(8,128)}) %reduce-scatter.2.cloned.1.call-update) | async-done | bytes 32784 | tf_op jit(solution)/shard_map/reduce_scatter | solution.py:63
  266.6 0.8 reshape.58
  267.4 0.6 copy.23
  (10 shorter events, 0.0 us)
Async XLA Ops:
  6.5 71.6 %copy-start = (f32[2,64,128]{2,1,0:T(8,128)S(1)}, f32[2,64,128]{2,1,0:T(8,128)}, u32[]{:S(2)}) copy-start(f32[2,64,128]{2,1,0:T(8,128)} %param.12) | copy-start | bytes 196612
  36.4 48.3 %all-to-all-start = ((f32[4,1,196608]{2,1,0:T(1,128)}), f32[4,1,196608]{2,1,0:T(1,128)S(1)}, u32[]{:S(2)}, u32[]{:S(2)}) async-start(f32[4,1,196608]{2,1,0:T(1,128)} %reshape.60), calls=%async_computation | async-start | bytes 6291456 | tf_op jit(solution)/shard_map/all_to_all | solution.py:56
  40.7 225.9 %reduce-scatter.2.cloned.1.call-start = ((), (), s32[]{:S(2)}) async-start(), calls=%async_computation.2 | async-start | bytes 163840 | tf_op jit(solution)/shard_map/reduce_scatter | solution.py:63
  40.7 8.9 %copy-start.3 = (s32[2]{0:T(128)S(1)}, s32[2]{0:T(128)}, u32[]{:S(2)}) copy-start(s32[2]{0:T(128)} %param.13) | copy-start | bytes 28
  40.7 37.4 %copy-start.2 = (f32[2,32,128]{2,1,0:T(8,128)S(1)}, f32[2,32,128]{2,1,0:T(8,128)}, u32[]{:S(2)}) copy-start(f32[2,32,128]{2,1,0:T(8,128)} %param.7) | copy-start | bytes 98308
  40.7 37.4 %copy-start.4 = (s32[2,64]{1,0:T(2,128)S(1)}, s32[2,64]{1,0:T(2,128)}, u32[]{:S(2)}) copy-start(s32[2,64]{1,0:T(2,128)} %param.11) | copy-start | bytes 1540
  40.7 37.4 %copy-start.5 = (f32[32]{0:T(128)S(1)}, f32[32]{0:T(128)}, u32[]{:S(2)}) copy-start(f32[32]{0:T(128)} %param.9) | copy-start | bytes 388
  239.9 28.1 %copy-start.1 = (f32[2,64,128]{2,1,0:T(8,128)S(1)}, f32[2,64,128]{2,1,0:T(8,128)}, u32[]{:S(2)}) copy-start(f32[2,64,128]{2,1,0:T(8,128)} %param.12) | copy-start | bytes 196612
Sparse Core Ops, SparseCore 0:
  245.7 20.8 reduce-scatter.1
where the time goes:
time: 278 us; the launch traced here: 275 us
  local copies, waits for them, and re-layouts  128 us (46%)
  matrix products  61.5 us (22%)
  blocking collectives  34.4 us (12%)
  waiting for transfers between devices  21.1 us (8%)
  between operations  13.5 us (5%)
  other arithmetic  12.2 us (4%)
  starting transfers between devices  4.29 us (2%)
    unnamed x16, local copies, waits for them, and re-layouts  58.2 us
    dot_general x1, matrix products, finish(): jnp.einsum('dvr,dotrq->dotvq', matched_filter_weights, masked_values, pre...  51.6 us
    psum x1, blocking collectives, finish(): response = lax.psum(response, 'blk')  28.2 us
    mul x1, local copies, waits for them, and re-layouts, finish(): scaled = matched_output * (L / jnp.sqrt(response))[None, :, None, :, None]  27.8 us
    reshape x1, local copies, waits for them, and re-layouts, finish(): (harmonics * kept_mask[:, :, None]).reshape(blocks, M, 2, F, SIMS)  25.3 us
    reduce_scatter x1, waiting for transfers between devices, body(): lax.psum_scatter(partial_running_sum.reshape(local * lax.axis_size('blk')...  21.1 us
    all_to_all x2, local copies, waits for them, and re-layouts, body(): lax.all_to_all(legendre, 'blk', split_axis=2, concat_axis=1, tiled=True)  14.5 us
    all_to_all x1, other arithmetic, body(): lax.all_to_all(legendre, 'blk', split_axis=2, concat_axis=1, tiled=True)  10.8 us
  transfers between devices with their start and end apart: 2, of which 1 were waited for; matrix products, arithmetic and copies ran while one was open for 3% of the time, Pallas kernels for 0%

commit v1 on v0

v1 whole, which is shorter than its diff:
```python
import functools

import jax
import jax.numpy as jnp
from jax import lax
from jax.experimental import pallas as pl
from jax.experimental.pallas import tpu as pltpu
from jax.sharding import PartitionSpec as P

LANES = 128
VMEM_LIMIT = 48 * 1024 * 1024


def partner(x, n):
    return [(i, i ^ x) for i in range(n)]


def split_degrees(blocks):
    tiles = blocks // LANES
    if tiles < 12:
        return [blocks]
    first = tiles // 6
    last = tiles // 12
    middle = tiles - first - last
    half = middle // 2
    return [w * LANES for w in (first, half, middle - half, last)]


def halves(value):
    high = value.astype(jnp.bfloat16)
    low = (value - high.astype(jnp.float32)).astype(jnp.bfloat16)
    return high, low


def compiler_params(**kwargs):
    return pltpu.CompilerParams(vmem_limit_bytes=VMEM_LIMIT, **kwargs)


def cut_kernel(pieces, blocks, me_ref, legendre_ref, *refs):
    outs, sems = refs[:-1], refs[-1]
    copies = []
    for number, (x, offset, width) in enumerate(pieces):
        start = pl.multiple_of((me_ref[0] ^ x) * blocks + offset, LANES)
        copies.append(
            pltpu.make_async_copy(
                legendre_ref.at[:, :, pl.ds(start, width)], outs[number], sems.at[number]
            )
        )
    for copy in copies:
        copy.start()
    for copy in copies:
        copy.wait()


def cut(me, legendre, pieces, blocks):
    orders, rows, _ = legendre.shape
    shapes = [jax.ShapeDtypeStruct((orders, rows, w), jnp.float32) for _, _, w in pieces]
    size = sum(orders * rows * w * 4 for _, _, w in pieces)
    return pl.pallas_call(
        functools.partial(cut_kernel, pieces, blocks),
        out_shape=shapes,
        in_specs=[pl.BlockSpec(memory_space=pltpu.SMEM), pl.BlockSpec(memory_space=pl.ANY)],
        out_specs=[pl.BlockSpec(memory_space=pl.ANY)] * len(pieces),
        scratch_shapes=[pltpu.SemaphoreType.DMA((len(pieces),))],
        compiler_params=compiler_params(),
        cost_estimate=pl.CostEstimate(flops=0, bytes_accessed=2 * size, transcendentals=0),
        name="cut",
    )(me, legendre)


def inject_kernel(me_ref, cycles_ref, weight_ref, hits_ref, flux_ref, out_ref):
    orders, rows, _ = cycles_ref.shape
    count = hits_ref.shape[1]
    eye = lax.broadcasted_iota(jnp.int32, (rows, rows), 0) == lax.broadcasted_iota(
        jnp.int32, (rows, rows), 1
    )
    weight = jnp.sum(jnp.where(eye, weight_ref[...], 0.0), axis=1, keepdims=True)
    ids = me_ref[0] * rows + lax.broadcasted_iota(jnp.int32, (rows, count), 0)
    for k in range(orders):
        hits = (ids == hits_ref[k : k + 1, :]).astype(jnp.float32)
        added = jnp.dot(
            hits,
            flux_ref[k],
            precision=lax.Precision.HIGHEST,
            preferred_element_type=jnp.float32,
        )
        out_ref[k] = weight * (cycles_ref[k] + added)


def inject(me, cycles, weight, cluster_cycles, flux):
    vmem = pl.BlockSpec(memory_space=pltpu.VMEM)
    return pl.pallas_call(
        inject_kernel,
        out_shape=jax.ShapeDtypeStruct(cycles.shape, jnp.float32),
        in_specs=[pl.BlockSpec(memory_space=pltpu.SMEM), vmem, vmem, vmem, vmem],
        out_specs=vmem,
        compiler_params=compiler_params(),
        name="inject",
    )(me, cycles, weight.reshape(1, -1), cluster_cycles, flux)


def response_kernel(blocks, scales, skies, me_ref, order_ref, weights_ref, out_ref):
    orders = order_ref.shape[0]
    degree = me_ref[0] * blocks + lax.broadcasted_iota(jnp.int32, (1, blocks), 1)
    factor = 2.0 * degree.astype(jnp.float32) + 1.0
    squares = jnp.concatenate(
        [
            jnp.sum(weights_ref[s] * weights_ref[s], axis=0, keepdims=True) * factor
            for s in range(scales)
        ],
        axis=0,
    )
    columns = out_ref.shape[1]
    scale_of = (lax.broadcasted_iota(jnp.int32, (scales, columns), 1) // skies) % scales
    chosen = scale_of == lax.broadcasted_iota(jnp.int32, (scales, columns), 0)
    out_ref[...] = jnp.zeros_like(out_ref)
    for k in range(orders):
        total = jnp.sum(jnp.where(degree >= order_ref[k], squares, 0.0), axis=1, keepdims=True)
        out_ref[k : k + 1, :] = jnp.sum(jnp.where(chosen, total, 0.0), axis=0, keepdims=True)


def response_rows(me, order_per_slot, weights, skies, columns):
    scales, _, blocks = weights.shape
    smem = pl.BlockSpec(memory_space=pltpu.SMEM)
    vmem = pl.BlockSpec(memory_space=pltpu.VMEM)
    rows = -(-order_per_slot.shape[0] // 8) * 8
    return pl.pallas_call(
        functools.partial(response_kernel, blocks, scales, skies),
        out_shape=jax.ShapeDtypeStruct((rows, columns), jnp.float32),
        in_specs=[smem, smem, vmem],
        out_specs=vmem,
        compiler_params=compiler_params(),
        name="response",
    )(me, order_per_slot, weights)


def prepare_kernel(*refs):
    pieces, out_ref = refs[:-1], refs[-1]
    for k in range(out_ref.shape[0]):
        whole = jnp.concatenate([piece[k] for piece in pieces], axis=0).T
        high, low = halves(whole)
        out_ref[k] = jnp.concatenate([high, low, high], axis=1)


def prepare(pieces):
    orders, rows, columns = pieces[0].shape
    vmem = pl.BlockSpec(memory_space=pltpu.VMEM)
    return pl.pallas_call(
        prepare_kernel,
        out_shape=jax.ShapeDtypeStruct((orders, columns, 3 * rows * len(pieces)), jnp.bfloat16),
        in_specs=[vmem] * len(pieces),
        out_specs=vmem,
        compiler_params=compiler_params(),
        name="prepare",
    )(*pieces)


def chunk_kernel(n, first, last, blocks, offset, tile, me_ref, order_ref, *refs):
    legendre = refs[:n]
    analysis_ref, weights_ref = refs[n : n + 2]
    rest = list(refs[n + 2 :])
    before = None if first else rest.pop(0)
    response = rest.pop(0) if last else None
    total = rest.pop()
    step = pl.program_id(0)
    orders, rows, _ = legendre[0].shape
    scales, channels, _ = weights_ref.shape
    columns = analysis_ref.shape[1]
    skies = columns // (2 * channels)
    everything = n * rows

    @pl.when(step == 0)
    def _():
        total[...] = jnp.zeros_like(total)

    degree = (
        me_ref[0] * blocks
        + offset
        + step * tile
        + lax.broadcasted_iota(jnp.int32, (1, tile), 1)
    )
    for k in range(orders):
        values = jnp.concatenate([block[k] for block in legendre], axis=0)
        high, low = halves(values)
        harmonics = jnp.dot(
            analysis_ref[k],
            jnp.concatenate([high, high, low], axis=0),
            preferred_element_type=jnp.float32,
        )
        harmonics = jnp.where(degree >= order_ref[k], harmonics, 0.0)
        matched = []
        for p in range(2):
            for s in range(scales):
                value = None
                for f in range(channels):
                    at = (p * channels + f) * skies
                    term = weights_ref[s, f : f + 1, :] * harmonics[at : at + skies, :]
                    value = term if value is None else value + term
                matched.append(value)
        matched_high, matched_low = halves(jnp.concatenate(matched, axis=0))
        total[k] += lax.dot_general(
            jnp.concatenate([high, low], axis=0),
            jnp.concatenate([matched_high, matched_low], axis=0),
            (((1,), (1,)), ((), ())),
            preferred_element_type=jnp.float32,
        )

    @pl.when(step == pl.num_programs(0) - 1)
    def _():
        wide = total.shape[2] // 2
        for k in range(orders):
            result = (
                (total[k, everything:, wide:] + total[k, everything:, :wide])
                + total[k, :everything, wide:]
            ) + total[k, :everything, :wide]
            if before is not None:
                result = result + before[k]
            if last:
                for x in range(n):
                    rest[x][k * rows : (k + 1) * rows, :] = result[x * rows : (x + 1) * rows, :]
            else:
                rest[0][k] = result
        if last:
            for x in range(n):
                rest[x][orders * rows :, :] = response[...]


def chunk(me, order_per_slot, legendre, parts, analysis, weights, before, response, blocks, offset, width):
    n = len(parts) + 1
    orders, rows, _ = legendre.shape
    columns = analysis.shape[1]
    scales, channels, _ = weights.shape
    tile = next(t for t in (512, 384, 256, 128) if width % t == 0 and offset % t == 0 and blocks % t == 0)
    last = response is not None
    first = before is None
    steps = width // tile

    def at(start):
        return pl.BlockSpec((orders, rows, tile), lambda i, me, order: (0, 0, start // tile + i))

    own = pl.BlockSpec(
        (orders, rows, tile),
        lambda i, me, order: (0, 0, me[0] * (blocks // tile) + offset // tile + i),
    )
    whole = lambda array: pl.BlockSpec(array.shape, lambda i, me, order: (0,) * array.ndim)
    operands = [legendre] + [array for array, _ in parts] + [analysis, weights]
    in_specs = [own] + [at(start) for _, start in parts]
    in_specs += [
        whole(analysis),
        pl.BlockSpec((scales, channels, tile), lambda i, me, order: (0, 0, offset // tile + i)),
    ]
    if not first:
        operands.append(before)
        in_specs.append(whole(before))
    if last:
        operands.append(response)
        in_specs.append(whole(response))
        out_shape = [
            jax.ShapeDtypeStruct((orders * rows + response.shape[0], columns), jnp.float32)
        ] * n
    else:
        out_shape = [jax.ShapeDtypeStruct((orders, n * rows, columns), jnp.float32)]
    macs = orders * width * columns * rows * n
    return pl.pallas_call(
        functools.partial(chunk_kernel, n, first, last, blocks, offset, tile),
        out_shape=out_shape,
        grid_spec=pltpu.PrefetchScalarGridSpec(
            num_scalar_prefetch=2,
            grid=(steps,),
            in_specs=in_specs,
            out_specs=[whole(shape) for shape in out_shape],
            scratch_shapes=[pltpu.VMEM((orders, 2 * n * rows, 2 * columns), jnp.float32)],
        ),
        compiler_params=compiler_params(dimension_semantics=("arbitrary",)),
        cost_estimate=pl.CostEstimate(
            flops=2 * 7 * macs,
            bytes_accessed=4 * orders * n * rows * width,
            transcendentals=0,
        ),
        name="chunk",
    )(me, order_per_slot, *operands)


def finish_kernel(degrees, *refs):
    parts, out_ref = refs[:-1], refs[-1]
    orders, rows, _ = out_ref.shape
    total = parts[0][...]
    for part in parts[1:]:
        total = total + part[...]
    for k in range(orders):
        at = orders * rows + k
        out_ref[k] = total[k * rows : (k + 1) * rows, :] * (
            degrees / jnp.sqrt(total[at : at + 1, :])
        )


def finish(parts, shape, degrees):
    vmem = pl.BlockSpec(memory_space=pltpu.VMEM)
    return pl.pallas_call(
        functools.partial(finish_kernel, degrees),
        out_shape=jax.ShapeDtypeStruct(shape, jnp.float32),
        in_specs=[vmem] * len(parts),
        out_specs=vmem,
        compiler_params=compiler_params(),
        name="finish",
    )(*parts)


def body(
    fourier_cycles,
    legendre,
    cycle_weight,
    matched_filter_weights,
    cluster_cycles,
    cluster_flux,
    order_per_slot,
):
    n = lax.axis_size("blk")
    blocks = legendre.shape[2] // n
    columns = fourier_cycles.shape[2]
    channels = matched_filter_weights.shape[2]
    skies = columns // (2 * channels)
    me = lax.axis_index("blk").reshape(1).astype(jnp.int32)
    weights = jnp.transpose(matched_filter_weights, (1, 2, 0))
    widths = split_degrees(blocks)
    offsets = [sum(widths[:c]) for c in range(len(widths))]

    def send(value, x):
        return lax.ppermute(value, "blk", partner(x, n))

    far = range(2, n)
    sent = []
    for c, (offset, width) in enumerate(zip(offsets, widths)):
        pieces = [(x, offset, width) for x in far]
        if c == 0:
            pieces.append((1, 0, blocks))
        cuts = list(cut(me, legendre, pieces, blocks))
        if c == 0:
            near = send(cuts.pop(), 1)
        sent.append([send(value, x) for value, x in zip(cuts, far)])

    own = inject(me, fourier_cycles, cycle_weight, cluster_cycles, cluster_flux)
    cycles = {0: own}
    bit = n // 2
    while bit:
        for x in list(cycles):
            cycles[x ^ bit] = send(cycles[x], bit)
        bit //= 2
    analysis = prepare([cycles[x] for x in range(n)])
    response = response_rows(me, order_per_slot, weights, skies, columns)

    total = None
    for c, (offset, width) in enumerate(zip(offsets, widths)):
        parts = [(near, offset)] + [(value, 0) for value in sent[c]]
        final = c == len(widths) - 1
        result = chunk(
            me,
            order_per_slot,
            legendre,
            parts,
            analysis,
            weights,
            total,
            response if final else None,
            blocks,
            offset,
            width,
        )
        total = result[0]
    returned = [result[0]] + [send(result[x], x) for x in range(1, n)]
    return finish(returned, fourier_cycles.shape, float(legendre.shape[2]))


def solution(mesh):
    return jax.shard_map(
        body,
        mesh=mesh,
        in_specs=(
            P("order", "blk", None),
            P("order", "blk", None),
            P("blk"),
            P("blk", None, None),
            P("order", None),
            P("order", None, None),
            P("order"),
        ),
        out_specs=P("order", "blk", None),
        check_vma=False,
    )
```

time: 278 us -> 56 us (0.20)
  local copies, waits for them, and re-layouts: 128 us -> 3.53 us
  matrix products: 61.5 us -> 0 us
  blocking collectives: 34.4 us -> 0 us
  Pallas kernels: 0 us -> 18.6 us
  between operations: 13.5 us -> 0.16 us
  other arithmetic: 12.2 us -> 0 us
  starting transfers between devices: 4.29 us -> 15.5 us
  waiting for transfers between devices: 21.1 us -> 17.6 us
    dot_general x5 -> x0, matrix products: 61.5 us -> none  [the longest x1 51.6 us: finish(): jnp.einsum('dvr,dotrq->dotvq', matched_filter_weights, masked_values, pre...]
    unnamed x16, local copies, waits for them, and re-layouts: 58.2 us -> 3.53 us
    psum x1 -> x0, blocking collectives: 28.2 us -> none  [finish(): response = lax.psum(response, 'blk')]
    mul x1 -> x0, local copies, waits for them, and re-layouts: 27.8 us -> none  [finish(): scaled = matched_output * (L / jnp.sqrt(response))[None, :, None, :, None]]
    reshape x3 -> x0, local copies, waits for them, and re-layouts: 26.8 us -> none  [the longest x1 25.3 us: finish(): (harmonics * kept_mask[:, :, None]).reshape(blocks, M, 2, F, SIMS)]
    reduce_scatter x1 -> x0, waiting for transfers between devices: 21.1 us -> none  [body(): lax.psum_scatter(partial_running_sum.reshape(local * lax.axis_size('blk')...]
    pallas_call x0 -> x12, Pallas kernels: none -> 18.6 us  [the longest x4 16.5 us: chunk(): pl.pallas_call(functools.partial(chunk_kernel, n, first, last, blocks, of...]
    ppermute x0 -> x15, waiting for transfers between devices: none -> 17.6 us  [send(): return lax.ppermute(value, 'blk', partner(x, n))]
  transfers between devices with their start and end apart: 2 -> 15, of which waited for: 1 -> 6; matrix products, arithmetic and copies ran while one was open for 3% -> 0% of each run, Pallas kernels for 0% -> 30%
where the time goes in v1:
time: 56 us; the launch traced here: 55.4 us
  Pallas kernels  18.6 us (33%)
  waiting for transfers between devices  17.6 us (31%)
  starting transfers between devices  15.5 us (28%)
  local copies, waits for them, and re-layouts  3.53 us (6%)
    ppermute x15, waiting for transfers between devices, send(): return lax.ppermute(value, 'blk', partner(x, n))  17.6 us
    pallas_call x4, Pallas kernels, chunk(): pl.pallas_call(functools.partial(chunk_kernel, n, first, last, blocks, of...  16.5 us
    ppermute x15, starting transfers between devices, send(): return lax.ppermute(value, 'blk', partner(x, n))  15.5 us
    unnamed x16, local copies, waits for them, and re-layouts  3.53 us
  transfers between devices with their start and end apart: 15, of which 6 were waited for; matrix products, arithmetic and copies ran while one was open for 0% of the time, Pallas kernels for 30%

profile of v1, /device:TPU:1, one launch (start us, length us, event | category | flops | bytes accessed | tf_op | source)
XLA Modules:
  0.0 55.4 jit_solution(7314237454218608145)
XLA Ops:
  0.0 1.9 %copy-done = f32[2,32,12288]{2,1,0:T(8,128)S(1)} copy-done((f32[2,32,12288]{2,1,0:T(8,128)S(1)}, f32[2,32,12288]{2,1,0:T(8,128)}, u32[]{:S(2)}) %copy-start) | copy-done | bytes 3145752
  1.9 0.1 cut.4
  2.1 0.1 collective-permute-start
  2.2 2.7 %collective-permute-start.10 = (f32[2,32,512]{2,1,0:T(8,128)S(1)}, f32[2,32,512]{2,1,0:T(8,128)S(1)}, u32[]{:S(2)}, u32[]{:S(2)}) collective-permute-start(f32[2,32,512]{2,1,0:T(8,128)S(1)} %get-tuple-element.25), channel_id=1, source_target_pairs={{0,2},{1,3},{2,0},{3,1},{4,6},{5,7},{6,4},{7,5},{8,10},{9,11},{10,... | collective-permute-start | bytes 393224 | tf_op jit(solution)/shard_map/ppermute | solution.py:329
  4.9 0.8 %copy-done.3 = f32[2,64,128]{2,1,0:T(8,128)S(1)} copy-done((f32[2,64,128]{2,1,0:T(8,128)S(1)}, f32[2,64,128]{2,1,0:T(8,128)}, u32[]{:S(2)}) %copy-start.3) | copy-done | bytes 65560
  5.8 0.8 %copy-done.4 = f32[2,32,128]{2,1,0:T(8,128)S(1)} copy-done((f32[2,32,128]{2,1,0:T(8,128)S(1)}, f32[2,32,128]{2,1,0:T(8,128)}, u32[]{:S(2)}) %copy-start.4) | copy-done | bytes 32792
  6.5 0.1 inject.1.refs_0_
  6.7 1.7 %collective-permute-start.4 = (f32[2,32,128]{2,1,0:T(8,128)S(1)}, f32[2,32,128]{2,1,0:T(8,128)S(1)}, u32[]{:S(2)}, u32[]{:S(2)}) collective-permute-start(f32[2,32,128]{2,1,0:T(8,128)S(1)} %inject.1.refs_0_), channel_id=1, source_target_pairs={{0,2},{1,3},{2,0},{3,1},{4,6},{5,7},{6,4},{7,5},{8,10},{9,11},{10,... | collective-permute-start | bytes 98312 | tf_op jit(solution)/shard_map/ppermute | solution.py:329
  8.4 0.4 collective-permute-start.3
  8.8 3.4 %collective-permute-done.4.refs_2_ = f32[2,32,128]{2,1,0:T(8,128)S(1)} collective-permute-done((f32[2,32,128]{2,1,0:T(8,128)S(1)}, f32[2,32,128]{2,1,0:T(8,128)S(1)}, u32[]{:S(2)}, u32[]{:S(2)}) %collective-permute-start.4) | collective-permute-done | bytes 32800 | tf_op jit(solution)/shard_map/ppermute | solution.py:329
  12.2 0.7 %collective-permute-start.5 = (f32[2,32,128]{2,1,0:T(8,128)S(1)}, f32[2,32,128]{2,1,0:T(8,128)S(1)}, u32[]{:S(2)}, u32[]{:S(2)}) collective-permute-start(f32[2,32,128]{2,1,0:T(8,128)S(1)} %collective-permute-done.4.refs_2_), channel_id=1, source_target_pairs={{0,1},{1,0},{2,3},{3,2},{4,5},{5,4},{6,7},{7,6},{8,9},{9,8},{10,11... | collective-permute-start | bytes 98312 | tf_op jit(solution)/shard_map/ppermute | solution.py:329
  12.9 1.5 %collective-permute-start.8 = (f32[2,32,1152]{2,1,0:T(8,128)S(1)}, f32[2,32,1152]{2,1,0:T(8,128)S(1)}, u32[]{:S(2)}, u32[]{:S(2)}) collective-permute-start(f32[2,32,1152]{2,1,0:T(8,128)S(1)} %get-tuple-element.23), channel_id=1, source_target_pairs={{0,2},{1,3},{2,0},{3,1},{4,6},{5,7},{6,4},{7,5},{8,10},{9,11},{10,... | collective-permute-start | bytes 884744 | tf_op jit(solution)/shard_map/ppermute | solution.py:329
  14.5 0.9 %collective-permute-start.9 = (f32[2,32,1152]{2,1,0:T(8,128)S(1)}, f32[2,32,1152]{2,1,0:T(8,128)S(1)}, u32[]{:S(2)}, u32[]{:S(2)}) collective-permute-start(f32[2,32,1152]{2,1,0:T(8,128)S(1)} %get-tuple-element.24), channel_id=1, source_target_pairs={{0,3},{1,2},{2,1},{3,0},{4,7},{5,6},{6,5},{7,4},{8,11},{9,10},{10,... | collective-permute-start | bytes 884744 | tf_op jit(solution)/shard_map/ppermute | solution.py:329
  15.5 0.8 %collective-permute-start.6 = (f32[2,32,1152]{2,1,0:T(8,128)S(1)}, f32[2,32,1152]{2,1,0:T(8,128)S(1)}, u32[]{:S(2)}, u32[]{:S(2)}) collective-permute-start(f32[2,32,1152]{2,1,0:T(8,128)S(1)} %get-tuple-element.21), channel_id=1, source_target_pairs={{0,2},{1,3},{2,0},{3,1},{4,6},{5,7},{6,4},{7,5},{8,10},{9,11},{10,... | collective-permute-start | bytes 884744 | tf_op jit(solution)/shard_map/ppermute | solution.py:329
  16.3 1.1 %collective-permute-start.7 = (f32[2,32,1152]{2,1,0:T(8,128)S(1)}, f32[2,32,1152]{2,1,0:T(8,128)S(1)}, u32[]{:S(2)}, u32[]{:S(2)}) collective-permute-start(f32[2,32,1152]{2,1,0:T(8,128)S(1)} %get-tuple-element.22), channel_id=1, source_target_pairs={{0,3},{1,2},{2,1},{3,0},{4,7},{5,6},{6,5},{7,4},{8,11},{9,10},{10,... | collective-permute-start | bytes 884744 | tf_op jit(solution)/shard_map/ppermute | solution.py:329
  17.4 0.9 %response.1.refs_7_ = f32[8,128]{1,0:T(8,128)S(1)} custom-call(s32[1]{0:T(128)} %bitcast.me_ref, s32[2]{0:T(128)S(1)} %copy-done.5, f32[8,8,3072]{2,1,0:T(8,128)S(1)} %bitcast.3), custom_call_target="tpu_custom_call" | custom-call | tf_op jit(solution)/shard_map/response/pallas_call | solution.py:127
  18.3 0.1 prepare.1.refs_4_
  18.5 0.8 %collective-permute-start.1 = (f32[2,32,256]{2,1,0:T(8,128)S(1)}, f32[2,32,256]{2,1,0:T(8,128)S(1)}, u32[]{:S(2)}, u32[]{:S(2)}) collective-permute-start(f32[2,32,256]{2,1,0:T(8,128)S(1)} %get-tuple-element.19), channel_id=1, source_target_pairs={{0,2},{1,3},{2,0},{3,1},{4,6},{5,7},{6,4},{7,5},{8,10},{9,11},{10,... | collective-permute-start | bytes 196616 | tf_op jit(solution)/shard_map/ppermute | solution.py:329
  19.3 1.6 %chunk.4.refs_6_ = f32[2,128,128]{2,1,0:T(8,128)S(1)} custom-call(s32[1]{0:T(128)} %bitcast.me_ref, s32[2]{0:T(128)S(1)} %copy-done.5, f32[2,32,12288]{2,1,0:T(8,128)S(1)} %copy-done.1, f32[2,32,3072]{2,1,0:T(8,128)S(1)} %collective-permute-done.refs_1_, f32[2,32,512]{2,1,0:T(8,128)S(1)} %collective-permute-done.10.refs_2_, ...), custom_call_target="tpu_custom_call" | custom-call | flops 234881024 | bytes 524288 | tf_op jit(solution)/shard_map/chunk/pallas_call | solution.py:264
  20.9 0.8 %collective-permute-done.8.refs_2_ = f32[2,32,1152]{2,1,0:T(8,128)S(1)} collective-permute-done((f32[2,32,1152]{2,1,0:T(8,128)S(1)}, f32[2,32,1152]{2,1,0:T(8,128)S(1)}, u32[]{:S(2)}, u32[]{:S(2)}) %collective-permute-start.8) | collective-permute-done | bytes 294944 | tf_op jit(solution)/shard_map/ppermute | solution.py:329
  21.7 2.5 %collective-permute-start.2 = (f32[2,32,256]{2,1,0:T(8,128)S(1)}, f32[2,32,256]{2,1,0:T(8,128)S(1)}, u32[]{:S(2)}, u32[]{:S(2)}) collective-permute-start(f32[2,32,256]{2,1,0:T(8,128)S(1)} %get-tuple-element.20), channel_id=1, source_target_pairs={{0,3},{1,2},{2,1},{3,0},{4,7},{5,6},{6,5},{7,4},{8,11},{9,10},{10,... | collective-permute-start | bytes 196616 | tf_op jit(solution)/shard_map/ppermute | solution.py:329
  24.2 4.3 %collective-permute-done.9.refs_3_ = f32[2,32,1152]{2,1,0:T(8,128)S(1)} collective-permute-done((f32[2,32,1152]{2,1,0:T(8,128)S(1)}, f32[2,32,1152]{2,1,0:T(8,128)S(1)}, u32[]{:S(2)}, u32[]{:S(2)}) %collective-permute-start.9) | collective-permute-done | bytes 294944 | tf_op jit(solution)/shard_map/ppermute | solution.py:329
  28.4 6.9 %chunk.5.refs_6_ = f32[2,128,128]{2,1,0:T(8,128)S(1)} custom-call(s32[1]{0:T(128)} %bitcast.me_ref, s32[2]{0:T(128)S(1)} %copy-done.5, f32[2,32,12288]{2,1,0:T(8,128)S(1)} %copy-done.1, f32[2,32,3072]{2,1,0:T(8,128)S(1)} %collective-permute-done.refs_1_, f32[2,32,1152]{2,1,0:T(8,128)S(1)} %collective-permute-done.8.refs_2_, ...), custom_call_target="tpu_custom_call" | custom-call | flops 528482304 | bytes 1179648 | tf_op jit(solution)/shard_map/chunk/pallas_call | solution.py:264
  35.3 5.7 %collective-permute-done.7.refs_3_ = f32[2,32,1152]{2,1,0:T(8,128)S(1)} collective-permute-done((f32[2,32,1152]{2,1,0:T(8,128)S(1)}, f32[2,32,1152]{2,1,0:T(8,128)S(1)}, u32[]{:S(2)}, u32[]{:S(2)}) %collective-permute-start.7) | collective-permute-done | bytes 294944 | tf_op jit(solution)/shard_map/ppermute | solution.py:329
  41.1 6.9 %chunk.6.refs_6_ = f32[2,128,128]{2,1,0:T(8,128)S(1)} custom-call(s32[1]{0:T(128)} %bitcast.me_ref, s32[2]{0:T(128)S(1)} %copy-done.5, f32[2,32,12288]{2,1,0:T(8,128)S(1)} %copy-done.1, f32[2,32,3072]{2,1,0:T(8,128)S(1)} %collective-permute-done.refs_1_, f32[2,32,1152]{2,1,0:T(8,128)S(1)} %collective-permute-done.6.refs_2_, ...), custom_call_target="tpu_custom_call" | custom-call | flops 528482304 | bytes 1179648 | tf_op jit(solution)/shard_map/chunk/pallas_call | solution.py:264
  48.0 1.1 %chunk.7 = (f32[72,128]{1,0:T(8,128)S(1)}, f32[72,128]{1,0:T(8,128)S(1)}, f32[72,128]{1,0:T(8,128)S(1)}, f32[72,128]{1,0:T(8,128)S(1)}) custom-call(s32[1]{0:T(128)} %bitcast.me_ref, s32[2]{0:T(128)S(1)} %copy-done.5, f32[2,32,12288]{2,1,0:T(8,128)S(1)} %copy-done.1, f32[2,32,3072]{2,1,0:T(8,128)S(1)} %collective-permute-done.refs_1_, ...), custom_call_target="tpu_custom_call" | custom-call | flops 117440512 | bytes 262144 | tf_op jit(solution)/shard_map/chunk/pallas_call | solution.py:264
  49.1 0.1 collective-permute-start.12
  49.2 1.5 %collective-permute-start.13 = (f32[72,128]{1,0:T(8,128)S(1)}, f32[72,128]{1,0:T(8,128)S(1)}, u32[]{:S(2)}, u32[]{:S(2)}) collective-permute-start(f32[72,128]{1,0:T(8,128)S(1)} %get-tuple-element.29), channel_id=1, source_target_pairs={{0,2},{1,3},{2,0},{3,1},{4,6},{5,7},{6,4},{7,5},{8,10},{9,11},{10,... | collective-permute-start | bytes 110600 | tf_op jit(solution)/shard_map/ppermute | solution.py:329
  50.7 0.6 %collective-permute-start.14 = (f32[72,128]{1,0:T(8,128)S(1)}, f32[72,128]{1,0:T(8,128)S(1)}, u32[]{:S(2)}, u32[]{:S(2)}) collective-permute-start(f32[72,128]{1,0:T(8,128)S(1)} %get-tuple-element.30), channel_id=1, source_target_pairs={{0,3},{1,2},{2,1},{3,0},{4,7},{5,6},{6,5},{7,4},{8,11},{9,10},{10,... | collective-permute-start | bytes 110600 | tf_op jit(solution)/shard_map/ppermute | solution.py:329
  51.3 0.8 %collective-permute-done.13.refs_2_ = f32[72,128]{1,0:T(8,128)S(1)} collective-permute-done((f32[72,128]{1,0:T(8,128)S(1)}, f32[72,128]{1,0:T(8,128)S(1)}, u32[]{:S(2)}, u32[]{:S(2)}) %collective-permute-start.13) | collective-permute-done | bytes 36896 | tf_op jit(solution)/shard_map/ppermute | solution.py:329
  52.1 2.7 %collective-permute-done.14.refs_3_ = f32[72,128]{1,0:T(8,128)S(1)} collective-permute-done((f32[72,128]{1,0:T(8,128)S(1)}, f32[72,128]{1,0:T(8,128)S(1)}, u32[]{:S(2)}, u32[]{:S(2)}) %collective-permute-start.14) | collective-permute-done | bytes 36896 | tf_op jit(solution)/shard_map/ppermute | solution.py:329
  54.8 0.6 %finish.1 = f32[2,32,128]{2,1,0:T(8,128)} custom-call(f32[72,128]{1,0:T(8,128)S(1)} %get-tuple-element.27.refs_0_, f32[72,128]{1,0:T(8,128)S(1)} %collective-permute-done.12.refs_1_, f32[72,128]{1,0:T(8,128)S(1)} %collective-permute-done.13.refs_2_, f32[72,128]{1,0:T(8,128)S(1)} %collective-permute-done.14.refs_3_), custom_call_target="tpu_custom_call" | custom-call | tf_op jit(solution)/shard_map/finish/pallas_call | solution.py:299
  (26 shorter events, 0.3 us)
Async XLA Ops:
  0.0 4.9 %copy-start.7 = (f32[32]{0:T(128)S(1)}, f32[32]{0:T(128)}, u32[]{:S(2)}) copy-start(f32[32]{0:T(128)} %param.9) | copy-start | bytes 388
  0.0 4.9 %copy-start.6 = (s32[2,64]{1,0:T(2,128)S(1)}, s32[2,64]{1,0:T(2,128)}, u32[]{:S(2)}) copy-start(s32[2,64]{1,0:T(2,128)} %hits_ref.1) | copy-start | bytes 1540
  0.0 1.9 %copy-start = (f32[2,32,12288]{2,1,0:T(8,128)S(1)}, f32[2,32,12288]{2,1,0:T(8,128)}, u32[]{:S(2)}) copy-start(f32[2,32,12288]{2,1,0:T(8,128)} %refs_0_.7) | copy-start | bytes 9437188
  1.9 10.9 %copy-start.1 = (f32[2,32,12288]{2,1,0:T(8,128)S(1)}, f32[2,32,12288]{2,1,0:T(8,128)}, u32[]{:S(2)}) copy-start(f32[2,32,12288]{2,1,0:T(8,128)} %refs_0_.7) | copy-start | bytes 9437188
  2.1 16.4 %collective-permute-start = (f32[2,32,3072]{2,1,0:T(8,128)S(1)}, f32[2,32,3072]{2,1,0:T(8,128)S(1)}, u32[]{:S(2)}, u32[]{:S(2)}) collective-permute-start(f32[2,32,3072]{2,1,0:T(8,128)S(1)} %get-tuple-element.18), channel_id=1, source_target_pairs={{0,1},{1,0},{2,3},{3,2},{4,5},{5,4},{6,7},{7,6},{8,9},{9,8},{10,11... | collective-permute-start | bytes 2359304 | tf_op jit(solution)/shard_map/ppermute | solution.py:329
  2.2 13.3 %collective-permute-start.10 = (f32[2,32,512]{2,1,0:T(8,128)S(1)}, f32[2,32,512]{2,1,0:T(8,128)S(1)}, u32[]{:S(2)}, u32[]{:S(2)}) collective-permute-start(f32[2,32,512]{2,1,0:T(8,128)S(1)} %get-tuple-element.25), channel_id=1, source_target_pairs={{0,2},{1,3},{2,0},{3,1},{4,6},{5,7},{6,4},{7,5},{8,10},{9,11},{10,... | collective-permute-start | bytes 393224 | tf_op jit(solution)/shard_map/ppermute | solution.py:329
  4.9 11.4 %collective-permute-start.11 = (f32[2,32,512]{2,1,0:T(8,128)S(1)}, f32[2,32,512]{2,1,0:T(8,128)S(1)}, u32[]{:S(2)}, u32[]{:S(2)}) collective-permute-start(f32[2,32,512]{2,1,0:T(8,128)S(1)} %get-tuple-element.26), channel_id=1, source_target_pairs={{0,3},{1,2},{2,1},{3,0},{4,7},{5,6},{6,5},{7,4},{8,11},{9,10},{10,... | collective-permute-start | bytes 393224 | tf_op jit(solution)/shard_map/ppermute | solution.py:329
  4.9 0.8 %copy-start.3 = (f32[2,64,128]{2,1,0:T(8,128)S(1)}, f32[2,64,128]{2,1,0:T(8,128)}, u32[]{:S(2)}) copy-start(f32[2,64,128]{2,1,0:T(8,128)} %flux_ref.1) | copy-start | bytes 196612
  5.8 0.8 %copy-start.4 = (f32[2,32,128]{2,1,0:T(8,128)S(1)}, f32[2,32,128]{2,1,0:T(8,128)}, u32[]{:S(2)}) copy-start(f32[2,32,128]{2,1,0:T(8,128)} %cycles_ref.1) | copy-start | bytes 98308
  6.7 5.5 %collective-permute-start.4 = (f32[2,32,128]{2,1,0:T(8,128)S(1)}, f32[2,32,128]{2,1,0:T(8,128)S(1)}, u32[]{:S(2)}, u32[]{:S(2)}) collective-permute-start(f32[2,32,128]{2,1,0:T(8,128)S(1)} %inject.1.refs_0_), channel_id=1, source_target_pairs={{0,2},{1,3},{2,0},{3,1},{4,6},{5,7},{6,4},{7,5},{8,10},{9,11},{10,... | collective-permute-start | bytes 98312 | tf_op jit(solution)/shard_map/ppermute | solution.py:329
  8.4 4.5 %collective-permute-start.3 = (f32[2,32,128]{2,1,0:T(8,128)S(1)}, f32[2,32,128]{2,1,0:T(8,128)S(1)}, u32[]{:S(2)}, u32[]{:S(2)}) collective-permute-start(f32[2,32,128]{2,1,0:T(8,128)S(1)} %inject.1.refs_0_), channel_id=1, source_target_pairs={{0,1},{1,0},{2,3},{3,2},{4,5},{5,4},{6,7},{7,6},{8,9},{9,8},{10,11... | collective-permute-start | bytes 98312 | tf_op jit(solution)/shard_map/ppermute | solution.py:329
  12.2 2.3 %collective-permute-start.5 = (f32[2,32,128]{2,1,0:T(8,128)S(1)}, f32[2,32,128]{2,1,0:T(8,128)S(1)}, u32[]{:S(2)}, u32[]{:S(2)}) collective-permute-start(f32[2,32,128]{2,1,0:T(8,128)S(1)} %collective-permute-done.4.refs_2_), channel_id=1, source_target_pairs={{0,1},{1,0},{2,3},{3,2},{4,5},{5,4},{6,7},{7,6},{8,9},{9,8},{10,11... | collective-permute-start | bytes 98312 | tf_op jit(solution)/shard_map/ppermute | solution.py:329
  12.9 8.7 %collective-permute-start.8 = (f32[2,32,1152]{2,1,0:T(8,128)S(1)}, f32[2,32,1152]{2,1,0:T(8,128)S(1)}, u32[]{:S(2)}, u32[]{:S(2)}) collective-permute-start(f32[2,32,1152]{2,1,0:T(8,128)S(1)} %get-tuple-element.23), channel_id=1, source_target_pairs={{0,2},{1,3},{2,0},{3,1},{4,6},{5,7},{6,4},{7,5},{8,10},{9,11},{10,... | collective-permute-start | bytes 884744 | tf_op jit(solution)/shard_map/ppermute | solution.py:329
  14.5 2.9 %copy-start.2 = (f32[3072,8,8]{0,2,1:T(8,128)S(1)}, f32[3072,8,8]{0,2,1:T(8,128)}, u32[]{:S(2)}) copy-start(f32[3072,8,8]{0,2,1:T(8,128)} %param.10) | copy-start | bytes 2359300
  14.5 2.9 %copy-start.5 = (s32[2]{0:T(128)S(1)}, s32[2]{0:T(128)}, u32[]{:S(2)}) copy-start(s32[2]{0:T(128)} %order_ref.9) | copy-start | bytes 28
  14.5 13.9 %collective-permute-start.9 = (f32[2,32,1152]{2,1,0:T(8,128)S(1)}, f32[2,32,1152]{2,1,0:T(8,128)S(1)}, u32[]{:S(2)}, u32[]{:S(2)}) collective-permute-start(f32[2,32,1152]{2,1,0:T(8,128)S(1)} %get-tuple-element.24), channel_id=1, source_target_pairs={{0,3},{1,2},{2,1},{3,0},{4,7},{5,6},{6,5},{7,4},{8,11},{9,10},{10,... | collective-permute-start | bytes 884744 | tf_op jit(solution)/shard_map/ppermute | solution.py:329
  15.5 19.8 %collective-permute-start.6 = (f32[2,32,1152]{2,1,0:T(8,128)S(1)}, f32[2,32,1152]{2,1,0:T(8,128)S(1)}, u32[]{:S(2)}, u32[]{:S(2)}) collective-permute-start(f32[2,32,1152]{2,1,0:T(8,128)S(1)} %get-tuple-element.21), channel_id=1, source_target_pairs={{0,2},{1,3},{2,0},{3,1},{4,6},{5,7},{6,4},{7,5},{8,10},{9,11},{10,... | collective-permute-start | bytes 884744 | tf_op jit(solution)/shard_map/ppermute | solution.py:329
  16.3 24.8 %collective-permute-start.7 = (f32[2,32,1152]{2,1,0:T(8,128)S(1)}, f32[2,32,1152]{2,1,0:T(8,128)S(1)}, u32[]{:S(2)}, u32[]{:S(2)}) collective-permute-start(f32[2,32,1152]{2,1,0:T(8,128)S(1)} %get-tuple-element.22), channel_id=1, source_target_pairs={{0,3},{1,2},{2,1},{3,0},{4,7},{5,6},{6,5},{7,4},{8,11},{9,10},{10,... | collective-permute-start | bytes 884744 | tf_op jit(solution)/shard_map/ppermute | solution.py:329
  18.5 29.5 %collective-permute-start.1 = (f32[2,32,256]{2,1,0:T(8,128)S(1)}, f32[2,32,256]{2,1,0:T(8,128)S(1)}, u32[]{:S(2)}, u32[]{:S(2)}) collective-permute-start(f32[2,32,256]{2,1,0:T(8,128)S(1)} %get-tuple-element.19), channel_id=1, source_target_pairs={{0,2},{1,3},{2,0},{3,1},{4,6},{5,7},{6,4},{7,5},{8,10},{9,11},{10,... | collective-permute-start | bytes 196616 | tf_op jit(solution)/shard_map/ppermute | solution.py:329
  21.7 26.3 %collective-permute-start.2 = (f32[2,32,256]{2,1,0:T(8,128)S(1)}, f32[2,32,256]{2,1,0:T(8,128)S(1)}, u32[]{:S(2)}, u32[]{:S(2)}) collective-permute-start(f32[2,32,256]{2,1,0:T(8,128)S(1)} %get-tuple-element.20), channel_id=1, source_target_pairs={{0,3},{1,2},{2,1},{3,0},{4,7},{5,6},{6,5},{7,4},{8,11},{9,10},{10,... | collective-permute-start | bytes 196616 | tf_op jit(solution)/shard_map/ppermute | solution.py:329
  49.1 2.2 %collective-permute-start.12 = (f32[72,128]{1,0:T(8,128)S(1)}, f32[72,128]{1,0:T(8,128)S(1)}, u32[]{:S(2)}, u32[]{:S(2)}) collective-permute-start(f32[72,128]{1,0:T(8,128)S(1)} %get-tuple-element.28), channel_id=1, source_target_pairs={{0,1},{1,0},{2,3},{3,2},{4,5},{5,4},{6,7},{7,6},{8,9},{9,8},{10,11... | collective-permute-start | bytes 110600 | tf_op jit(solution)/shard_map/ppermute | solution.py:329
  49.2 2.9 %collective-permute-start.13 = (f32[72,128]{1,0:T(8,128)S(1)}, f32[72,128]{1,0:T(8,128)S(1)}, u32[]{:S(2)}, u32[]{:S(2)}) collective-permute-start(f32[72,128]{1,0:T(8,128)S(1)} %get-tuple-element.29), channel_id=1, source_target_pairs={{0,2},{1,3},{2,0},{3,1},{4,6},{5,7},{6,4},{7,5},{8,10},{9,11},{10,... | collective-permute-start | bytes 110600 | tf_op jit(solution)/shard_map/ppermute | solution.py:329
  50.7 4.0 %collective-permute-start.14 = (f32[72,128]{1,0:T(8,128)S(1)}, f32[72,128]{1,0:T(8,128)S(1)}, u32[]{:S(2)}, u32[]{:S(2)}) collective-permute-start(f32[72,128]{1,0:T(8,128)S(1)} %get-tuple-element.30), channel_id=1, source_target_pairs={{0,3},{1,2},{2,1},{3,0},{4,7},{5,6},{6,5},{7,4},{8,11},{9,10},{10,... | collective-permute-start | bytes 110600 | tf_op jit(solution)/shard_map/ppermute | solution.py:329

commit v2 on v1

--- a/solution.py
+++ b/solution.py
@@ -8,6 +8,7 @@
 from jax.sharding import PartitionSpec as P
 
 LANES = 128
+FREE = pl.CostEstimate(flops=0, bytes_accessed=0, transcendentals=0)
 VMEM_LIMIT = 48 * 1024 * 1024
 
 
@@ -17,13 +18,14 @@
 
 def split_degrees(blocks):
     tiles = blocks // LANES
-    if tiles < 12:
+    if tiles < 24:
         return [blocks]
-    first = tiles // 6
-    last = tiles // 12
-    middle = tiles - first - last
-    half = middle // 2
-    return [w * LANES for w in (first, half, middle - half, last)]
+    widths = [8, tiles - 14, 4, 2]
+    return [w * LANES for w in widths]
+
+
+def in_hbm(*arrays):
+    return [pltpu.with_memory_space_constraint(array, pltpu.HBM) for array in arrays]
 
 
 def halves(value):
@@ -36,16 +38,22 @@
     return pltpu.CompilerParams(vmem_limit_bytes=VMEM_LIMIT, **kwargs)
 
 
-def cut_kernel(pieces, blocks, me_ref, legendre_ref, *refs):
-    outs, sems = refs[:-1], refs[-1]
+def cut_copies(pieces, blocks, me, legendre_ref, outs, sems):
     copies = []
     for number, (x, offset, width) in enumerate(pieces):
-        start = pl.multiple_of((me_ref[0] ^ x) * blocks + offset, LANES)
+        start = pl.multiple_of((me ^ x) * blocks + offset, LANES)
         copies.append(
             pltpu.make_async_copy(
-                legendre_ref.at[:, :, pl.ds(start, width)], outs[number], sems.at[number]
+                legendre_ref.at[:, :, pl.ds(start, width)],
+                outs[number].at[:, :, pl.ds(0, width)],
+                sems.at[number],
             )
         )
+    return copies
+
+
+def cut_kernel(pieces, blocks, me_ref, legendre_ref, *refs):
+    copies = cut_copies(pieces, blocks, me_ref[0], legendre_ref, refs[:-1], refs[-1])
     for copy in copies:
         copy.start()
     for copy in copies:
@@ -59,44 +67,82 @@
     return pl.pallas_call(
         functools.partial(cut_kernel, pieces, blocks),
         out_shape=shapes,
-        in_specs=[pl.BlockSpec(memory_space=pltpu.SMEM), pl.BlockSpec(memory_space=pl.ANY)],
+        in_specs=[pl.BlockSpec(memory_space=pltpu.SMEM), pl.BlockSpec(memory_space=pltpu.HBM)],
         out_specs=[pl.BlockSpec(memory_space=pl.ANY)] * len(pieces),
         scratch_shapes=[pltpu.SemaphoreType.DMA((len(pieces),))],
         compiler_params=compiler_params(),
-        cost_estimate=pl.CostEstimate(flops=0, bytes_accessed=2 * size, transcendentals=0),
+        cost_estimate=pl.CostEstimate(flops=0, bytes_accessed=40 * size, transcendentals=0),
         name="cut",
-    )(me, legendre)
-
-
-def inject_kernel(me_ref, cycles_ref, weight_ref, hits_ref, flux_ref, out_ref):
-    orders, rows, _ = cycles_ref.shape
-    count = hits_ref.shape[1]
+    )(me, *in_hbm(legendre))
+
+
+def open_kernel(
+    pieces, blocks, me_ref, legendre_ref, cycles_ref, weight_ref, hits_ref, flux_ref, *refs
+):
+    count = len(pieces)
+    outs, own_ref = refs[:count], refs[count]
+    cycles, weight, hit_cycles, flux, sems, small_sems = refs[count + 1 :]
+    orders, rows, columns = cycles.shape
+    clusters = flux.shape[1]
+    small = [
+        pltpu.make_async_copy(source, target, small_sems.at[number])
+        for number, (source, target) in enumerate(
+            [(cycles_ref, cycles), (weight_ref, weight), (hits_ref, hit_cycles), (flux_ref, flux)]
+        )
+    ]
+    copies = cut_copies(pieces, blocks, me_ref[0], legendre_ref, outs, sems)
+    for copy in small + copies:
+        copy.start()
+    for copy in small:
+        copy.wait()
     eye = lax.broadcasted_iota(jnp.int32, (rows, rows), 0) == lax.broadcasted_iota(
         jnp.int32, (rows, rows), 1
     )
-    weight = jnp.sum(jnp.where(eye, weight_ref[...], 0.0), axis=1, keepdims=True)
-    ids = me_ref[0] * rows + lax.broadcasted_iota(jnp.int32, (rows, count), 0)
+    weight_column = jnp.sum(jnp.where(eye, weight[...], 0.0), axis=1, keepdims=True)
+    ids = me_ref[0] * rows + lax.broadcasted_iota(jnp.int32, (rows, clusters), 0)
     for k in range(orders):
-        hits = (ids == hits_ref[k : k + 1, :]).astype(jnp.float32)
+        hits = (ids == hit_cycles[k : k + 1, :]).astype(jnp.float32)
         added = jnp.dot(
             hits,
-            flux_ref[k],
+            flux[k],
             precision=lax.Precision.HIGHEST,
             preferred_element_type=jnp.float32,
         )
-        out_ref[k] = weight * (cycles_ref[k] + added)
-
-
-def inject(me, cycles, weight, cluster_cycles, flux):
-    vmem = pl.BlockSpec(memory_space=pltpu.VMEM)
-    return pl.pallas_call(
-        inject_kernel,
-        out_shape=jax.ShapeDtypeStruct(cycles.shape, jnp.float32),
-        in_specs=[pl.BlockSpec(memory_space=pltpu.SMEM), vmem, vmem, vmem, vmem],
-        out_specs=vmem,
+        own_ref[k] = weight_column * (cycles[k] + added)
+    tail = pltpu.make_async_copy(
+        own_ref, outs[0].at[:, :, pl.ds(pieces[0][2], columns)], small_sems.at[0]
+    )
+    tail.start()
+    for copy in copies + [tail]:
+        copy.wait()
+
+
+def open_blocks(me, legendre, cycles, weight, cluster_cycles, flux, pieces, blocks):
+    orders, rows, columns = cycles.shape
+    shapes = [jax.ShapeDtypeStruct((orders, rows, w), jnp.float32) for _, _, w in pieces]
+    shapes[0] = jax.ShapeDtypeStruct((orders, rows, pieces[0][2] + columns), jnp.float32)
+    shapes.append(jax.ShapeDtypeStruct(cycles.shape, jnp.float32))
+    size = sum(orders * rows * w * 4 for _, _, w in pieces)
+    hbm = pl.BlockSpec(memory_space=pltpu.HBM)
+    weight = weight.reshape(1, -1)
+    return pl.pallas_call(
+        functools.partial(open_kernel, pieces, blocks),
+        out_shape=shapes,
+        in_specs=[pl.BlockSpec(memory_space=pltpu.SMEM)] + [hbm] * 5,
+        out_specs=[pl.BlockSpec(memory_space=pl.ANY)] * len(pieces)
+        + [pl.BlockSpec(memory_space=pltpu.VMEM)],
+        scratch_shapes=[
+            pltpu.VMEM(cycles.shape, jnp.float32),
+            pltpu.VMEM(weight.shape, jnp.float32),
+            pltpu.VMEM(cluster_cycles.shape, jnp.int32),
+            pltpu.VMEM(flux.shape, jnp.float32),
+            pltpu.SemaphoreType.DMA((len(pieces),)),
+            pltpu.SemaphoreType.DMA((4,)),
+        ],
         compiler_params=compiler_params(),
-        name="inject",
-    )(me, cycles, weight.reshape(1, -1), cluster_cycles, flux)
+        cost_estimate=FREE,
+        name="open",
+    )(me, *in_hbm(legendre, cycles, weight, cluster_cycles, flux))
 
 
 def response_kernel(blocks, scales, skies, me_ref, order_ref, weights_ref, out_ref):
@@ -130,6 +176,7 @@
         in_specs=[smem, smem, vmem],
         out_specs=vmem,
         compiler_params=compiler_params(),
+        cost_estimate=FREE,
         name="response",
     )(me, order_per_slot, weights)
 
@@ -143,16 +190,21 @@
 
 
 def prepare(pieces):
-    orders, rows, columns = pieces[0].shape
-    vmem = pl.BlockSpec(memory_space=pltpu.VMEM)
+    orders, rows, columns = pieces[0][0].shape
+    count = len(pieces)
     return pl.pallas_call(
         prepare_kernel,
-        out_shape=jax.ShapeDtypeStruct((orders, columns, 3 * rows * len(pieces)), jnp.bfloat16),
-        in_specs=[vmem] * len(pieces),
-        out_specs=vmem,
+        out_shape=jax.ShapeDtypeStruct((orders, columns, 3 * rows * count), jnp.bfloat16),
+        grid=(1,),
+        in_specs=[
+            pl.BlockSpec((orders, rows, columns), lambda i, block=at // columns: (0, 0, block))
+            for _, at in pieces
+        ],
+        out_specs=pl.BlockSpec((orders, columns, 3 * rows * count), lambda i: (0, 0, 0)),
         compiler_params=compiler_params(),
+        cost_estimate=FREE,
         name="prepare",
-    )(*pieces)
+    )(*[array for array, _ in pieces])
 
 
 def chunk_kernel(n, first, last, blocks, offset, tile, me_ref, order_ref, *refs):
@@ -225,9 +277,9 @@
                 rest[x][orders * rows :, :] = response[...]
 
 
-def chunk(me, order_per_slot, legendre, parts, analysis, weights, before, response, blocks, offset, width):
-    n = len(parts) + 1
-    orders, rows, _ = legendre.shape
+def chunk(me, order_per_slot, parts, analysis, weights, before, response, blocks, offset, width):
+    n = len(parts)
+    orders, rows, _ = parts[0][0].shape
     columns = analysis.shape[1]
     scales, channels, _ = weights.shape
     tile = next(t for t in (512, 384, 256, 128) if width % t == 0 and offset % t == 0 and blocks % t == 0)
@@ -238,13 +290,9 @@
     def at(start):
         return pl.BlockSpec((orders, rows, tile), lambda i, me, order: (0, 0, start // tile + i))
 
-    own = pl.BlockSpec(
-        (orders, rows, tile),
-        lambda i, me, order: (0, 0, me[0] * (blocks // tile) + offset // tile + i),
-    )
     whole = lambda array: pl.BlockSpec(array.shape, lambda i, me, order: (0,) * array.ndim)
-    operands = [legendre] + [array for array, _ in parts] + [analysis, weights]
-    in_specs = [own] + [at(start) for _, start in parts]
+    operands = [array for array, _ in parts] + [analysis, weights]
+    in_specs = [at(start) for _, start in parts]
     in_specs += [
         whole(analysis),
         pl.BlockSpec((scales, channels, tile), lambda i, me, order: (0, 0, offset // tile + i)),
@@ -272,11 +320,7 @@
             scratch_shapes=[pltpu.VMEM((orders, 2 * n * rows, 2 * columns), jnp.float32)],
         ),
         compiler_params=compiler_params(dimension_semantics=("arbitrary",)),
-        cost_estimate=pl.CostEstimate(
-            flops=2 * 7 * macs,
-            bytes_accessed=4 * orders * n * rows * width,
-            transcendentals=0,
-        ),
+        cost_estimate=FREE,
         name="chunk",
     )(me, order_per_slot, *operands)
 
@@ -302,6 +346,7 @@
         in_specs=[vmem] * len(parts),
         out_specs=vmem,
         compiler_params=compiler_params(),
+        cost_estimate=FREE,
         name="finish",
     )(*parts)
 
@@ -329,35 +374,48 @@
         return lax.ppermute(value, "blk", partner(x, n))
 
     far = range(2, n)
-    sent = []
-    for c, (offset, width) in enumerate(zip(offsets, widths)):
-        pieces = [(x, offset, width) for x in far]
-        if c == 0:
-            pieces.append((1, 0, blocks))
-        cuts = list(cut(me, legendre, pieces, blocks))
-        if c == 0:
-            near = send(cuts.pop(), 1)
-        sent.append([send(value, x) for value, x in zip(cuts, far)])
-
-    own = inject(me, fourier_cycles, cycle_weight, cluster_cycles, cluster_flux)
-    cycles = {0: own}
-    bit = n // 2
+    first = widths[0]
+    top = n // 2
+    order = [top] + [x for x in far if x != top]
+    *cuts, near, own = open_blocks(
+        me,
+        legendre,
+        fourier_cycles,
+        cycle_weight,
+        cluster_cycles,
+        cluster_flux,
+        [(x, 0, first) for x in order] + [(1, 0, blocks)],
+        blocks,
+    )
+    sent = [{x: send(value, x) for value, x in zip(cuts, order)}]
+    then, _ = lax.optimization_barrier((me, cuts[0]))
+    pieces = [(x, at, w) for at, w in zip(offsets[1:], widths[1:]) for x in order]
+    *cuts, home = cut(then, legendre, pieces + [(0, 0, blocks)], blocks)
+    for c in range(len(widths) - 1):
+        sent.append({x: send(value, x) for value, x in zip(cuts[c * (n - 2) :], order)})
+    near = send(near, 1)
+    for c, offset in enumerate(offsets):
+        sent[c] = {x: (value, 0) for x, value in sent[c].items()}
+        sent[c][0] = (home, offset)
+        sent[c][1] = (near, offset)
+
+    cycles = {0: (own, 0), top: (sent[0][top][0], first)}
+    bit = top // 2
     while bit:
         for x in list(cycles):
-            cycles[x ^ bit] = send(cycles[x], bit)
+            value, at = cycles[x]
+            cycles[x ^ bit] = (send(value[:, :, at : at + columns], bit), 0)
         bit //= 2
     analysis = prepare([cycles[x] for x in range(n)])
     response = response_rows(me, order_per_slot, weights, skies, columns)
 
     total = None
     for c, (offset, width) in enumerate(zip(offsets, widths)):
-        parts = [(near, offset)] + [(value, 0) for value in sent[c]]
         final = c == len(widths) - 1
         result = chunk(
             me,
             order_per_slot,
-            legendre,
-            parts,
+            [sent[c][x] for x in range(n)],
             analysis,
             weights,
             total,

time: 56 us -> 47.5 us (0.85)
  Pallas kernels: 18.6 us -> 14.5 us
  local copies, waits for them, and re-layouts: 3.53 us -> 0.01 us
  starting transfers between devices: 15.5 us -> 12.8 us
  waiting for transfers between devices: 17.6 us -> 19.7 us
    pallas_call x4, Pallas kernels: 16.5 us -> 9.8 us  [chunk(): pl.pallas_call(functools.partial(chunk_kernel, n, first, last, blocks, of...]
    unnamed x16 -> x4, local copies, waits for them, and re-layouts: 3.53 us -> 0.01 us
    ppermute x15 -> x14, starting transfers between devices: 15.5 us -> 12.8 us  [send(): return lax.ppermute(value, 'blk', partner(x, n))]
    ppermute x15 -> x14, waiting for transfers between devices: 17.6 us -> 19.7 us  [send(): return lax.ppermute(value, 'blk', partner(x, n))]
    pallas_call x1, Pallas kernels: 0.14 us -> 1.5 us  [open_blocks(): pl.pallas_call(functools.partial(open_kernel, pieces, blocks), out_shape=...]
    pallas_call x4 -> x1, Pallas kernels: 0.3 us -> 1.52 us  [cut(): pl.pallas_call(functools.partial(cut_kernel, pieces, blocks), out_shape=s...]
  transfers between devices with their start and end apart: 15 -> 14, of which waited for: 6 -> 9; matrix products, arithmetic and copies ran while one was open for 0% -> 0% of each run, Pallas kernels for 30% -> 24%
where the time goes in v2:
time: 47.5 us; the launch traced here: 47 us
  waiting for transfers between devices  19.7 us (41%)
  Pallas kernels  14.5 us (31%)
  starting transfers between devices  12.8 us (27%)
    ppermute x14, waiting for transfers between devices, send(): return lax.ppermute(value, 'blk', partner(x, n))  19.7 us
    ppermute x14, starting transfers between devices, send(): return lax.ppermute(value, 'blk', partner(x, n))  12.8 us
    pallas_call x4, Pallas kernels, chunk(): pl.pallas_call(functools.partial(chunk_kernel, n, first, last, blocks, of...  9.8 us
    pallas_call x1, Pallas kernels, cut(): pl.pallas_call(functools.partial(cut_kernel, pieces, blocks), out_shape=s...  1.52 us
    pallas_call x1, Pallas kernels, open_blocks(): pl.pallas_call(functools.partial(open_kernel, pieces, blocks), out_shape=...  1.5 us
  transfers between devices with their start and end apart: 14, of which 9 were waited for; matrix products, arithmetic and copies ran while one was open for 0% of the time, Pallas kernels for 24%

profile of v2, /device:TPU:1, one launch (start us, length us, event | category | flops | bytes accessed | tf_op | source)
XLA Modules:
  0.0 47.0 jit_solution(392895869984518124)
XLA Ops:
  0.0 1.5 %open.1 = (f32[2,32,1152]{2,1,0:T(8,128)S(1)}, f32[2,32,1024]{2,1,0:T(8,128)S(1)}, f32[2,32,3072]{2,1,0:T(8,128)S(1)}, f32[2,32,128]{2,1,0:T(8,128)S(1)}) custom-call(s32[1]{0:T(128)} %bitcast.me_ref, f32[2,32,12288]{2,1,0:T(8,128)} %legendre_ref.3, f32[2,32,128]{2,1,0:T(8,128)} %cycles_ref.1, f32[1,32]{1,0:T(1,128)} %bitcast.8, s32[2,64]{1,0:T(2,128)} %hits_ref.1, ...), custom_call_target="tpu_custom_call" | custom-call | tf_op jit(solution)/shard_map/open/pallas_call | solution.py:128
  1.5 0.1 collective-permute-start
  1.6 2.7 %collective-permute-start.4 = (f32[2,32,1152]{2,1,0:T(8,128)S(1)}, f32[2,32,1152]{2,1,0:T(8,128)S(1)}, u32[]{:S(2)}, u32[]{:S(2)}) collective-permute-start(f32[2,32,1152]{2,1,0:T(8,128)S(1)} %get-tuple-element.21), channel_id=1, source_target_pairs={{0,2},{1,3},{2,0},{3,1},{4,6},{5,7},{6,4},{7,5},{8,10},{9,11},{10,... | collective-permute-start | bytes 884744 | tf_op jit(solution)/shard_map/ppermute | solution.py:374
  4.3 0.0 collective-permute-start.10
  4.4 1.5 %cut.1 = (f32[2,32,1280]{2,1,0:T(8,128)S(1)}, f32[2,32,1280]{2,1,0:T(8,128)S(1)}, f32[2,32,512]{2,1,0:T(8,128)S(1)}, f32[2,32,512]{2,1,0:T(8,128)S(1)}, f32[2,32...) custom-call(s32[1]{0:T(128)} %bitcast.me_ref, f32[2,32,12288]{2,1,0:T(8,128)} %legendre_ref.3), custom_call_target="tpu_custom_call" | custom-call | bytes 73400320 | tf_op jit(solution)/shard_map/cut/pallas_call | solution.py:67
  5.9 1.7 %collective-permute-start.8 = (f32[2,32,1280]{2,1,0:T(8,128)S(1)}, f32[2,32,1280]{2,1,0:T(8,128)S(1)}, u32[]{:S(2)}, u32[]{:S(2)}) collective-permute-start(f32[2,32,1280]{2,1,0:T(8,128)S(1)} %get-tuple-element.30), channel_id=1, source_target_pairs={{0,2},{1,3},{2,0},{3,1},{4,6},{5,7},{6,4},{7,5},{8,10},{9,11},{10,... | collective-permute-start | bytes 983048 | tf_op jit(solution)/shard_map/ppermute | solution.py:374
  7.6 0.3 collective-permute-start.9
  8.0 3.7 %collective-permute-done.4.refs_2_ = f32[2,32,1152]{2,1,0:T(8,128)S(1)} collective-permute-done((f32[2,32,1152]{2,1,0:T(8,128)S(1)}, f32[2,32,1152]{2,1,0:T(8,128)S(1)}, u32[]{:S(2)}, u32[]{:S(2)}) %collective-permute-start.4) | collective-permute-done | bytes 294944 | tf_op jit(solution)/shard_map/ppermute | solution.py:374
  11.6 0.9 %collective-permute-start.3 = (f32[2,32,128]{2,1,0:T(8,128)S(1)}, f32[2,32,128]{2,1,0:T(8,128)S(1)}, u32[]{:S(2)}, u32[]{:S(2)}) collective-permute-start(f32[2,32,128]{2,1,0:T(8,128)S(1)} %get-tuple-element.27.refs_0_), channel_id=1, source_target_pairs={{0,1},{1,0},{2,3},{3,2},{4,5},{5,4},{6,7},{7,6},{8,9},{9,8},{10,11... | collective-permute-start | bytes 98312 | tf_op jit(solution)/shard_map/ppermute | solution.py:374
  12.5 0.9 %collective-permute-done.3.refs_1_ = f32[2,32,128]{2,1,0:T(8,128)S(1)} collective-permute-done((f32[2,32,128]{2,1,0:T(8,128)S(1)}, f32[2,32,128]{2,1,0:T(8,128)S(1)}, u32[]{:S(2)}, u32[]{:S(2)}) %collective-permute-start.3) | collective-permute-done | bytes 32800 | tf_op jit(solution)/shard_map/ppermute | solution.py:374
  13.4 0.3 collective-permute-start.5
  13.7 3.7 %collective-permute-done.10.refs_3_ = f32[2,32,1024]{2,1,0:T(8,128)S(1)} collective-permute-done((f32[2,32,1024]{2,1,0:T(8,128)S(1)}, f32[2,32,1024]{2,1,0:T(8,128)S(1)}, u32[]{:S(2)}, u32[]{:S(2)}) %collective-permute-start.10) | collective-permute-done | bytes 262176 | tf_op jit(solution)/shard_map/ppermute | solution.py:374
  17.5 1.7 %collective-permute-start.6 = (f32[2,32,512]{2,1,0:T(8,128)S(1)}, f32[2,32,512]{2,1,0:T(8,128)S(1)}, u32[]{:S(2)}, u32[]{:S(2)}) collective-permute-start(f32[2,32,512]{2,1,0:T(8,128)S(1)} %get-tuple-element.28), channel_id=1, source_target_pairs={{0,2},{1,3},{2,0},{3,1},{4,6},{5,7},{6,4},{7,5},{8,10},{9,11},{10,... | collective-permute-start | bytes 393224 | tf_op jit(solution)/shard_map/ppermute | solution.py:374
  19.1 0.1 collective-permute-start.7
  19.3 5.0 %collective-permute-done.8.refs_2_ = f32[2,32,1280]{2,1,0:T(8,128)S(1)} collective-permute-done((f32[2,32,1280]{2,1,0:T(8,128)S(1)}, f32[2,32,1280]{2,1,0:T(8,128)S(1)}, u32[]{:S(2)}, u32[]{:S(2)}) %collective-permute-start.8) | collective-permute-done | bytes 327712 | tf_op jit(solution)/shard_map/ppermute | solution.py:374
  24.3 1.3 %collective-permute-start.1 = (f32[2,32,256]{2,1,0:T(8,128)S(1)}, f32[2,32,256]{2,1,0:T(8,128)S(1)}, u32[]{:S(2)}, u32[]{:S(2)}) collective-permute-start(f32[2,32,256]{2,1,0:T(8,128)S(1)} %get-tuple-element.25), channel_id=1, source_target_pairs={{0,2},{1,3},{2,0},{3,1},{4,6},{5,7},{6,4},{7,5},{8,10},{9,11},{10,... | collective-permute-start | bytes 196616 | tf_op jit(solution)/shard_map/ppermute | solution.py:374
  25.6 1.3 %collective-permute-start.2 = (f32[2,32,256]{2,1,0:T(8,128)S(1)}, f32[2,32,256]{2,1,0:T(8,128)S(1)}, u32[]{:S(2)}, u32[]{:S(2)}) collective-permute-start(f32[2,32,256]{2,1,0:T(8,128)S(1)} %get-tuple-element.26), channel_id=1, source_target_pairs={{0,3},{1,2},{2,1},{3,0},{4,7},{5,6},{6,5},{7,4},{8,11},{9,10},{10,... | collective-permute-start | bytes 196616 | tf_op jit(solution)/shard_map/ppermute | solution.py:374
  26.8 0.9 %response.1.refs_7_ = f32[8,128]{1,0:T(8,128)S(1)} custom-call(s32[1]{0:T(128)} %bitcast.me_ref, s32[2]{0:T(128)S(1)} %copy-done.1, f32[8,8,3072]{2,1,0:T(8,128)S(1)} %bitcast.3), custom_call_target="tpu_custom_call" | custom-call | tf_op jit(solution)/shard_map/response/pallas_call | solution.py:173
  27.7 0.1 prepare.1.refs_4_
  27.9 2.9 %chunk.4.refs_6_ = f32[2,128,128]{2,1,0:T(8,128)S(1)} custom-call(s32[1]{0:T(128)} %bitcast.me_ref, s32[2]{0:T(128)S(1)} %copy-done.1, f32[2,32,3072]{2,1,0:T(8,128)S(1)} %get-tuple-element.23.refs_0_, f32[2,32,3072]{2,1,0:T(8,128)S(1)} %collective-permute-done.refs_1_, f32[2,32,1152]{2,1,0:T(8,128)S(1)} %collective-permute-done.4.refs_2_, ...), custom_call_target="tpu_custom_call" | custom-call | tf_op jit(solution)/shard_map/chunk/pallas_call | solution.py:312
  30.8 0.7 %collective-permute-done.9.refs_3_ = f32[2,32,1280]{2,1,0:T(8,128)S(1)} collective-permute-done((f32[2,32,1280]{2,1,0:T(8,128)S(1)}, f32[2,32,1280]{2,1,0:T(8,128)S(1)}, u32[]{:S(2)}, u32[]{:S(2)}) %collective-permute-start.9) | collective-permute-done | bytes 327712 | tf_op jit(solution)/shard_map/ppermute | solution.py:374
  31.5 3.8 %chunk.5.refs_6_ = f32[2,128,128]{2,1,0:T(8,128)S(1)} custom-call(s32[1]{0:T(128)} %bitcast.me_ref, s32[2]{0:T(128)S(1)} %copy-done.1, f32[2,32,3072]{2,1,0:T(8,128)S(1)} %get-tuple-element.23.refs_0_, f32[2,32,3072]{2,1,0:T(8,128)S(1)} %collective-permute-done.refs_1_, f32[2,32,1280]{2,1,0:T(8,128)S(1)} %collective-permute-done.8.refs_2_, ...), custom_call_target="tpu_custom_call" | custom-call | tf_op jit(solution)/shard_map/chunk/pallas_call | solution.py:312
  35.4 1.8 %collective-permute-done.7.refs_3_ = f32[2,32,512]{2,1,0:T(8,128)S(1)} collective-permute-done((f32[2,32,512]{2,1,0:T(8,128)S(1)}, f32[2,32,512]{2,1,0:T(8,128)S(1)}, u32[]{:S(2)}, u32[]{:S(2)}) %collective-permute-start.7) | collective-permute-done | bytes 131104 | tf_op jit(solution)/shard_map/ppermute | solution.py:374
  37.1 1.9 %chunk.6.refs_6_ = f32[2,128,128]{2,1,0:T(8,128)S(1)} custom-call(s32[1]{0:T(128)} %bitcast.me_ref, s32[2]{0:T(128)S(1)} %copy-done.1, f32[2,32,3072]{2,1,0:T(8,128)S(1)} %get-tuple-element.23.refs_0_, f32[2,32,3072]{2,1,0:T(8,128)S(1)} %collective-permute-done.refs_1_, f32[2,32,512]{2,1,0:T(8,128)S(1)} %collective-permute-done.6.refs_2_, ...), custom_call_target="tpu_custom_call" | custom-call | tf_op jit(solution)/shard_map/chunk/pallas_call | solution.py:312
  39.1 0.7 %collective-permute-done.2.refs_3_ = f32[2,32,256]{2,1,0:T(8,128)S(1)} collective-permute-done((f32[2,32,256]{2,1,0:T(8,128)S(1)}, f32[2,32,256]{2,1,0:T(8,128)S(1)}, u32[]{:S(2)}, u32[]{:S(2)}) %collective-permute-start.2) | collective-permute-done | bytes 65568 | tf_op jit(solution)/shard_map/ppermute | solution.py:374
  39.7 1.1 %chunk.7 = (f32[72,128]{1,0:T(8,128)S(1)}, f32[72,128]{1,0:T(8,128)S(1)}, f32[72,128]{1,0:T(8,128)S(1)}, f32[72,128]{1,0:T(8,128)S(1)}) custom-call(s32[1]{0:T(128)} %bitcast.me_ref, s32[2]{0:T(128)S(1)} %copy-done.1, f32[2,32,3072]{2,1,0:T(8,128)S(1)} %get-tuple-element.23.refs_0_, f32[2,32,3072]{2,1,0:T(8,128)S(1)} %collective-permute-done.refs_1_, ...), custom_call_target="tpu_custom_call" | custom-call | tf_op jit(solution)/shard_map/chunk/pallas_call | solution.py:312
  40.8 0.5 collective-permute-start.11
  41.3 1.3 %collective-permute-start.12 = (f32[72,128]{1,0:T(8,128)S(1)}, f32[72,128]{1,0:T(8,128)S(1)}, u32[]{:S(2)}, u32[]{:S(2)}) collective-permute-start(f32[72,128]{1,0:T(8,128)S(1)} %get-tuple-element.35), channel_id=1, source_target_pairs={{0,2},{1,3},{2,0},{3,1},{4,6},{5,7},{6,4},{7,5},{8,10},{9,11},{10,... | collective-permute-start | bytes 110600 | tf_op jit(solution)/shard_map/ppermute | solution.py:374
  42.6 0.5 %collective-permute-start.13 = (f32[72,128]{1,0:T(8,128)S(1)}, f32[72,128]{1,0:T(8,128)S(1)}, u32[]{:S(2)}, u32[]{:S(2)}) collective-permute-start(f32[72,128]{1,0:T(8,128)S(1)} %get-tuple-element.36), channel_id=1, source_target_pairs={{0,3},{1,2},{2,1},{3,0},{4,7},{5,6},{6,5},{7,4},{8,11},{9,10},{10,... | collective-permute-start | bytes 110600 | tf_op jit(solution)/shard_map/ppermute | solution.py:374
  43.1 1.0 %collective-permute-done.12.refs_2_ = f32[72,128]{1,0:T(8,128)S(1)} collective-permute-done((f32[72,128]{1,0:T(8,128)S(1)}, f32[72,128]{1,0:T(8,128)S(1)}, u32[]{:S(2)}, u32[]{:S(2)}) %collective-permute-start.12) | collective-permute-done | bytes 36896 | tf_op jit(solution)/shard_map/ppermute | solution.py:374
  44.1 2.3 %collective-permute-done.13.refs_3_ = f32[72,128]{1,0:T(8,128)S(1)} collective-permute-done((f32[72,128]{1,0:T(8,128)S(1)}, f32[72,128]{1,0:T(8,128)S(1)}, u32[]{:S(2)}, u32[]{:S(2)}) %collective-permute-start.13) | collective-permute-done | bytes 36896 | tf_op jit(solution)/shard_map/ppermute | solution.py:374
  46.4 0.6 %finish.1 = f32[2,32,128]{2,1,0:T(8,128)} custom-call(f32[72,128]{1,0:T(8,128)S(1)} %get-tuple-element.33.refs_0_, f32[72,128]{1,0:T(8,128)S(1)} %collective-permute-done.11.refs_1_, f32[72,128]{1,0:T(8,128)S(1)} %collective-permute-done.12.refs_2_, f32[72,128]{1,0:T(8,128)S(1)} %collective-permute-done.13.refs_3_), custom_call_target="tpu_custom_call" | custom-call | tf_op jit(solution)/shard_map/finish/pallas_call | solution.py:343
  (10 shorter events, 0.0 us)
Async XLA Ops:
  0.0 26.8 %copy-start = (f32[3072,8,8]{0,2,1:T(8,128)S(1)}, f32[3072,8,8]{0,2,1:T(8,128)}, u32[]{:S(2)}) copy-start(f32[3072,8,8]{0,2,1:T(8,128)} %param.10) | copy-start | bytes 2359300
  0.0 26.8 %copy-start.1 = (s32[2]{0:T(128)S(1)}, s32[2]{0:T(128)}, u32[]{:S(2)}) copy-start(s32[2]{0:T(128)} %order_ref.9) | copy-start | bytes 28
  1.5 24.0 %collective-permute-start = (f32[2,32,3072]{2,1,0:T(8,128)S(1)}, f32[2,32,3072]{2,1,0:T(8,128)S(1)}, u32[]{:S(2)}, u32[]{:S(2)}) collective-permute-start(f32[2,32,3072]{2,1,0:T(8,128)S(1)} %get-tuple-element.24), channel_id=1, source_target_pairs={{0,1},{1,0},{2,3},{3,2},{4,5},{5,4},{6,7},{7,6},{8,9},{9,8},{10,11... | collective-permute-start | bytes 2359304 | tf_op jit(solution)/shard_map/ppermute | solution.py:374
  1.6 10.0 %collective-permute-start.4 = (f32[2,32,1152]{2,1,0:T(8,128)S(1)}, f32[2,32,1152]{2,1,0:T(8,128)S(1)}, u32[]{:S(2)}, u32[]{:S(2)}) collective-permute-start(f32[2,32,1152]{2,1,0:T(8,128)S(1)} %get-tuple-element.21), channel_id=1, source_target_pairs={{0,2},{1,3},{2,0},{3,1},{4,6},{5,7},{6,4},{7,5},{8,10},{9,11},{10,... | collective-permute-start | bytes 884744 | tf_op jit(solution)/shard_map/ppermute | solution.py:374
  4.3 13.1 %collective-permute-start.10 = (f32[2,32,1024]{2,1,0:T(8,128)S(1)}, f32[2,32,1024]{2,1,0:T(8,128)S(1)}, u32[]{:S(2)}, u32[]{:S(2)}) collective-permute-start(f32[2,32,1024]{2,1,0:T(8,128)S(1)} %get-tuple-element.32), channel_id=1, source_target_pairs={{0,3},{1,2},{2,1},{3,0},{4,7},{5,6},{6,5},{7,4},{8,11},{9,10},{10,... | collective-permute-start | bytes 786440 | tf_op jit(solution)/shard_map/ppermute | solution.py:374
  5.9 18.4 %collective-permute-start.8 = (f32[2,32,1280]{2,1,0:T(8,128)S(1)}, f32[2,32,1280]{2,1,0:T(8,128)S(1)}, u32[]{:S(2)}, u32[]{:S(2)}) collective-permute-start(f32[2,32,1280]{2,1,0:T(8,128)S(1)} %get-tuple-element.30), channel_id=1, source_target_pairs={{0,2},{1,3},{2,0},{3,1},{4,6},{5,7},{6,4},{7,5},{8,10},{9,11},{10,... | collective-permute-start | bytes 983048 | tf_op jit(solution)/shard_map/ppermute | solution.py:374
  7.6 23.9 %collective-permute-start.9 = (f32[2,32,1280]{2,1,0:T(8,128)S(1)}, f32[2,32,1280]{2,1,0:T(8,128)S(1)}, u32[]{:S(2)}, u32[]{:S(2)}) collective-permute-start(f32[2,32,1280]{2,1,0:T(8,128)S(1)} %get-tuple-element.31), channel_id=1, source_target_pairs={{0,3},{1,2},{2,1},{3,0},{4,7},{5,6},{6,5},{7,4},{8,11},{9,10},{10,... | collective-permute-start | bytes 983048 | tf_op jit(solution)/shard_map/ppermute | solution.py:374
  11.6 1.8 %collective-permute-start.3 = (f32[2,32,128]{2,1,0:T(8,128)S(1)}, f32[2,32,128]{2,1,0:T(8,128)S(1)}, u32[]{:S(2)}, u32[]{:S(2)}) collective-permute-start(f32[2,32,128]{2,1,0:T(8,128)S(1)} %get-tuple-element.27.refs_0_), channel_id=1, source_target_pairs={{0,1},{1,0},{2,3},{3,2},{4,5},{5,4},{6,7},{7,6},{8,9},{9,8},{10,11... | collective-permute-start | bytes 98312 | tf_op jit(solution)/shard_map/ppermute | solution.py:374
  13.4 5.7 %collective-permute-start.5 = (f32[2,32,128]{2,1,0:T(8,128)S(1)}, f32[2,32,128]{2,1,0:T(8,128)S(1)}, u32[]{:S(2)}, u32[]{:S(2)}) collective-permute-start(f32[2,32,128]{2,1,0:T(8,128)S(1)} %slice.4), channel_id=1, source_target_pairs={{0,1},{1,0},{2,3},{3,2},{4,5},{5,4},{6,7},{7,6},{8,9},{9,8},{10,11... | collective-permute-start | bytes 98312 | tf_op jit(solution)/shard_map/ppermute | solution.py:374
  17.5 17.9 %collective-permute-start.6 = (f32[2,32,512]{2,1,0:T(8,128)S(1)}, f32[2,32,512]{2,1,0:T(8,128)S(1)}, u32[]{:S(2)}, u32[]{:S(2)}) collective-permute-start(f32[2,32,512]{2,1,0:T(8,128)S(1)} %get-tuple-element.28), channel_id=1, source_target_pairs={{0,2},{1,3},{2,0},{3,1},{4,6},{5,7},{6,4},{7,5},{8,10},{9,11},{10,... | collective-permute-start | bytes 393224 | tf_op jit(solution)/shard_map/ppermute | solution.py:374
  19.1 18.0 %collective-permute-start.7 = (f32[2,32,512]{2,1,0:T(8,128)S(1)}, f32[2,32,512]{2,1,0:T(8,128)S(1)}, u32[]{:S(2)}, u32[]{:S(2)}) collective-permute-start(f32[2,32,512]{2,1,0:T(8,128)S(1)} %get-tuple-element.29), channel_id=1, source_target_pairs={{0,3},{1,2},{2,1},{3,0},{4,7},{5,6},{6,5},{7,4},{8,11},{9,10},{10,... | collective-permute-start | bytes 393224 | tf_op jit(solution)/shard_map/ppermute | solution.py:374
  24.3 14.8 %collective-permute-start.1 = (f32[2,32,256]{2,1,0:T(8,128)S(1)}, f32[2,32,256]{2,1,0:T(8,128)S(1)}, u32[]{:S(2)}, u32[]{:S(2)}) collective-permute-start(f32[2,32,256]{2,1,0:T(8,128)S(1)} %get-tuple-element.25), channel_id=1, source_target_pairs={{0,2},{1,3},{2,0},{3,1},{4,6},{5,7},{6,4},{7,5},{8,10},{9,11},{10,... | collective-permute-start | bytes 196616 | tf_op jit(solution)/shard_map/ppermute | solution.py:374
  25.6 14.2 %collective-permute-start.2 = (f32[2,32,256]{2,1,0:T(8,128)S(1)}, f32[2,32,256]{2,1,0:T(8,128)S(1)}, u32[]{:S(2)}, u32[]{:S(2)}) collective-permute-start(f32[2,32,256]{2,1,0:T(8,128)S(1)} %get-tuple-element.26), channel_id=1, source_target_pairs={{0,3},{1,2},{2,1},{3,0},{4,7},{5,6},{6,5},{7,4},{8,11},{9,10},{10,... | collective-permute-start | bytes 196616 | tf_op jit(solution)/shard_map/ppermute | solution.py:374
  40.8 2.2 %collective-permute-start.11 = (f32[72,128]{1,0:T(8,128)S(1)}, f32[72,128]{1,0:T(8,128)S(1)}, u32[]{:S(2)}, u32[]{:S(2)}) collective-permute-start(f32[72,128]{1,0:T(8,128)S(1)} %get-tuple-element.34), channel_id=1, source_target_pairs={{0,1},{1,0},{2,3},{3,2},{4,5},{5,4},{6,7},{7,6},{8,9},{9,8},{10,11... | collective-permute-start | bytes 110600 | tf_op jit(solution)/shard_map/ppermute | solution.py:374
  41.3 2.8 %collective-permute-start.12 = (f32[72,128]{1,0:T(8,128)S(1)}, f32[72,128]{1,0:T(8,128)S(1)}, u32[]{:S(2)}, u32[]{:S(2)}) collective-permute-start(f32[72,128]{1,0:T(8,128)S(1)} %get-tuple-element.35), channel_id=1, source_target_pairs={{0,2},{1,3},{2,0},{3,1},{4,6},{5,7},{6,4},{7,5},{8,10},{9,11},{10,... | collective-permute-start | bytes 110600 | tf_op jit(solution)/shard_map/ppermute | solution.py:374
  42.6 3.8 %collective-permute-start.13 = (f32[72,128]{1,0:T(8,128)S(1)}, f32[72,128]{1,0:T(8,128)S(1)}, u32[]{:S(2)}, u32[]{:S(2)}) collective-permute-start(f32[72,128]{1,0:T(8,128)S(1)} %get-tuple-element.36), channel_id=1, source_target_pairs={{0,3},{1,2},{2,1},{3,0},{4,7},{5,6},{6,5},{7,4},{8,11},{9,10},{10,... | collective-permute-start | bytes 110600 | tf_op jit(solution)/shard_map/ppermute | solution.py:374

commit v3 on v2

v3 whole, which is shorter than its diff:
```python
import functools

import jax
import jax.numpy as jnp
from jax import lax
from jax.experimental import pallas as pl
from jax.experimental.pallas import tpu as pltpu
from jax.sharding import PartitionSpec as P

LANES = 128
FREE = pl.CostEstimate(flops=0, bytes_accessed=0, transcendentals=0)
VMEM_LIMIT = 48 * 1024 * 1024


def partner(x, n):
    return [(i, i ^ x) for i in range(n)]


def split_degrees(blocks):
    tiles = blocks // LANES
    if tiles < 24:
        return [blocks]
    last = 2
    first = (tiles - last) * 5 // 11
    return [w * LANES for w in (first, tiles - first - last, last)]


def in_hbm(*arrays):
    return [pltpu.with_memory_space_constraint(array, pltpu.HBM) for array in arrays]


def halves(value):
    high = value.astype(jnp.bfloat16)
    low = (value - high.astype(jnp.float32)).astype(jnp.bfloat16)
    return high, low


def compiler_params(**kwargs):
    return pltpu.CompilerParams(vmem_limit_bytes=VMEM_LIMIT, **kwargs)


def cut_copies(pieces, blocks, me, legendre_ref, outs, sems):
    copies = []
    for number, (x, offset, width) in enumerate(pieces):
        start = pl.multiple_of((me ^ x) * blocks + offset, LANES)
        copies.append(
            pltpu.make_async_copy(
                legendre_ref.at[:, :, pl.ds(start, width)],
                outs[number].at[:, :, pl.ds(0, width)],
                sems.at[number],
            )
        )
    return copies


def cut_kernel(pieces, blocks, legendre_ref, *refs):
    copies = cut_copies(pieces, blocks, lax.axis_index("blk"), legendre_ref, refs[:-1], refs[-1])
    for copy in copies:
        copy.start()
    for copy in copies:
        copy.wait()


def cut(legendre, pieces, blocks):
    orders, rows, _ = legendre.shape
    shapes = [jax.ShapeDtypeStruct((orders, rows, w), jnp.float32) for _, _, w in pieces]
    size = sum(orders * rows * w * 4 for _, _, w in pieces)
    return pl.pallas_call(
        functools.partial(cut_kernel, pieces, blocks),
        out_shape=shapes,
        in_specs=[pl.BlockSpec(memory_space=pltpu.HBM)],
        out_specs=[pl.BlockSpec(memory_space=pl.ANY)] * len(pieces),
        scratch_shapes=[pltpu.SemaphoreType.DMA((len(pieces),))],
        compiler_params=compiler_params(),
        cost_estimate=pl.CostEstimate(flops=0, bytes_accessed=40 * size, transcendentals=0),
        name="cut",
    )(*in_hbm(legendre))


def open_kernel(
    pieces, carry, blocks, legendre_ref, cycles_ref, weight_ref, hits_ref, flux_ref, *refs
):
    count = len(pieces)
    me = lax.axis_index("blk")
    outs, own_ref = refs[:count], refs[count]
    cycles, weight, hit_cycles, flux, sems, small_sems = refs[count + 1 :]
    orders, rows, columns = cycles.shape
    clusters = flux.shape[1]
    small = [
        pltpu.make_async_copy(source, target, small_sems.at[number])
        for number, (source, target) in enumerate(
            [(cycles_ref, cycles), (weight_ref, weight), (hits_ref, hit_cycles), (flux_ref, flux)]
        )
    ]
    copies = cut_copies(pieces, blocks, me, legendre_ref, outs, sems)
    for copy in small + copies:
        copy.start()
    small[1].wait()
    eye = lax.broadcasted_iota(jnp.int32, (rows, rows), 0) == lax.broadcasted_iota(
        jnp.int32, (rows, rows), 1
    )
    weight_column = jnp.sum(jnp.where(eye, weight[...], 0.0), axis=1, keepdims=True)
    ids = me * rows + lax.broadcasted_iota(jnp.int32, (rows, clusters), 0)
    for copy in small[:1] + small[2:]:
        copy.wait()
    for k in range(orders):
        hits = (ids == hit_cycles[k : k + 1, :]).astype(jnp.bfloat16)
        terms = []
        left = flux[k]
        for _ in range(3):
            terms.append(left.astype(jnp.bfloat16))
            left = left - terms[-1].astype(jnp.float32)
        sums = jnp.dot(
            hits, jnp.concatenate(terms, axis=1), preferred_element_type=jnp.float32
        )
        added = (sums[:, 2 * columns :] + sums[:, columns : 2 * columns]) + sums[:, :columns]
        value = weight_column * (cycles[k] + added)
        own_ref[k] = value
        for i in carry:
            outs[i][k, :, pl.ds(pieces[i][2], columns)] = value
    for copy in copies:
        copy.wait()


def open_blocks(legendre, cycles, weight, cluster_cycles, flux, pieces, carry, blocks):
    orders, rows, columns = cycles.shape
    shapes = [jax.ShapeDtypeStruct((orders, rows, w), jnp.float32) for _, _, w in pieces]
    for i in carry:
        shapes[i] = jax.ShapeDtypeStruct((orders, rows, pieces[i][2] + columns), jnp.float32)
    shapes.append(jax.ShapeDtypeStruct(cycles.shape, jnp.float32))
    size = sum(orders * rows * w * 4 for _, _, w in pieces)
    hbm = pl.BlockSpec(memory_space=pltpu.HBM)
    weight = weight.reshape(1, -1)
    return pl.pallas_call(
        functools.partial(open_kernel, pieces, carry, blocks),
        out_shape=shapes,
        in_specs=[hbm] * 5,
        out_specs=[
            pl.BlockSpec(memory_space=pltpu.VMEM if i in carry else pl.ANY)
            for i in range(len(pieces))
        ]
        + [pl.BlockSpec(memory_space=pltpu.VMEM)],
        scratch_shapes=[
            pltpu.VMEM(cycles.shape, jnp.float32),
            pltpu.VMEM(weight.shape, jnp.float32),
            pltpu.VMEM(cluster_cycles.shape, jnp.int32),
            pltpu.VMEM(flux.shape, jnp.float32),
            pltpu.SemaphoreType.DMA((len(pieces),)),
            pltpu.SemaphoreType.DMA((4,)),
        ],
        compiler_params=compiler_params(),
        cost_estimate=FREE,
        name="open",
    )(*in_hbm(legendre, cycles, weight, cluster_cycles, flux))


def response_kernel(blocks, scales, skies, order_ref, weights_ref, out_ref, limit_ref):
    orders = order_ref.shape[0]
    begin = lax.axis_index("blk") * blocks
    degree = begin + lax.broadcasted_iota(jnp.int32, (1, blocks), 1)
    factor = 2.0 * degree.astype(jnp.float32) + 1.0
    squares = jnp.concatenate(
        [
            jnp.sum(weights_ref[s] * weights_ref[s], axis=0, keepdims=True) * factor
            for s in range(scales)
        ],
        axis=0,
    )
    columns = out_ref.shape[1]
    scale_of = (lax.broadcasted_iota(jnp.int32, (scales, columns), 1) // skies) % scales
    chosen = scale_of == lax.broadcasted_iota(jnp.int32, (scales, columns), 0)
    out_ref[...] = jnp.zeros_like(out_ref)
    limit_ref[...] = jnp.zeros_like(limit_ref)
    for k in range(orders):
        total = jnp.sum(jnp.where(degree >= order_ref[k], squares, 0.0), axis=1, keepdims=True)
        out_ref[k : k + 1, :] = jnp.sum(jnp.where(chosen, total, 0.0), axis=0, keepdims=True)
        limit_ref[k : k + 1, :] = jnp.full((1, LANES), order_ref[k] - begin, jnp.int32)


def response_rows(order_per_slot, weights, skies, columns):
    scales, _, blocks = weights.shape
    smem = pl.BlockSpec(memory_space=pltpu.SMEM)
    vmem = pl.BlockSpec(memory_space=pltpu.VMEM)
    rows = -(-order_per_slot.shape[0] // 8) * 8
    return pl.pallas_call(
        functools.partial(response_kernel, blocks, scales, skies),
        out_shape=[
            jax.ShapeDtypeStruct((rows, columns), jnp.float32),
            jax.ShapeDtypeStruct((rows, LANES), jnp.int32),
        ],
        in_specs=[smem, vmem],
        out_specs=[vmem, vmem],
        compiler_params=compiler_params(),
        cost_estimate=FREE,
        name="response",
    )(order_per_slot, weights)


def prepare_kernel(*refs):
    pieces, out_ref = refs[:-1], refs[-1]
    for k in range(out_ref.shape[0]):
        whole = jnp.concatenate([piece[k] for piece in pieces], axis=0).T
        high, low = halves(whole)
        out_ref[k] = jnp.concatenate([high, low, high], axis=1)


def prepare(pieces):
    orders, rows, columns = pieces[0][0].shape
    count = len(pieces)
    return pl.pallas_call(
        prepare_kernel,
        out_shape=jax.ShapeDtypeStruct((orders, columns, 3 * rows * count), jnp.bfloat16),
        grid=(1,),
        in_specs=[
            pl.BlockSpec((orders, rows, columns), lambda i, block=at // columns: (0, 0, block))
            for _, at in pieces
        ],
        out_specs=pl.BlockSpec((orders, columns, 3 * rows * count), lambda i: (0, 0, 0)),
        compiler_params=compiler_params(),
        cost_estimate=FREE,
        name="prepare",
    )(*[array for array, _ in pieces])


def chunk_kernel(n, first, last, blocks, offset, starts, tiles, limits_ref, *refs):
    legendre = refs[:n]
    analysis_ref, weights_ref = refs[n : n + 2]
    rest = list(refs[n + 2 :])
    before = None if first else rest.pop(0)
    response = rest.pop(0) if last else None
    orders, rows, _ = legendre[0].shape
    scales, channels, _ = weights_ref.shape
    columns = analysis_ref.shape[1]
    skies = columns // (2 * channels)
    everything = n * rows
    totals = [None] * orders

    def begin_of(start):
        if start is None:
            return pl.multiple_of(lax.axis_index("blk") * blocks + offset, LANES)
        return start

    at = 0
    for tile in tiles:
        degree = offset + at + lax.broadcasted_iota(jnp.int32, (1, tile), 1)
        weights = [
            [weights_ref[s, f : f + 1, offset + at : offset + at + tile] for f in range(channels)]
            for s in range(scales)
        ]
        for k in range(orders):
            values = jnp.concatenate(
                [
                    block[k, :, pl.ds(begin_of(start) + at, tile)]
                    for block, start in zip(legendre, starts)
                ],
                axis=0,
            )
            high, low = halves(values)
            harmonics = jnp.dot(
                analysis_ref[k],
                jnp.concatenate([high, high, low], axis=0),
                preferred_element_type=jnp.float32,
            )
            harmonics = jnp.where(degree >= limits_ref[k : k + 1, :1], harmonics, 0.0)
            matched = []
            for p in range(2):
                for s in range(scales):
                    value = None
                    for f in range(channels):
                        begin = (p * channels + f) * skies
                        term = weights[s][f] * harmonics[begin : begin + skies, :]
                        value = term if value is None else value + term
                    matched.append(value)
            matched_high, matched_low = halves(jnp.concatenate(matched, axis=0))
            product = lax.dot_general(
                jnp.concatenate([high, low], axis=0),
                jnp.concatenate([matched_high, matched_low], axis=0),
                (((1,), (1,)), ((), ())),
                preferred_element_type=jnp.float32,
            )
            totals[k] = product if totals[k] is None else totals[k] + product
        at += tile

    for k in range(orders):
        total = totals[k]
        result = (
            (total[everything:, columns:] + total[everything:, :columns])
            + total[:everything, columns:]
        ) + total[:everything, :columns]
        if before is not None:
            result = result + before[k]
        if last:
            for x in range(n):
                rest[x][k * rows : (k + 1) * rows, :] = result[x * rows : (x + 1) * rows, :]
        else:
            rest[0][k] = result
    if last:
        for x in range(n):
            rest[x][orders * rows :, :] = response[...]


def chunk(limits, parts, analysis, weights, before, response, blocks, offset, width):
    n = len(parts)
    orders, rows, _ = parts[0][0].shape
    columns = analysis.shape[1]
    last = response is not None
    first = before is None
    tiles = [2 * LANES] * (width // (2 * LANES)) + [LANES] * (width // LANES % 2)
    operands = [array for array, _ in parts] + [analysis, weights]
    if not first:
        operands.append(before)
    if last:
        operands.append(response)
        out_shape = [
            jax.ShapeDtypeStruct((orders * rows + response.shape[0], columns), jnp.float32)
        ] * n
    else:
        out_shape = [jax.ShapeDtypeStruct((orders, n * rows, columns), jnp.float32)]
    vmem = pl.BlockSpec(memory_space=pltpu.VMEM)
    return pl.pallas_call(
        functools.partial(
            chunk_kernel,
            n,
            first,
            last,
            blocks,
            offset,
            [start for _, start in parts],
            tiles,
        ),
        out_shape=out_shape,
        in_specs=[vmem] * (len(operands) + 1),
        out_specs=[vmem] * len(out_shape),
        compiler_params=compiler_params(),
        cost_estimate=FREE,
        name="chunk",
    )(limits, *operands)


def finish_kernel(degrees, *refs):
    parts, out_ref = refs[:-1], refs[-1]
    orders, rows, _ = out_ref.shape
    total = parts[0][...]
    for part in parts[1:]:
        total = total + part[...]
    for k in range(orders):
        at = orders * rows + k
        out_ref[k] = total[k * rows : (k + 1) * rows, :] * (
            degrees / jnp.sqrt(total[at : at + 1, :])
        )


def finish(parts, shape, degrees):
    vmem = pl.BlockSpec(memory_space=pltpu.VMEM)
    return pl.pallas_call(
        functools.partial(finish_kernel, degrees),
        out_shape=jax.ShapeDtypeStruct(shape, jnp.float32),
        in_specs=[vmem] * len(parts),
        out_specs=vmem,
        compiler_params=compiler_params(),
        cost_estimate=FREE,
        name="finish",
    )(*parts)


def body(
    fourier_cycles,
    legendre,
    cycle_weight,
    matched_filter_weights,
    cluster_cycles,
    cluster_flux,
    order_per_slot,
):
    n = lax.axis_size("blk")
    blocks = legendre.shape[2] // n
    columns = fourier_cycles.shape[2]
    channels = matched_filter_weights.shape[2]
    skies = columns // (2 * channels)
    weights = jnp.transpose(matched_filter_weights, (1, 2, 0))
    widths = split_degrees(blocks)
    offsets = [sum(widths[:c]) for c in range(len(widths))]

    def send(value, x):
        return lax.ppermute(value, "blk", partner(x, n))

    far = range(2, n)
    first = widths[0]
    top = n - 1
    order = [top] + [x for x in far if x != top]
    *cuts, own = open_blocks(
        legendre,
        fourier_cycles,
        cycle_weight,
        cluster_cycles,
        cluster_flux,
        [(x, 0, first) for x in order],
        [0],
        blocks,
    )
    sent = [{x: (send(value, x), 0) for value, x in zip(cuts, order)}]
    then, _ = lax.optimization_barrier((legendre, cuts[0]))
    pieces = [(x, at, w) for at, w in zip(offsets[1:], widths[1:]) for x in order]
    *cuts, home = cut(then, pieces + [(0, 0, blocks)], blocks)
    for c in range(1, len(widths)):
        here = cuts[(c - 1) * len(order) : c * len(order)]
        sent.append({x: (send(value, x), 0) for value, x in zip(here, order)})
    near = send(legendre, 1)
    for c, offset in enumerate(offsets):
        sent[c][0] = (home, offset)
        sent[c][1] = (near, None)

    cycles = {0: (own, 0), top: (sent[0][top][0], first)}
    bit = n // 4
    while bit:
        for x in list(cycles):
            value, at = cycles[x]
            cycles[x ^ bit] = (send(value[:, :, at : at + columns], bit), 0)
        bit //= 2
    analysis = prepare([cycles[x] for x in range(n)])
    response, limits = response_rows(order_per_slot, weights, skies, columns)

    total = None
    for c, (offset, width) in enumerate(zip(offsets, widths)):
        final = c == len(widths) - 1
        result = chunk(
            limits,
            [sent[c][x] for x in range(n)],
            analysis,
            weights,
            total,
            response if final else None,
            blocks,
            offset,
            width,
        )
        total = result[0]
    returned = [result[0]] + [send(result[x], x) for x in list(far) + [1]]
    return finish(returned, fourier_cycles.shape, float(legendre.shape[2]))


def solution(mesh):
    return jax.shard_map(
        body,
        mesh=mesh,
        in_specs=(
            P("order", "blk", None),
            P("order", "blk", None),
            P("blk"),
            P("blk", None, None),
            P("order", None),
            P("order", None, None),
            P("order"),
        ),
        out_specs=P("order", "blk", None),
        check_vma=False,
    )
```

time: 47.5 us -> 46 us (0.968)
  waiting for transfers between devices: 19.7 us -> 26 us
  Pallas kernels: 14.5 us -> 9.58 us
  starting transfers between devices: 12.8 us -> 10.2 us
    ppermute x14 -> x12, waiting for transfers between devices: 19.7 us -> 26 us  [send(): return lax.ppermute(value, 'blk', partner(x, n))]
    pallas_call x4 -> x3, Pallas kernels: 9.8 us -> 5.17 us  [chunk(): pl.pallas_call(functools.partial(chunk_kernel, n, first, last, blocks, of...]
    ppermute x14 -> x12, starting transfers between devices: 12.8 us -> 10.2 us  [send(): return lax.ppermute(value, 'blk', partner(x, n))]
  transfers between devices with their start and end apart: 14 -> 12, of which waited for: 9 -> 8; matrix products, arithmetic and copies ran while one was open for 0% -> 0% of each run, Pallas kernels for 24% -> 18%
where the time goes in v3:
time: 46 us; the launch traced here: 45.9 us
  waiting for transfers between devices  26 us (57%)
  starting transfers between devices  10.2 us (22%)
  Pallas kernels  9.58 us (21%)
    ppermute x12, waiting for transfers between devices, send(): return lax.ppermute(value, 'blk', partner(x, n))  26 us
    ppermute x12, starting transfers between devices, send(): return lax.ppermute(value, 'blk', partner(x, n))  10.2 us
    pallas_call x3, Pallas kernels, chunk(): pl.pallas_call(functools.partial(chunk_kernel, n, first, last, blocks, of...  5.17 us
    pallas_call x1, Pallas kernels, cut(): pl.pallas_call(functools.partial(cut_kernel, pieces, blocks), out_shape=s...  1.46 us
    pallas_call x1, Pallas kernels, open_blocks(): pl.pallas_call(functools.partial(open_kernel, pieces, carry, blocks), out...  1.28 us
    pallas_call x1, Pallas kernels, response_rows(): pl.pallas_call(functools.partial(response_kernel, blocks, scales, skies),...  0.93 us
  transfers between devices with their start and end apart: 12, of which 8 were waited for; matrix products, arithmetic and copies ran while one was open for 0% of the time, Pallas kernels for 18%

profile of v3, /device:TPU:1, one launch (start us, length us, event | category | flops | bytes accessed | tf_op | source)
XLA Modules:
  0.0 45.9 jit_solution(15620606956089679779)
XLA Ops:
  0.0 0.1 collective-permute-start
  0.1 1.3 %open.1 = (f32[2,32,1408]{2,1,0:T(8,128)S(1)}, f32[2,32,1280]{2,1,0:T(8,128)S(1)}, f32[2,32,128]{2,1,0:T(8,128)S(1)}) custom-call(f32[2,32,12288]{2,1,0:T(8,128)} %legendre_ref.2, f32[2,32,128]{2,1,0:T(8,128)} %cycles_ref.1, f32[1,32]{1,0:T(1,128)} %bitcast.6, s32[2,64]{1,0:T(2,128)} %hits_ref.1, f32[2,64,128]{2,1,0:T(8,128)} %flux_ref.1), custom_call_target="tpu_custom_call" | custom-call | tf_op jit(solution)/shard_map/open/pallas_call | solution.py:134
  1.3 2.6 %collective-permute-start.4 = (f32[2,32,1408]{2,1,0:T(8,128)S(1)}, f32[2,32,1408]{2,1,0:T(8,128)S(1)}, u32[]{:S(2)}, u32[]{:S(2)}) collective-permute-start(f32[2,32,1408]{2,1,0:T(8,128)S(1)} %get-tuple-element.21), channel_id=1, source_target_pairs={{0,3},{1,2},{2,1},{3,0},{4,7},{5,6},{6,5},{7,4},{8,11},{9,10},{10,... | collective-permute-start | bytes 1081352 | tf_op jit(solution)/shard_map/ppermute | solution.py:385
  4.0 0.2 collective-permute-start.8
  4.2 1.5 %cut.1 = (f32[2,32,1536]{2,1,0:T(8,128)S(1)}, f32[2,32,1536]{2,1,0:T(8,128)S(1)}, f32[2,32,256]{2,1,0:T(8,128)S(1)}, f32[2,32,256]{2,1,0:T(8,128)S(1)}, f32[2,32,3072]{2,1,0:T(8,128)S(1)}) custom-call(f32[2,32,12288]{2,1,0:T(8,128)} %legendre_ref.2), custom_call_target="tpu_custom_call" | custom-call | bytes 68157440 | tf_op jit(solution)/shard_map/cut/pallas_call | solution.py:68
  5.6 1.3 %collective-permute-start.6 = (f32[2,32,1536]{2,1,0:T(8,128)S(1)}, f32[2,32,1536]{2,1,0:T(8,128)S(1)}, u32[]{:S(2)}, u32[]{:S(2)}) collective-permute-start(f32[2,32,1536]{2,1,0:T(8,128)S(1)} %get-tuple-element.27), channel_id=1, source_target_pairs={{0,2},{1,3},{2,0},{3,1},{4,6},{5,7},{6,4},{7,5},{8,10},{9,11},{10,... | collective-permute-start | bytes 1179656 | tf_op jit(solution)/shard_map/ppermute | solution.py:385
  7.0 0.8 %collective-permute-start.7 = (f32[2,32,1536]{2,1,0:T(8,128)S(1)}, f32[2,32,1536]{2,1,0:T(8,128)S(1)}, u32[]{:S(2)}, u32[]{:S(2)}) collective-permute-start(f32[2,32,1536]{2,1,0:T(8,128)S(1)} %get-tuple-element.28), channel_id=1, source_target_pairs={{0,3},{1,2},{2,1},{3,0},{4,7},{5,6},{6,5},{7,4},{8,11},{9,10},{10,... | collective-permute-start | bytes 1179656 | tf_op jit(solution)/shard_map/ppermute | solution.py:385
  7.8 5.2 %collective-permute-done.4.refs_3_ = f32[2,32,1408]{2,1,0:T(8,128)S(1)} collective-permute-done((f32[2,32,1408]{2,1,0:T(8,128)S(1)}, f32[2,32,1408]{2,1,0:T(8,128)S(1)}, u32[]{:S(2)}, u32[]{:S(2)}) %collective-permute-start.4) | collective-permute-done | bytes 360480 | tf_op jit(solution)/shard_map/ppermute | solution.py:385
  13.0 0.3 collective-permute-start.3
  13.3 0.9 %collective-permute-done.3.refs_1_ = f32[2,32,128]{2,1,0:T(8,128)S(1)} collective-permute-done((f32[2,32,128]{2,1,0:T(8,128)S(1)}, f32[2,32,128]{2,1,0:T(8,128)S(1)}, u32[]{:S(2)}, u32[]{:S(2)}) %collective-permute-start.3) | collective-permute-done | bytes 32800 | tf_op jit(solution)/shard_map/ppermute | solution.py:385
  14.2 0.3 collective-permute-start.5
  14.5 5.4 %collective-permute-done.8.refs_2_ = f32[2,32,1280]{2,1,0:T(8,128)S(1)} collective-permute-done((f32[2,32,1280]{2,1,0:T(8,128)S(1)}, f32[2,32,1280]{2,1,0:T(8,128)S(1)}, u32[]{:S(2)}, u32[]{:S(2)}) %collective-permute-start.8) | collective-permute-done | bytes 327712 | tf_op jit(solution)/shard_map/ppermute | solution.py:385
  19.9 0.9 %collective-permute-start.1 = (f32[2,32,256]{2,1,0:T(8,128)S(1)}, f32[2,32,256]{2,1,0:T(8,128)S(1)}, u32[]{:S(2)}, u32[]{:S(2)}) collective-permute-start(f32[2,32,256]{2,1,0:T(8,128)S(1)} %get-tuple-element.24), channel_id=1, source_target_pairs={{0,2},{1,3},{2,0},{3,1},{4,6},{5,7},{6,4},{7,5},{8,10},{9,11},{10,... | collective-permute-start | bytes 196616 | tf_op jit(solution)/shard_map/ppermute | solution.py:385
  20.8 0.0 collective-permute-done.5.refs_2_
  20.8 1.6 %collective-permute-start.2 = (f32[2,32,256]{2,1,0:T(8,128)S(1)}, f32[2,32,256]{2,1,0:T(8,128)S(1)}, u32[]{:S(2)}, u32[]{:S(2)}) collective-permute-start(f32[2,32,256]{2,1,0:T(8,128)S(1)} %get-tuple-element.25), channel_id=1, source_target_pairs={{0,3},{1,2},{2,1},{3,0},{4,7},{5,6},{6,5},{7,4},{8,11},{9,10},{10,... | collective-permute-start | bytes 196616 | tf_op jit(solution)/shard_map/ppermute | solution.py:385
  22.4 0.9 %response.1 = (f32[8,128]{1,0:T(8,128)S(1)}, s32[8,128]{1,0:T(8,128)S(1)}) custom-call(s32[2]{0:T(128)S(1)} %copy-done.1, f32[8,8,3072]{2,1,0:T(8,128)S(1)} %bitcast.2), custom_call_target="tpu_custom_call" | custom-call | tf_op jit(solution)/shard_map/response/pallas_call | solution.py:185
  23.3 0.1 prepare.1.refs_4_
  23.5 0.0 collective-permute-done.refs_1_
  23.5 2.1 %chunk.3.refs_6_ = f32[2,128,128]{2,1,0:T(8,128)S(1)} custom-call(s32[8,128]{1,0:T(8,128)S(1)} %get-tuple-element.20.limits_ref, f32[2,32,3072]{2,1,0:T(8,128)S(1)} %get-tuple-element.23.refs_0_, f32[2,32,12288]{2,1,0:T(8,128)S(1)} %collective-permute-done.refs_1_, f32[2,32,1280]{2,1,0:T(8,128)S(1)} %collective-permute-done.8.refs_2_, ...), custom_call_target="tpu_custom_call" | custom-call | tf_op jit(solution)/shard_map/chunk/pallas_call | solution.py:320
  25.6 2.8 %collective-permute-done.6.refs_2_ = f32[2,32,1536]{2,1,0:T(8,128)S(1)} collective-permute-done((f32[2,32,1536]{2,1,0:T(8,128)S(1)}, f32[2,32,1536]{2,1,0:T(8,128)S(1)}, u32[]{:S(2)}, u32[]{:S(2)}) %collective-permute-start.6) | collective-permute-done | bytes 393248 | tf_op jit(solution)/shard_map/ppermute | solution.py:385
  28.3 8.5 %collective-permute-done.7.refs_3_ = f32[2,32,1536]{2,1,0:T(8,128)S(1)} collective-permute-done((f32[2,32,1536]{2,1,0:T(8,128)S(1)}, f32[2,32,1536]{2,1,0:T(8,128)S(1)}, u32[]{:S(2)}, u32[]{:S(2)}) %collective-permute-start.7) | collective-permute-done | bytes 393248 | tf_op jit(solution)/shard_map/ppermute | solution.py:385
  36.8 2.5 %chunk.4.refs_6_ = f32[2,128,128]{2,1,0:T(8,128)S(1)} custom-call(s32[8,128]{1,0:T(8,128)S(1)} %get-tuple-element.20.limits_ref, f32[2,32,3072]{2,1,0:T(8,128)S(1)} %get-tuple-element.23.refs_0_, f32[2,32,12288]{2,1,0:T(8,128)S(1)} %collective-permute-done.refs_1_, f32[2,32,1536]{2,1,0:T(8,128)S(1)} %collective-permute-done.6.refs_2_, ...), custom_call_target="tpu_custom_call" | custom-call | tf_op jit(solution)/shard_map/chunk/pallas_call | solution.py:320
  39.3 0.0 collective-permute-done.1.refs_2_
  39.3 0.2 collective-permute-done.2.refs_3_
  39.6 0.6 %chunk.5 = (f32[72,128]{1,0:T(8,128)S(1)}, f32[72,128]{1,0:T(8,128)S(1)}, f32[72,128]{1,0:T(8,128)S(1)}, f32[72,128]{1,0:T(8,128)S(1)}) custom-call(s32[8,128]{1,0:T(8,128)S(1)} %get-tuple-element.20.limits_ref, f32[2,32,3072]{2,1,0:T(8,128)S(1)} %get-tuple-element.23.refs_0_, f32[2,32,12288]{2,1,0:T(8,128)S(1)} %collective-permute-done.refs_1_, ...), custom_call_target="tpu_custom_call" | custom-call | tf_op jit(solution)/shard_map/chunk/pallas_call | solution.py:320
  40.2 1.6 %collective-permute-start.9 = (f32[72,128]{1,0:T(8,128)S(1)}, f32[72,128]{1,0:T(8,128)S(1)}, u32[]{:S(2)}, u32[]{:S(2)}) collective-permute-start(f32[72,128]{1,0:T(8,128)S(1)} %get-tuple-element.32), channel_id=1, source_target_pairs={{0,2},{1,3},{2,0},{3,1},{4,6},{5,7},{6,4},{7,5},{8,10},{9,11},{10,... | collective-permute-start | bytes 110600 | tf_op jit(solution)/shard_map/ppermute | solution.py:385
  41.8 0.4 collective-permute-start.10
  42.3 0.0 collective-permute-start.11
  42.3 0.9 %collective-permute-done.9.refs_1_ = f32[72,128]{1,0:T(8,128)S(1)} collective-permute-done((f32[72,128]{1,0:T(8,128)S(1)}, f32[72,128]{1,0:T(8,128)S(1)}, u32[]{:S(2)}, u32[]{:S(2)}) %collective-permute-start.9) | collective-permute-done | bytes 36896 | tf_op jit(solution)/shard_map/ppermute | solution.py:385
  43.2 2.0 %collective-permute-done.10.refs_2_ = f32[72,128]{1,0:T(8,128)S(1)} collective-permute-done((f32[72,128]{1,0:T(8,128)S(1)}, f32[72,128]{1,0:T(8,128)S(1)}, u32[]{:S(2)}, u32[]{:S(2)}) %collective-permute-start.10) | collective-permute-done | bytes 36896 | tf_op jit(solution)/shard_map/ppermute | solution.py:385
  45.2 0.0 collective-permute-done.11.refs_3_
  45.2 0.6 %finish.1 = f32[2,32,128]{2,1,0:T(8,128)} custom-call(f32[72,128]{1,0:T(8,128)S(1)} %get-tuple-element.31.refs_0_, f32[72,128]{1,0:T(8,128)S(1)} %collective-permute-done.9.refs_1_, f32[72,128]{1,0:T(8,128)S(1)} %collective-permute-done.10.refs_2_, f32[72,128]{1,0:T(8,128)S(1)} %collective-permute-done.11.refs_3_), custom_call_target="tpu_custom_call" | custom-call | tf_op jit(solution)/shard_map/finish/pallas_call | solution.py:355
  (5 shorter events, 0.0 us)
Async XLA Ops:
  0.0 23.5 %collective-permute-start = (f32[2,32,12288]{2,1,0:T(8,128)}, f32[2,32,12288]{2,1,0:T(8,128)S(1)}, u32[]{:S(2)}, u32[]{:S(2)}) collective-permute-start(f32[2,32,12288]{2,1,0:T(8,128)} %legendre_ref.2), channel_id=1, source_target_pairs={{0,1},{1,0},{2,3},{3,2},{4,5},{5,4},{6,7},{7,6},{8,9},{9,8},{10,11... | collective-permute-start | bytes 9437192 | tf_op jit(solution)/shard_map/ppermute | solution.py:385
  0.1 22.4 %copy-start = (f32[3072,8,8]{0,2,1:T(8,128)S(1)}, f32[3072,8,8]{0,2,1:T(8,128)}, u32[]{:S(2)}) copy-start(f32[3072,8,8]{0,2,1:T(8,128)} %param.10) | copy-start | bytes 2359300
  0.1 22.4 %copy-start.1 = (s32[2]{0:T(128)S(1)}, s32[2]{0:T(128)}, u32[]{:S(2)}) copy-start(s32[2]{0:T(128)} %order_ref.1) | copy-start | bytes 28
  1.3 11.6 %collective-permute-start.4 = (f32[2,32,1408]{2,1,0:T(8,128)S(1)}, f32[2,32,1408]{2,1,0:T(8,128)S(1)}, u32[]{:S(2)}, u32[]{:S(2)}) collective-permute-start(f32[2,32,1408]{2,1,0:T(8,128)S(1)} %get-tuple-element.21), channel_id=1, source_target_pairs={{0,3},{1,2},{2,1},{3,0},{4,7},{5,6},{6,5},{7,4},{8,11},{9,10},{10,... | collective-permute-start | bytes 1081352 | tf_op jit(solution)/shard_map/ppermute | solution.py:385
  4.0 15.9 %collective-permute-start.8 = (f32[2,32,1280]{2,1,0:T(8,128)S(1)}, f32[2,32,1280]{2,1,0:T(8,128)S(1)}, u32[]{:S(2)}, u32[]{:S(2)}) collective-permute-start(f32[2,32,1280]{2,1,0:T(8,128)S(1)} %get-tuple-element.29), channel_id=1, source_target_pairs={{0,2},{1,3},{2,0},{3,1},{4,6},{5,7},{6,4},{7,5},{8,10},{9,11},{10,... | collective-permute-start | bytes 983048 | tf_op jit(solution)/shard_map/ppermute | solution.py:385
  5.6 22.7 %collective-permute-start.6 = (f32[2,32,1536]{2,1,0:T(8,128)S(1)}, f32[2,32,1536]{2,1,0:T(8,128)S(1)}, u32[]{:S(2)}, u32[]{:S(2)}) collective-permute-start(f32[2,32,1536]{2,1,0:T(8,128)S(1)} %get-tuple-element.27), channel_id=1, source_target_pairs={{0,2},{1,3},{2,0},{3,1},{4,6},{5,7},{6,4},{7,5},{8,10},{9,11},{10,... | collective-permute-start | bytes 1179656 | tf_op jit(solution)/shard_map/ppermute | solution.py:385
  7.0 29.8 %collective-permute-start.7 = (f32[2,32,1536]{2,1,0:T(8,128)S(1)}, f32[2,32,1536]{2,1,0:T(8,128)S(1)}, u32[]{:S(2)}, u32[]{:S(2)}) collective-permute-start(f32[2,32,1536]{2,1,0:T(8,128)S(1)} %get-tuple-element.28), channel_id=1, source_target_pairs={{0,3},{1,2},{2,1},{3,0},{4,7},{5,6},{6,5},{7,4},{8,11},{9,10},{10,... | collective-permute-start | bytes 1179656 | tf_op jit(solution)/shard_map/ppermute | solution.py:385
  13.0 1.2 %collective-permute-start.3 = (f32[2,32,128]{2,1,0:T(8,128)S(1)}, f32[2,32,128]{2,1,0:T(8,128)S(1)}, u32[]{:S(2)}, u32[]{:S(2)}) collective-permute-start(f32[2,32,128]{2,1,0:T(8,128)S(1)} %get-tuple-element.26.refs_0_), channel_id=1, source_target_pairs={{0,1},{1,0},{2,3},{3,2},{4,5},{5,4},{6,7},{7,6},{8,9},{9,8},{10,11... | collective-permute-start | bytes 98312 | tf_op jit(solution)/shard_map/ppermute | solution.py:385
  14.2 6.6 %collective-permute-start.5 = (f32[2,32,128]{2,1,0:T(8,128)S(1)}, f32[2,32,128]{2,1,0:T(8,128)S(1)}, u32[]{:S(2)}, u32[]{:S(2)}) collective-permute-start(f32[2,32,128]{2,1,0:T(8,128)S(1)} %slice.4), channel_id=1, source_target_pairs={{0,1},{1,0},{2,3},{3,2},{4,5},{5,4},{6,7},{7,6},{8,9},{9,8},{10,11... | collective-permute-start | bytes 98312 | tf_op jit(solution)/shard_map/ppermute | solution.py:385
  19.9 19.4 %collective-permute-start.1 = (f32[2,32,256]{2,1,0:T(8,128)S(1)}, f32[2,32,256]{2,1,0:T(8,128)S(1)}, u32[]{:S(2)}, u32[]{:S(2)}) collective-permute-start(f32[2,32,256]{2,1,0:T(8,128)S(1)} %get-tuple-element.24), channel_id=1, source_target_pairs={{0,2},{1,3},{2,0},{3,1},{4,6},{5,7},{6,4},{7,5},{8,10},{9,11},{10,... | collective-permute-start | bytes 196616 | tf_op jit(solution)/shard_map/ppermute | solution.py:385
  20.8 18.8 %collective-permute-start.2 = (f32[2,32,256]{2,1,0:T(8,128)S(1)}, f32[2,32,256]{2,1,0:T(8,128)S(1)}, u32[]{:S(2)}, u32[]{:S(2)}) collective-permute-start(f32[2,32,256]{2,1,0:T(8,128)S(1)} %get-tuple-element.25), channel_id=1, source_target_pairs={{0,3},{1,2},{2,1},{3,0},{4,7},{5,6},{6,5},{7,4},{8,11},{9,10},{10,... | collective-permute-start | bytes 196616 | tf_op jit(solution)/shard_map/ppermute | solution.py:385
  40.2 3.0 %collective-permute-start.9 = (f32[72,128]{1,0:T(8,128)S(1)}, f32[72,128]{1,0:T(8,128)S(1)}, u32[]{:S(2)}, u32[]{:S(2)}) collective-permute-start(f32[72,128]{1,0:T(8,128)S(1)} %get-tuple-element.32), channel_id=1, source_target_pairs={{0,2},{1,3},{2,0},{3,1},{4,6},{5,7},{6,4},{7,5},{8,10},{9,11},{10,... | collective-permute-start | bytes 110600 | tf_op jit(solution)/shard_map/ppermute | solution.py:385
  41.8 3.4 %collective-permute-start.10 = (f32[72,128]{1,0:T(8,128)S(1)}, f32[72,128]{1,0:T(8,128)S(1)}, u32[]{:S(2)}, u32[]{:S(2)}) collective-permute-start(f32[72,128]{1,0:T(8,128)S(1)} %get-tuple-element.33), channel_id=1, source_target_pairs={{0,3},{1,2},{2,1},{3,0},{4,7},{5,6},{6,5},{7,4},{8,11},{9,10},{10,... | collective-permute-start | bytes 110600 | tf_op jit(solution)/shard_map/ppermute | solution.py:385
  42.3 2.9 %collective-permute-start.11 = (f32[72,128]{1,0:T(8,128)S(1)}, f32[72,128]{1,0:T(8,128)S(1)}, u32[]{:S(2)}, u32[]{:S(2)}) collective-permute-start(f32[72,128]{1,0:T(8,128)S(1)} %get-tuple-element.34), channel_id=1, source_target_pairs={{0,1},{1,0},{2,3},{3,2},{4,5},{5,4},{6,7},{7,6},{8,9},{9,8},{10,11... | collective-permute-start | bytes 110600 | tf_op jit(solution)/shard_map/ppermute | solution.py:385

commit v4 on v3

--- a/solution.py
+++ b/solution.py
@@ -9,20 +9,17 @@
 
 LANES = 128
 FREE = pl.CostEstimate(flops=0, bytes_accessed=0, transcendentals=0)
-VMEM_LIMIT = 48 * 1024 * 1024
+VMEM_LIMIT = 32 * 1024 * 1024
 
 
 def partner(x, n):
     return [(i, i ^ x) for i in range(n)]
 
 
-def split_degrees(blocks):
-    tiles = blocks // LANES
-    if tiles < 24:
-        return [blocks]
+def split_degrees(tiles):
     last = 2
-    first = (tiles - last) * 5 // 11
-    return [w * LANES for w in (first, tiles - first - last, last)]
+    first = (tiles - last) * 10 // 21
+    return [first, tiles - last - first, last]
 
 
 def in_hbm(*arrays):
@@ -39,17 +36,24 @@
     return pltpu.CompilerParams(vmem_limit_bytes=VMEM_LIMIT, **kwargs)
 
 
+def width_of(piece):
+    return sum(width for _, _, width in piece)
+
+
 def cut_copies(pieces, blocks, me, legendre_ref, outs, sems):
     copies = []
-    for number, (x, offset, width) in enumerate(pieces):
-        start = pl.multiple_of((me ^ x) * blocks + offset, LANES)
-        copies.append(
-            pltpu.make_async_copy(
-                legendre_ref.at[:, :, pl.ds(start, width)],
-                outs[number].at[:, :, pl.ds(0, width)],
-                sems.at[number],
+    for piece, out in zip(pieces, outs):
+        at = 0
+        for x, offset, width in piece:
+            start = pl.multiple_of((me ^ x) * blocks + offset, LANES)
+            copies.append(
+                pltpu.make_async_copy(
+                    legendre_ref.at[:, :, pl.ds(start, width)],
+                    out.at[:, :, pl.ds(at, width)],
+                    sems.at[len(copies)],
+                )
             )
-        )
+            at += width
     return copies
 
 
@@ -63,14 +67,14 @@
 
 def cut(legendre, pieces, blocks):
     orders, rows, _ = legendre.shape
-    shapes = [jax.ShapeDtypeStruct((orders, rows, w), jnp.float32) for _, _, w in pieces]
-    size = sum(orders * rows * w * 4 for _, _, w in pieces)
+    shapes = [jax.ShapeDtypeStruct((orders, rows, width_of(p)), jnp.float32) for p in pieces]
+    size = sum(orders * rows * width_of(p) * 4 for p in pieces)
     return pl.pallas_call(
         functools.partial(cut_kernel, pieces, blocks),
         out_shape=shapes,
         in_specs=[pl.BlockSpec(memory_space=pltpu.HBM)],
         out_specs=[pl.BlockSpec(memory_space=pl.ANY)] * len(pieces),
-        scratch_shapes=[pltpu.SemaphoreType.DMA((len(pieces),))],
+        scratch_shapes=[pltpu.SemaphoreType.DMA((sum(map(len, pieces)),))],
         compiler_params=compiler_params(),
         cost_estimate=pl.CostEstimate(flops=0, bytes_accessed=40 * size, transcendentals=0),
         name="cut",
@@ -78,12 +82,12 @@
 
 
 def open_kernel(
-    pieces, carry, blocks, legendre_ref, cycles_ref, weight_ref, hits_ref, flux_ref, *refs
+    pieces, carry, blocks, ending, legendre_ref, cycles_ref, weight_ref, hits_ref, flux_ref, filter_ref, *refs
 ):
     count = len(pieces)
     me = lax.axis_index("blk")
     outs, own_ref = refs[:count], refs[count]
-    cycles, weight, hit_cycles, flux, sems, small_sems = refs[count + 1 :]
+    cycles, weight, hit_cycles, flux, sems, small_sems, filter_sems = refs[count + 1 :]
     orders, rows, columns = cycles.shape
     clusters = flux.shape[1]
     small = [
@@ -93,6 +97,19 @@
         )
     ]
     copies = cut_copies(pieces, blocks, me, legendre_ref, outs, sems)
+    if ending:
+        scales, channels, _ = filter_ref.shape
+        for s in range(scales):
+            k, row = divmod(s * channels, rows)
+            copies.append(
+                pltpu.make_async_copy(
+                    filter_ref.at[s, :, pl.ds(blocks - ending, ending)],
+                    outs[carry[0]].at[
+                        k, pl.ds(row, channels), pl.ds(width_of(pieces[carry[0]]) + columns, ending)
+                    ],
+                    filter_sems.at[s],
+                )
+            )
     for copy in small + copies:
         copy.start()
     small[1].wait()
@@ -117,24 +134,27 @@
         value = weight_column * (cycles[k] + added)
         own_ref[k] = value
         for i in carry:
-            outs[i][k, :, pl.ds(pieces[i][2], columns)] = value
+            outs[i][k, :, pl.ds(width_of(pieces[i]), columns)] = value
     for copy in copies:
         copy.wait()
 
 
-def open_blocks(legendre, cycles, weight, cluster_cycles, flux, pieces, carry, blocks):
+def open_blocks(
+    legendre, cycles, weight, cluster_cycles, flux, weights, pieces, carry, blocks, ending
+):
     orders, rows, columns = cycles.shape
-    shapes = [jax.ShapeDtypeStruct((orders, rows, w), jnp.float32) for _, _, w in pieces]
-    for i in carry:
-        shapes[i] = jax.ShapeDtypeStruct((orders, rows, pieces[i][2] + columns), jnp.float32)
+    shapes = [
+        jax.ShapeDtypeStruct((orders, rows, width_of(p) + (columns + ending if i in carry else 0)), jnp.float32)
+        for i, p in enumerate(pieces)
+    ]
     shapes.append(jax.ShapeDtypeStruct(cycles.shape, jnp.float32))
-    size = sum(orders * rows * w * 4 for _, _, w in pieces)
+    size = sum(orders * rows * width_of(p) * 4 for p in pieces)
     hbm = pl.BlockSpec(memory_space=pltpu.HBM)
     weight = weight.reshape(1, -1)
     return pl.pallas_call(
-        functools.partial(open_kernel, pieces, carry, blocks),
+        functools.partial(open_kernel, pieces, carry, blocks, ending),
         out_shape=shapes,
-        in_specs=[hbm] * 5,
+        in_specs=[hbm] * 6,
         out_specs=[
             pl.BlockSpec(memory_space=pltpu.VMEM if i in carry else pl.ANY)
             for i in range(len(pieces))
@@ -145,13 +165,14 @@
             pltpu.VMEM(weight.shape, jnp.float32),
             pltpu.VMEM(cluster_cycles.shape, jnp.int32),
             pltpu.VMEM(flux.shape, jnp.float32),
-            pltpu.SemaphoreType.DMA((len(pieces),)),
+            pltpu.SemaphoreType.DMA((sum(map(len, pieces)),)),
             pltpu.SemaphoreType.DMA((4,)),
+            pltpu.SemaphoreType.DMA((weights.shape[0],)),
         ],
         compiler_params=compiler_params(),
         cost_estimate=FREE,
         name="open",
-    )(*in_hbm(legendre, cycles, weight, cluster_cycles, flux))
+    )(*in_hbm(legendre, cycles, weight, cluster_cycles, flux, weights))
 
 
 def response_kernel(blocks, scales, skies, order_ref, weights_ref, out_ref, limit_ref):
@@ -222,6 +243,42 @@
     )(*[array for array, _ in pieces])
 
 
+def tile_sum(values, analysis, weights, keep, rows):
+    scales, channels = len(weights), len(weights[0])
+    columns = analysis.shape[0]
+    skies = columns // (2 * channels)
+    high, low = halves(values)
+    harmonics = jnp.dot(
+        analysis,
+        jnp.concatenate([high, high, low], axis=0),
+        preferred_element_type=jnp.float32,
+    )
+    harmonics = jnp.where(keep, harmonics, 0.0)
+    matched = []
+    for p in range(2):
+        for s in range(scales):
+            value = None
+            for f in range(channels):
+                begin = (p * channels + f) * skies
+                term = weights[s][f] * harmonics[begin : begin + skies, :]
+                value = term if value is None else value + term
+            matched.append(value)
+    matched_high, matched_low = halves(jnp.concatenate(matched, axis=0))
+    return lax.dot_general(
+        jnp.concatenate([high[:rows], low[:rows]], axis=0),
+        jnp.concatenate([matched_high, matched_low], axis=0),
+        (((1,), (1,)), ((), ())),
+        preferred_element_type=jnp.float32,
+    )
+
+
+def fold(total):
+    rows, columns = total.shape[0] // 2, total.shape[1] // 2
+    return (
+        (total[rows:, columns:] + total[rows:, :columns]) + total[:rows, columns:]
+    ) + total[:rows, :columns]
+
+
 def chunk_kernel(n, first, last, blocks, offset, starts, tiles, limits_ref, *refs):
     legendre = refs[:n]
     analysis_ref, weights_ref = refs[n : n + 2]
@@ -230,9 +287,6 @@
     response = rest.pop(0) if last else None
     orders, rows, _ = legendre[0].shape
     scales, channels, _ = weights_ref.shape
-    columns = analysis_ref.shape[1]
-    skies = columns // (2 * channels)
-    everything = n * rows
     totals = [None] * orders
 
     def begin_of(start):
@@ -255,38 +309,13 @@
                 ],
                 axis=0,
             )
-            high, low = halves(values)
-            harmonics = jnp.dot(
-                analysis_ref[k],
-                jnp.concatenate([high, high, low], axis=0),
-                preferred_element_type=jnp.float32,
-            )
-            harmonics = jnp.where(degree >= limits_ref[k : k + 1, :1], harmonics, 0.0)
-            matched = []
-            for p in range(2):
-                for s in range(scales):
-                    value = None
-                    for f in range(channels):
-                        begin = (p * channels + f) * skies
-                        term = weights[s][f] * harmonics[begin : begin + skies, :]
-                        value = term if value is None else value + term
-                    matched.append(value)
-            matched_high, matched_low = halves(jnp.concatenate(matched, axis=0))
-            product = lax.dot_general(
-                jnp.concatenate([high, low], axis=0),
-                jnp.concatenate([matched_high, matched_low], axis=0),
-                (((1,), (1,)), ((), ())),
-                preferred_element_type=jnp.float32,
-            )
+            keep = degree >= limits_ref[k : k + 1, :1]
+            product = tile_sum(values, analysis_ref[k], weights, keep, n * rows)
             totals[k] = product if totals[k] is None else totals[k] + product
         at += tile
 
     for k in range(orders):
-        total = totals[k]
-        result = (
-            (total[everything:, columns:] + total[everything:, :columns])
-            + total[:everything, columns:]
-        ) + total[:everything, :columns]
+        result = fold(totals[k])
         if before is not None:
             result = result + before[k]
         if last:
@@ -337,17 +366,69 @@
     )(limits, *operands)
 
 
+def ends_kernel(n, across, blocks, at, limits_ref, *refs):
+    home, near, *others = refs[:n]
+    analysis_ref, weights_ref, across_ref, own_in, own_out, near_out = refs[n:]
+    orders, rows, both = home.shape
+    size = both // 2
+    scales, channels, _ = weights_ref.shape
+    me = lax.axis_index("blk")
+    places = [
+        pl.multiple_of((me ^ x) * blocks + blocks - size, LANES) for x in (0, across)
+    ]
+    degree = blocks - size + lax.broadcasted_iota(jnp.int32, (1, size), 1)
+    degree = jnp.concatenate([degree, degree + ((me ^ across) - me) * blocks], axis=1)
+
+    def across_row(index):
+        k, row = divmod(index, rows)
+        return across_ref[k, row : row + 1, at : at + size]
+
+    weights = [
+        [
+            jnp.concatenate(
+                [weights_ref[s, f : f + 1, blocks - size :], across_row(s * channels + f)], axis=1
+            )
+            for f in range(channels)
+        ]
+        for s in range(scales)
+    ]
+    own_out[...] = own_in[...]
+    for k in range(orders):
+        beside = jnp.concatenate([near[k, :, pl.ds(place, size)] for place in places], axis=1)
+        values = jnp.concatenate([home[k], beside] + [other[k] for other in others], axis=0)
+        keep = degree >= limits_ref[k : k + 1, :1]
+        result = fold(tile_sum(values, analysis_ref[k], weights, keep, 2 * rows))
+        own_out[k * rows : (k + 1) * rows, :] += result[:rows]
+        near_out[k * rows : (k + 1) * rows, :] = result[rows:]
+
+
+def ends(limits, parts, analysis, weights, across_weights, at, own, across, blocks):
+    n = len(parts)
+    orders, rows, _ = parts[0].shape
+    vmem = pl.BlockSpec(memory_space=pltpu.VMEM)
+    operands = parts + [analysis, weights, across_weights, own]
+    return pl.pallas_call(
+        functools.partial(ends_kernel, n, across, blocks, at),
+        out_shape=[
+            jax.ShapeDtypeStruct(own.shape, own.dtype),
+            jax.ShapeDtypeStruct((orders * rows, own.shape[1]), own.dtype),
+        ],
+        in_specs=[vmem] * (len(operands) + 1),
+        out_specs=[vmem] * 2,
+        compiler_params=compiler_params(),
+        cost_estimate=FREE,
+        name="ends",
+    )(limits, *operands)
+
+
 def finish_kernel(degrees, *refs):
     parts, out_ref = refs[:-1], refs[-1]
     orders, rows, _ = out_ref.shape
-    total = parts[0][...]
-    for part in parts[1:]:
-        total = total + part[...]
     for k in range(orders):
+        total = sum(part[k * rows : (k + 1) * rows, :] for part in parts)
         at = orders * rows + k
-        out_ref[k] = total[k * rows : (k + 1) * rows, :] * (
-            degrees / jnp.sqrt(total[at : at + 1, :])
-        )
+        response = sum(part[at : at + 1, :] for part in parts if part.shape[0] > orders * rows)
+        out_ref[k] = total * (degrees / jnp.sqrt(response))
 
 
 def finish(parts, shape, degrees):
@@ -378,39 +459,55 @@
     channels = matched_filter_weights.shape[2]
     skies = columns // (2 * channels)
     weights = jnp.transpose(matched_filter_weights, (1, 2, 0))
-    widths = split_degrees(blocks)
+    scales = weights.shape[0]
+    orders, rows, _ = fourier_cycles.shape
+    far = list(range(2, n))
+    across = n - 1
+    order = [across] + [x for x in far if x != across]
+    tiles = blocks // LANES
+    if n == 4 and tiles >= 24 and scales * channels == orders * rows and rows % channels == 0:
+        ending = LANES
+        widths = [w * LANES for w in split_degrees(tiles - 1)]
+    else:
+        ending = 0
+        widths = [blocks]
     offsets = [sum(widths[:c]) for c in range(len(widths))]
 
     def send(value, x):
         return lax.ppermute(value, "blk", partner(x, n))
 
-    far = range(2, n)
-    first = widths[0]
-    top = n - 1
-    order = [top] + [x for x in far if x != top]
     *cuts, own = open_blocks(
         legendre,
         fourier_cycles,
         cycle_weight,
         cluster_cycles,
         cluster_flux,
-        [(x, 0, first) for x in order],
+        weights,
+        [[(x, 0, widths[0])] for x in order],
         [0],
         blocks,
+        ending,
     )
-    sent = [{x: (send(value, x), 0) for value, x in zip(cuts, order)}]
     then, _ = lax.optimization_barrier((legendre, cuts[0]))
-    pieces = [(x, at, w) for at, w in zip(offsets[1:], widths[1:]) for x in order]
-    *cuts, home = cut(then, pieces + [(0, 0, blocks)], blocks)
-    for c in range(1, len(widths)):
-        here = cuts[(c - 1) * len(order) : c * len(order)]
-        sent.append({x: (send(value, x), 0) for value, x in zip(here, order)})
+    pieces = [[(x, at, w)] for at, w in zip(offsets[1:], widths[1:]) for x in order]
+    if ending:
+        at = blocks - ending
+        pieces += [[(x, at, ending), (x ^ across, at, ending)] for x in order + [0]]
+    *more, home = cut(then, pieces + [[(0, 0, blocks)]], blocks)
+    cuts += more
+    sent = []
+    for offset in offsets:
+        sent.append({x: (send(cuts.pop(0), x), 0) for x in order})
+    if ending:
+        last_parts = {x: send(cuts.pop(0), x) for x in order}
+        (last_parts[0],) = cuts
     near = send(legendre, 1)
-    for c, offset in enumerate(offsets):
-        sent[c][0] = (home, offset)
-        sent[c][1] = (near, None)
-
-    cycles = {0: (own, 0), top: (sent[0][top][0], first)}
+    for offset, parts in zip(offsets, sent):
+        parts[0] = (home, offset)
+        parts[1] = (near, None)
+
+    carrier = sent[0][across][0]
+    cycles = {0: (own, 0), across: (carrier, widths[0])}
     bit = n // 4
     while bit:
         for x in list(cycles):
@@ -422,7 +519,7 @@
 
     total = None
     for c, (offset, width) in enumerate(zip(offsets, widths)):
-        final = c == len(widths) - 1
+        final = c == len(offsets) - 1
         result = chunk(
             limits,
             [sent[c][x] for x in range(n)],
@@ -435,8 +532,23 @@
             width,
         )
         total = result[0]
-    returned = [result[0]] + [send(result[x], x) for x in list(far) + [1]]
-    return finish(returned, fourier_cycles.shape, float(legendre.shape[2]))
+    returned = [send(result[x], x) for x in far + [1]]
+    own = result[0]
+    if ending:
+        last_parts[1] = near
+        own, beside = ends(
+            limits,
+            [last_parts[x] for x in range(n)],
+            analysis,
+            weights,
+            carrier,
+            widths[0] + columns,
+            own,
+            across,
+            blocks,
+        )
+        returned.append(send(beside, 1))
+    return finish([own] + returned, fourier_cycles.shape, float(legendre.shape[2]))
 
 
 def solution(mesh):

time: 46 us -> 45.7 us (level)
  waiting for transfers between devices: 26 us -> 22.4 us
  starting transfers between devices: 10.2 us -> 12.7 us
  Pallas kernels: 9.58 us -> 10.4 us
    ppermute x12 -> x15, waiting for transfers between devices: 26 us -> 22.4 us  [send(): return lax.ppermute(value, 'blk', partner(x, n))]
    ppermute x12 -> x15, starting transfers between devices: 10.2 us -> 12.7 us  [send(): return lax.ppermute(value, 'blk', partner(x, n))]
    pallas_call x1 -> x2, Pallas kernels: 1.28 us -> 1.98 us  [the longest x1 1.4 us: open_blocks(): pl.pallas_call(functools.partial(open_kernel, pieces, carry, blocks, endi...]
  transfers between devices with their start and end apart: 12 -> 15, of which waited for: 8 -> 7; matrix products, arithmetic and copies ran while one was open for 0% -> 0% of each run, Pallas kernels for 18% -> 21%
where the time goes in v4:
time: 45.7 us; the launch traced here: 45.6 us
  waiting for transfers between devices  22.4 us (49%)
  starting transfers between devices  12.7 us (28%)
  Pallas kernels  10.4 us (23%)
    ppermute x15, waiting for transfers between devices, send(): return lax.ppermute(value, 'blk', partner(x, n))  22.4 us
    ppermute x15, starting transfers between devices, send(): return lax.ppermute(value, 'blk', partner(x, n))  12.7 us
    pallas_call x3, Pallas kernels, chunk(): pl.pallas_call(functools.partial(chunk_kernel, n, first, last, blocks, of...  5.19 us
    pallas_call x1, Pallas kernels, cut(): pl.pallas_call(functools.partial(cut_kernel, pieces, blocks), out_shape=s...  1.58 us
    pallas_call x1, Pallas kernels, open_blocks(): pl.pallas_call(functools.partial(open_kernel, pieces, carry, blocks, endi...  1.4 us
    pallas_call x1, Pallas kernels, response_rows(): pl.pallas_call(functools.partial(response_kernel, blocks, scales, skies),...  0.93 us
  transfers between devices with their start and end apart: 15, of which 7 were waited for; matrix products, arithmetic and copies ran while one was open for 0% of the time, Pallas kernels for 21%

profile of v4, /device:TPU:1, one launch (start us, length us, event | category | flops | bytes accessed | tf_op | source)
XLA Modules:
  0.0 45.6 jit_solution(1149772251495689197)
XLA Ops:
  0.0 0.1 collective-permute-start
  0.1 1.4 %open.1 = (f32[2,32,1536]{2,1,0:T(8,128)S(1)}, f32[2,32,1280]{2,1,0:T(8,128)S(1)}, f32[2,32,128]{2,1,0:T(8,128)S(1)}) custom-call(f32[2,32,12288]{2,1,0:T(8,128)} %legendre_ref.2, f32[2,32,128]{2,1,0:T(8,128)} %cycles_ref.1, f32[1,32]{1,0:T(1,128)} %bitcast.8, s32[2,64]{1,0:T(2,128)} %hits_ref.1, f32[2,64,128]{2,1,0:T(8,128)} %flux_ref.1, f32[8,8,3072]{2,1,0:T(8,128)} %bitcast.2), custom_call_target="tpu_custom_call" | custom-call | tf_op jit(solution)/shard_map/open/pallas_call | solution.py:154
  1.5 2.7 %collective-permute-start.4 = (f32[2,32,1536]{2,1,0:T(8,128)S(1)}, f32[2,32,1536]{2,1,0:T(8,128)S(1)}, u32[]{:S(2)}, u32[]{:S(2)}) collective-permute-start(f32[2,32,1536]{2,1,0:T(8,128)S(1)} %get-tuple-element.26), channel_id=1, source_target_pairs={{0,3},{1,2},{2,1},{3,0},{4,7},{5,6},{6,5},{7,4},{8,11},{9,10},{10,... | collective-permute-start | bytes 1179656 | tf_op jit(solution)/shard_map/ppermute | solution.py:477
  4.1 1.6 %cut.1 = (f32[2,32,1408]{2,1,0:T(8,128)S(1)}, f32[2,32,1408]{2,1,0:T(8,128)S(1)}, f32[2,32,256]{2,1,0:T(8,128)S(1)}, f32[2,32,256]{2,1,0:T(8,128)S(1)}, f32[2,32...) custom-call(f32[2,32,12288]{2,1,0:T(8,128)} %legendre_ref.2), custom_call_target="tpu_custom_call" | custom-call | bytes 73400320 | tf_op jit(solution)/shard_map/cut/pallas_call | solution.py:72
  5.7 0.2 collective-permute-start.8
  5.9 1.3 %collective-permute-start.10 = (f32[2,32,1280]{2,1,0:T(8,128)S(1)}, f32[2,32,1280]{2,1,0:T(8,128)S(1)}, u32[]{:S(2)}, u32[]{:S(2)}) collective-permute-start(f32[2,32,1280]{2,1,0:T(8,128)S(1)} %get-tuple-element.37), channel_id=1, source_target_pairs={{0,2},{1,3},{2,0},{3,1},{4,6},{5,7},{6,4},{7,5},{8,10},{9,11},{10,... | collective-permute-start | bytes 983048 | tf_op jit(solution)/shard_map/ppermute | solution.py:477
  7.2 0.7 %collective-permute-start.9 = (f32[2,32,1408]{2,1,0:T(8,128)S(1)}, f32[2,32,1408]{2,1,0:T(8,128)S(1)}, u32[]{:S(2)}, u32[]{:S(2)}) collective-permute-start(f32[2,32,1408]{2,1,0:T(8,128)S(1)} %get-tuple-element.36), channel_id=1, source_target_pairs={{0,3},{1,2},{2,1},{3,0},{4,7},{5,6},{6,5},{7,4},{8,11},{9,10},{10,... | collective-permute-start | bytes 1081352 | tf_op jit(solution)/shard_map/ppermute | solution.py:477
  8.0 5.8 %collective-permute-done.4.refs_3_.refs_6_ = f32[2,32,1536]{2,1,0:T(8,128)S(1)} collective-permute-done((f32[2,32,1536]{2,1,0:T(8,128)S(1)}, f32[2,32,1536]{2,1,0:T(8,128)S(1)}, u32[]{:S(2)}, u32[]{:S(2)}) %collective-permute-start.4) | collective-permute-done | bytes 393248 | tf_op jit(solution)/shard_map/ppermute | solution.py:477
  13.8 0.3 collective-permute-start.3
  14.1 0.9 %collective-permute-done.3.refs_1_ = f32[2,32,128]{2,1,0:T(8,128)S(1)} collective-permute-done((f32[2,32,128]{2,1,0:T(8,128)S(1)}, f32[2,32,128]{2,1,0:T(8,128)S(1)}, u32[]{:S(2)}, u32[]{:S(2)}) %collective-permute-start.3) | collective-permute-done | bytes 32800 | tf_op jit(solution)/shard_map/ppermute | solution.py:477
  15.0 0.3 collective-permute-start.5
  15.3 13.1 %collective-permute-done.10.refs_2_ = f32[2,32,1280]{2,1,0:T(8,128)S(1)} collective-permute-done((f32[2,32,1280]{2,1,0:T(8,128)S(1)}, f32[2,32,1280]{2,1,0:T(8,128)S(1)}, u32[]{:S(2)}, u32[]{:S(2)}) %collective-permute-start.10) | collective-permute-done | bytes 327712 | tf_op jit(solution)/shard_map/ppermute | solution.py:477
  28.4 0.9 %collective-permute-start.6 = (f32[2,32,256]{2,1,0:T(8,128)S(1)}, f32[2,32,256]{2,1,0:T(8,128)S(1)}, u32[]{:S(2)}, u32[]{:S(2)}) collective-permute-start(f32[2,32,256]{2,1,0:T(8,128)S(1)} %get-tuple-element.33), channel_id=1, source_target_pairs={{0,2},{1,3},{2,0},{3,1},{4,6},{5,7},{6,4},{7,5},{8,10},{9,11},{10,... | collective-permute-start | bytes 196616 | tf_op jit(solution)/shard_map/ppermute | solution.py:477
  29.4 1.6 %collective-permute-start.7 = (f32[2,32,256]{2,1,0:T(8,128)S(1)}, f32[2,32,256]{2,1,0:T(8,128)S(1)}, u32[]{:S(2)}, u32[]{:S(2)}) collective-permute-start(f32[2,32,256]{2,1,0:T(8,128)S(1)} %get-tuple-element.34), channel_id=1, source_target_pairs={{0,3},{1,2},{2,1},{3,0},{4,7},{5,6},{6,5},{7,4},{8,11},{9,10},{10,... | collective-permute-start | bytes 196616 | tf_op jit(solution)/shard_map/ppermute | solution.py:477
  30.9 1.7 %collective-permute-start.1 = (f32[2,32,256]{2,1,0:T(8,128)S(1)}, f32[2,32,256]{2,1,0:T(8,128)S(1)}, u32[]{:S(2)}, u32[]{:S(2)}) collective-permute-start(f32[2,32,256]{2,1,0:T(8,128)S(1)} %get-tuple-element.29), channel_id=1, source_target_pairs={{0,2},{1,3},{2,0},{3,1},{4,6},{5,7},{6,4},{7,5},{8,10},{9,11},{10,... | collective-permute-start | bytes 196616 | tf_op jit(solution)/shard_map/ppermute | solution.py:477
  32.7 0.0 collective-permute-done.refs_1_
  32.7 0.3 collective-permute-start.2
  33.0 0.9 %response.1 = (f32[8,128]{1,0:T(8,128)S(1)}, s32[8,128]{1,0:T(8,128)S(1)}) custom-call(s32[2]{0:T(128)S(1)} %copy-done.1, f32[8,8,3072]{2,1,0:T(8,128)S(1)} %bitcast.3), custom_call_target="tpu_custom_call" | custom-call | tf_op jit(solution)/shard_map/response/pallas_call | solution.py:206
  34.0 0.1 prepare.1.refs_4_
  34.1 2.1 %chunk.3.refs_6_ = f32[2,128,128]{2,1,0:T(8,128)S(1)} custom-call(s32[8,128]{1,0:T(8,128)S(1)} %get-tuple-element.25.limits_ref, f32[2,32,3072]{2,1,0:T(8,128)S(1)} %get-tuple-element.32.refs_0_, f32[2,32,12288]{2,1,0:T(8,128)S(1)} %collective-permute-done.refs_1_, f32[2,32,1280]{2,1,0:T(8,128)S(1)} %collective-permute-done.10.refs_2_, ...), custom_call_target="tpu_custom_call" | custom-call | tf_op jit(solution)/shard_map/chunk/pallas_call | solution.py:349
  36.2 0.1 collective-permute-done.9.refs_3_
  36.3 2.5 %chunk.4.refs_6_ = f32[2,128,128]{2,1,0:T(8,128)S(1)} custom-call(s32[8,128]{1,0:T(8,128)S(1)} %get-tuple-element.25.limits_ref, f32[2,32,3072]{2,1,0:T(8,128)S(1)} %get-tuple-element.32.refs_0_, f32[2,32,12288]{2,1,0:T(8,128)S(1)} %collective-permute-done.refs_1_, f32[2,32,1408]{2,1,0:T(8,128)S(1)} %collective-permute-done.8.refs_2_, ...), custom_call_target="tpu_custom_call" | custom-call | tf_op jit(solution)/shard_map/chunk/pallas_call | solution.py:349
  38.8 0.3 collective-permute-done.7.refs_3_
  39.1 0.6 %chunk.5 = (f32[72,128]{1,0:T(8,128)S(1)}, f32[72,128]{1,0:T(8,128)S(1)}, f32[72,128]{1,0:T(8,128)S(1)}, f32[72,128]{1,0:T(8,128)S(1)}) custom-call(s32[8,128]{1,0:T(8,128)S(1)} %get-tuple-element.25.limits_ref, f32[2,32,3072]{2,1,0:T(8,128)S(1)} %get-tuple-element.32.refs_0_, f32[2,32,12288]{2,1,0:T(8,128)S(1)} %collective-permute-done.refs_1_, ...), custom_call_target="tpu_custom_call" | custom-call | tf_op jit(solution)/shard_map/chunk/pallas_call | solution.py:349
  39.7 1.9 %collective-permute-start.11 = (f32[72,128]{1,0:T(8,128)S(1)}, f32[72,128]{1,0:T(8,128)S(1)}, u32[]{:S(2)}, u32[]{:S(2)}) collective-permute-start(f32[72,128]{1,0:T(8,128)S(1)} %get-tuple-element.41), channel_id=1, source_target_pairs={{0,2},{1,3},{2,0},{3,1},{4,6},{5,7},{6,4},{7,5},{8,10},{9,11},{10,... | collective-permute-start | bytes 110600 | tf_op jit(solution)/shard_map/ppermute | solution.py:477
  41.5 0.1 collective-permute-start.12
  41.7 0.3 collective-permute-start.13
  42.0 0.6 %ends.1 = (f32[72,128]{1,0:T(8,128)S(1)}, f32[64,128]{1,0:T(8,128)S(1)}) custom-call(s32[8,128]{1,0:T(8,128)S(1)} %get-tuple-element.25.limits_ref, f32[2,32,256]{2,1,0:T(8,128)S(1)} %get-tuple-element.28.refs_0_, f32[2,32,12288]{2,1,0:T(8,128)S(1)} %collective-permute-done.refs_1_, f32[2,32,256]{2,1,0:T(8,128)S(1)} %collective-permute-done.1.refs_2_, ...), custom_call_target="tpu_custom_call" | custom-call | tf_op jit(solution)/shard_map/ends/pallas_call | solution.py:410
  42.6 0.2 collective-permute-start.14
  42.9 1.0 %collective-permute-done.14.refs_4_ = f32[64,128]{1,0:T(8,128)S(1)} collective-permute-done((f32[64,128]{1,0:T(8,128)S(1)}, f32[64,128]{1,0:T(8,128)S(1)}, u32[]{:S(2)}, u32[]{:S(2)}) %collective-permute-start.14) | collective-permute-done | bytes 32800 | tf_op jit(solution)/shard_map/ppermute | solution.py:477
  43.9 1.0 %collective-permute-done.12.refs_2_ = f32[72,128]{1,0:T(8,128)S(1)} collective-permute-done((f32[72,128]{1,0:T(8,128)S(1)}, f32[72,128]{1,0:T(8,128)S(1)}, u32[]{:S(2)}, u32[]{:S(2)}) %collective-permute-start.12) | collective-permute-done | bytes 36896 | tf_op jit(solution)/shard_map/ppermute | solution.py:477
  44.9 0.6 %finish.1 = f32[2,32,128]{2,1,0:T(8,128)} custom-call(f32[72,128]{1,0:T(8,128)S(1)} %get-tuple-element.40.refs_0_, f32[72,128]{1,0:T(8,128)S(1)} %collective-permute-done.11.refs_1_, f32[72,128]{1,0:T(8,128)S(1)} %collective-permute-done.12.refs_2_, f32[72,128]{1,0:T(8,128)S(1)} %collective-permute-done.13.refs_3_, f32[64,128]{1,0:T(8,128)S(1)} %collective-permute-done.14.refs_4_), custom_call_target="tpu_custom_call" | custom-call | tf_op jit(solution)/shard_map/finish/pallas_call | solution.py:436
  (12 shorter events, 0.0 us)
Async XLA Ops:
  0.0 32.7 %collective-permute-start = (f32[2,32,12288]{2,1,0:T(8,128)}, f32[2,32,12288]{2,1,0:T(8,128)S(1)}, u32[]{:S(2)}, u32[]{:S(2)}) collective-permute-start(f32[2,32,12288]{2,1,0:T(8,128)} %legendre_ref.2), channel_id=1, source_target_pairs={{0,1},{1,0},{2,3},{3,2},{4,5},{5,4},{6,7},{7,6},{8,9},{9,8},{10,11... | collective-permute-start | bytes 9437192 | tf_op jit(solution)/shard_map/ppermute | solution.py:477
  0.1 33.0 %copy-start = (f32[3072,8,8]{0,2,1:T(8,128)S(1)}, f32[3072,8,8]{0,2,1:T(8,128)}, u32[]{:S(2)}) copy-start(f32[3072,8,8]{0,2,1:T(8,128)} %param.10) | copy-start | bytes 2359300
  0.1 33.0 %copy-start.1 = (s32[2]{0:T(128)S(1)}, s32[2]{0:T(128)}, u32[]{:S(2)}) copy-start(s32[2]{0:T(128)} %order_ref.1) | copy-start | bytes 28
  1.5 12.3 %collective-permute-start.4 = (f32[2,32,1536]{2,1,0:T(8,128)S(1)}, f32[2,32,1536]{2,1,0:T(8,128)S(1)}, u32[]{:S(2)}, u32[]{:S(2)}) collective-permute-start(f32[2,32,1536]{2,1,0:T(8,128)S(1)} %get-tuple-element.26), channel_id=1, source_target_pairs={{0,3},{1,2},{2,1},{3,0},{4,7},{5,6},{6,5},{7,4},{8,11},{9,10},{10,... | collective-permute-start | bytes 1179656 | tf_op jit(solution)/shard_map/ppermute | solution.py:477
  5.7 23.7 %collective-permute-start.8 = (f32[2,32,1408]{2,1,0:T(8,128)S(1)}, f32[2,32,1408]{2,1,0:T(8,128)S(1)}, u32[]{:S(2)}, u32[]{:S(2)}) collective-permute-start(f32[2,32,1408]{2,1,0:T(8,128)S(1)} %get-tuple-element.35), channel_id=1, source_target_pairs={{0,2},{1,3},{2,0},{3,1},{4,6},{5,7},{6,4},{7,5},{8,10},{9,11},{10,... | collective-permute-start | bytes 1081352 | tf_op jit(solution)/shard_map/ppermute | solution.py:477
  5.9 22.5 %collective-permute-start.10 = (f32[2,32,1280]{2,1,0:T(8,128)S(1)}, f32[2,32,1280]{2,1,0:T(8,128)S(1)}, u32[]{:S(2)}, u32[]{:S(2)}) collective-permute-start(f32[2,32,1280]{2,1,0:T(8,128)S(1)} %get-tuple-element.37), channel_id=1, source_target_pairs={{0,2},{1,3},{2,0},{3,1},{4,6},{5,7},{6,4},{7,5},{8,10},{9,11},{10,... | collective-permute-start | bytes 983048 | tf_op jit(solution)/shard_map/ppermute | solution.py:477
  7.2 29.0 %collective-permute-start.9 = (f32[2,32,1408]{2,1,0:T(8,128)S(1)}, f32[2,32,1408]{2,1,0:T(8,128)S(1)}, u32[]{:S(2)}, u32[]{:S(2)}) collective-permute-start(f32[2,32,1408]{2,1,0:T(8,128)S(1)} %get-tuple-element.36), channel_id=1, source_target_pairs={{0,3},{1,2},{2,1},{3,0},{4,7},{5,6},{6,5},{7,4},{8,11},{9,10},{10,... | collective-permute-start | bytes 1081352 | tf_op jit(solution)/shard_map/ppermute | solution.py:477
  13.8 1.2 %collective-permute-start.3 = (f32[2,32,128]{2,1,0:T(8,128)S(1)}, f32[2,32,128]{2,1,0:T(8,128)S(1)}, u32[]{:S(2)}, u32[]{:S(2)}) collective-permute-start(f32[2,32,128]{2,1,0:T(8,128)S(1)} %get-tuple-element.31.refs_0_), channel_id=1, source_target_pairs={{0,1},{1,0},{2,3},{3,2},{4,5},{5,4},{6,7},{7,6},{8,9},{9,8},{10,11... | collective-permute-start | bytes 98312 | tf_op jit(solution)/shard_map/ppermute | solution.py:477
  15.0 15.9 %collective-permute-start.5 = (f32[2,32,128]{2,1,0:T(8,128)S(1)}, f32[2,32,128]{2,1,0:T(8,128)S(1)}, u32[]{:S(2)}, u32[]{:S(2)}) collective-permute-start(f32[2,32,128]{2,1,0:T(8,128)S(1)} %slice.4), channel_id=1, source_target_pairs={{0,1},{1,0},{2,3},{3,2},{4,5},{5,4},{6,7},{7,6},{8,9},{9,8},{10,11... | collective-permute-start | bytes 98312 | tf_op jit(solution)/shard_map/ppermute | solution.py:477
  28.4 10.3 %collective-permute-start.6 = (f32[2,32,256]{2,1,0:T(8,128)S(1)}, f32[2,32,256]{2,1,0:T(8,128)S(1)}, u32[]{:S(2)}, u32[]{:S(2)}) collective-permute-start(f32[2,32,256]{2,1,0:T(8,128)S(1)} %get-tuple-element.33), channel_id=1, source_target_pairs={{0,2},{1,3},{2,0},{3,1},{4,6},{5,7},{6,4},{7,5},{8,10},{9,11},{10,... | collective-permute-start | bytes 196616 | tf_op jit(solution)/shard_map/ppermute | solution.py:477
  29.4 9.7 %collective-permute-start.7 = (f32[2,32,256]{2,1,0:T(8,128)S(1)}, f32[2,32,256]{2,1,0:T(8,128)S(1)}, u32[]{:S(2)}, u32[]{:S(2)}) collective-permute-start(f32[2,32,256]{2,1,0:T(8,128)S(1)} %get-tuple-element.34), channel_id=1, source_target_pairs={{0,3},{1,2},{2,1},{3,0},{4,7},{5,6},{6,5},{7,4},{8,11},{9,10},{10,... | collective-permute-start | bytes 196616 | tf_op jit(solution)/shard_map/ppermute | solution.py:477
  30.9 11.1 %collective-permute-start.1 = (f32[2,32,256]{2,1,0:T(8,128)S(1)}, f32[2,32,256]{2,1,0:T(8,128)S(1)}, u32[]{:S(2)}, u32[]{:S(2)}) collective-permute-start(f32[2,32,256]{2,1,0:T(8,128)S(1)} %get-tuple-element.29), channel_id=1, source_target_pairs={{0,2},{1,3},{2,0},{3,1},{4,6},{5,7},{6,4},{7,5},{8,10},{9,11},{10,... | collective-permute-start | bytes 196616 | tf_op jit(solution)/shard_map/ppermute | solution.py:477
  32.7 9.4 %collective-permute-start.2 = (f32[2,32,256]{2,1,0:T(8,128)S(1)}, f32[2,32,256]{2,1,0:T(8,128)S(1)}, u32[]{:S(2)}, u32[]{:S(2)}) collective-permute-start(f32[2,32,256]{2,1,0:T(8,128)S(1)} %get-tuple-element.30), channel_id=1, source_target_pairs={{0,3},{1,2},{2,1},{3,0},{4,7},{5,6},{6,5},{7,4},{8,11},{9,10},{10,... | collective-permute-start | bytes 196616 | tf_op jit(solution)/shard_map/ppermute | solution.py:477
  39.7 4.2 %collective-permute-start.11 = (f32[72,128]{1,0:T(8,128)S(1)}, f32[72,128]{1,0:T(8,128)S(1)}, u32[]{:S(2)}, u32[]{:S(2)}) collective-permute-start(f32[72,128]{1,0:T(8,128)S(1)} %get-tuple-element.41), channel_id=1, source_target_pairs={{0,2},{1,3},{2,0},{3,1},{4,6},{5,7},{6,4},{7,5},{8,10},{9,11},{10,... | collective-permute-start | bytes 110600 | tf_op jit(solution)/shard_map/ppermute | solution.py:477
  41.5 3.4 %collective-permute-start.12 = (f32[72,128]{1,0:T(8,128)S(1)}, f32[72,128]{1,0:T(8,128)S(1)}, u32[]{:S(2)}, u32[]{:S(2)}) collective-permute-start(f32[72,128]{1,0:T(8,128)S(1)} %get-tuple-element.42), channel_id=1, source_target_pairs={{0,3},{1,2},{2,1},{3,0},{4,7},{5,6},{6,5},{7,4},{8,11},{9,10},{10,... | collective-permute-start | bytes 110600 | tf_op jit(solution)/shard_map/ppermute | solution.py:477
  41.7 3.2 %collective-permute-start.13 = (f32[72,128]{1,0:T(8,128)S(1)}, f32[72,128]{1,0:T(8,128)S(1)}, u32[]{:S(2)}, u32[]{:S(2)}) collective-permute-start(f32[72,128]{1,0:T(8,128)S(1)} %get-tuple-element.43), channel_id=1, source_target_pairs={{0,1},{1,0},{2,3},{3,2},{4,5},{5,4},{6,7},{7,6},{8,9},{9,8},{10,11... | collective-permute-start | bytes 110600 | tf_op jit(solution)/shard_map/ppermute | solution.py:477
  42.6 1.3 %collective-permute-start.14 = (f32[64,128]{1,0:T(8,128)S(1)}, f32[64,128]{1,0:T(8,128)S(1)}, u32[]{:S(2)}, u32[]{:S(2)}) collective-permute-start(f32[64,128]{1,0:T(8,128)S(1)} %get-tuple-element.44), channel_id=1, source_target_pairs={{0,1},{1,0},{2,3},{3,2},{4,5},{5,4},{6,7},{7,6},{8,9},{9,8},{10,11... | collective-permute-start | bytes 98312 | tf_op jit(solution)/shard_map/ppermute | solution.py:477

commit v5 on v4

--- a/solution.py
+++ b/solution.py
@@ -18,7 +18,7 @@
 
 def split_degrees(tiles):
     last = 2
-    first = (tiles - last) * 10 // 21
+    first = (tiles - last) * 11 // 21
     return [first, tiles - last - first, last]
 
 
@@ -57,37 +57,57 @@
     return copies
 
 
-def cut_kernel(pieces, blocks, legendre_ref, *refs):
-    copies = cut_copies(pieces, blocks, lax.axis_index("blk"), legendre_ref, refs[:-1], refs[-1])
+def cut_kernel(pieces, blocks, carry, ending, legendre_ref, *refs):
+    filter_ref, *outs = refs[:-2] if ending else (None, *refs[:-2])
+    copies = cut_copies(pieces, blocks, lax.axis_index("blk"), legendre_ref, outs, refs[-2])
+    if ending:
+        scales, channels, _ = filter_ref.shape
+        rows, at = legendre_ref.shape[1], width_of(pieces[carry])
+        for s in range(scales):
+            k, row = divmod(s * channels, rows)
+            copies.append(
+                pltpu.make_async_copy(
+                    filter_ref.at[s, :, pl.ds(blocks - ending, ending)],
+                    outs[carry].at[k, pl.ds(row, channels), pl.ds(at, ending)],
+                    refs[-1].at[s],
+                )
+            )
     for copy in copies:
         copy.start()
     for copy in copies:
         copy.wait()
 
 
-def cut(legendre, pieces, blocks):
+def cut(legendre, weights, pieces, blocks, carry, ending):
     orders, rows, _ = legendre.shape
-    shapes = [jax.ShapeDtypeStruct((orders, rows, width_of(p)), jnp.float32) for p in pieces]
+    shapes = [
+        jax.ShapeDtypeStruct((orders, rows, width_of(p) + (ending if i == carry else 0)), jnp.float32)
+        for i, p in enumerate(pieces)
+    ]
+    operands = in_hbm(legendre, weights) if ending else in_hbm(legendre)
     size = sum(orders * rows * width_of(p) * 4 for p in pieces)
     return pl.pallas_call(
-        functools.partial(cut_kernel, pieces, blocks),
+        functools.partial(cut_kernel, pieces, blocks, carry, ending),
         out_shape=shapes,
-        in_specs=[pl.BlockSpec(memory_space=pltpu.HBM)],
+        in_specs=[pl.BlockSpec(memory_space=pltpu.HBM)] * len(operands),
         out_specs=[pl.BlockSpec(memory_space=pl.ANY)] * len(pieces),
-        scratch_shapes=[pltpu.SemaphoreType.DMA((sum(map(len, pieces)),))],
+        scratch_shapes=[
+            pltpu.SemaphoreType.DMA((sum(map(len, pieces)),)),
+            pltpu.SemaphoreType.DMA((weights.shape[0],)),
+        ],
         compiler_params=compiler_params(),
         cost_estimate=pl.CostEstimate(flops=0, bytes_accessed=40 * size, transcendentals=0),
         name="cut",
-    )(*in_hbm(legendre))
+    )(*operands)
 
 
 def open_kernel(
-    pieces, carry, blocks, ending, legendre_ref, cycles_ref, weight_ref, hits_ref, flux_ref, filter_ref, *refs
+    pieces, carry, blocks, legendre_ref, cycles_ref, weight_ref, hits_ref, flux_ref, *refs
 ):
     count = len(pieces)
     me = lax.axis_index("blk")
     outs, own_ref = refs[:count], refs[count]
-    cycles, weight, hit_cycles, flux, sems, small_sems, filter_sems = refs[count + 1 :]
+    cycles, weight, hit_cycles, flux, sems, small_sems = refs[count + 1 :]
     orders, rows, columns = cycles.shape
     clusters = flux.shape[1]
     small = [
@@ -97,19 +117,6 @@
         )
     ]
     copies = cut_copies(pieces, blocks, me, legendre_ref, outs, sems)
-    if ending:
-        scales, channels, _ = filter_ref.shape
-        for s in range(scales):
-            k, row = divmod(s * channels, rows)
-            copies.append(
-                pltpu.make_async_copy(
-                    filter_ref.at[s, :, pl.ds(blocks - ending, ending)],
-                    outs[carry[0]].at[
-                        k, pl.ds(row, channels), pl.ds(width_of(pieces[carry[0]]) + columns, ending)
-                    ],
-                    filter_sems.at[s],
-                )
-            )
     for copy in small + copies:
         copy.start()
     small[1].wait()
@@ -139,12 +146,10 @@
         copy.wait()
 
 
-def open_blocks(
-    legendre, cycles, weight, cluster_cycles, flux, weights, pieces, carry, blocks, ending
-):
+def open_blocks(legendre, cycles, weight, cluster_cycles, flux, pieces, carry, blocks):
     orders, rows, columns = cycles.shape
     shapes = [
-        jax.ShapeDtypeStruct((orders, rows, width_of(p) + (columns + ending if i in carry else 0)), jnp.float32)
+        jax.ShapeDtypeStruct((orders, rows, width_of(p) + (columns if i in carry else 0)), jnp.float32)
         for i, p in enumerate(pieces)
     ]
     shapes.append(jax.ShapeDtypeStruct(cycles.shape, jnp.float32))
@@ -152,9 +157,9 @@
     hbm = pl.BlockSpec(memory_space=pltpu.HBM)
     weight = weight.reshape(1, -1)
     return pl.pallas_call(
-        functools.partial(open_kernel, pieces, carry, blocks, ending),
+        functools.partial(open_kernel, pieces, carry, blocks),
         out_shape=shapes,
-        in_specs=[hbm] * 6,
+        in_specs=[hbm] * 5,
         out_specs=[
             pl.BlockSpec(memory_space=pltpu.VMEM if i in carry else pl.ANY)
             for i in range(len(pieces))
@@ -167,12 +172,11 @@
             pltpu.VMEM(flux.shape, jnp.float32),
             pltpu.SemaphoreType.DMA((sum(map(len, pieces)),)),
             pltpu.SemaphoreType.DMA((4,)),
-            pltpu.SemaphoreType.DMA((weights.shape[0],)),
         ],
         compiler_params=compiler_params(),
         cost_estimate=FREE,
         name="open",
-    )(*in_hbm(legendre, cycles, weight, cluster_cycles, flux, weights))
+    )(*in_hbm(legendre, cycles, weight, cluster_cycles, flux))
 
 
 def response_kernel(blocks, scales, skies, order_ref, weights_ref, out_ref, limit_ref):
@@ -482,18 +486,17 @@
         cycle_weight,
         cluster_cycles,
         cluster_flux,
-        weights,
-        [[(x, 0, widths[0])] for x in order],
+        [[(across, 0, widths[0])]],
         [0],
         blocks,
-        ending,
     )
     then, _ = lax.optimization_barrier((legendre, cuts[0]))
-    pieces = [[(x, at, w)] for at, w in zip(offsets[1:], widths[1:]) for x in order]
+    pieces = [[(x, at, w)] for at, w in zip(offsets, widths) for x in order][1:]
     if ending:
         at = blocks - ending
         pieces += [[(x, at, ending), (x ^ across, at, ending)] for x in order + [0]]
-    *more, home = cut(then, pieces + [[(0, 0, blocks)]], blocks)
+    carry = [p[0] for p in pieces].index((across, offsets[1], widths[1])) if ending else 0
+    *more, home = cut(then, weights, pieces + [[(0, 0, blocks)]], blocks, carry, ending)
     cuts += more
     sent = []
     for offset in offsets:
@@ -541,8 +544,8 @@
             [last_parts[x] for x in range(n)],
             analysis,
             weights,
-            carrier,
-            widths[0] + columns,
+            sent[1][across][0],
+            widths[1],
             own,
             across,
             blocks,

time: 45.7 us -> 45.5 us (level)
  transfers between devices with their start and end apart: 15 -> 15, of which waited for: 7 -> 6; matrix products, arithmetic and copies ran while one was open for 0% -> 0% of each run, Pallas kernels for 21% -> 22%
where the time goes in v5:
time: 45.5 us; the launch traced here: 45.4 us
  waiting for transfers between devices  22.1 us (49%)
  starting transfers between devices  12.7 us (28%)
  Pallas kernels  10.4 us (23%)
    ppermute x15, waiting for transfers between devices, send(): return lax.ppermute(value, 'blk', partner(x, n))  22.1 us
    ppermute x15, starting transfers between devices, send(): return lax.ppermute(value, 'blk', partner(x, n))  12.7 us
    pallas_call x3, Pallas kernels, chunk(): pl.pallas_call(functools.partial(chunk_kernel, n, first, last, blocks, of...  5.21 us
    pallas_call x1, Pallas kernels, cut(): pl.pallas_call(functools.partial(cut_kernel, pieces, blocks, carry, endin...  1.8 us
    pallas_call x1, Pallas kernels, open_blocks(): pl.pallas_call(functools.partial(open_kernel, pieces, carry, blocks), out...  1.18 us
    pallas_call x1, Pallas kernels, response_rows(): pl.pallas_call(functools.partial(response_kernel, blocks, scales, skies),...  0.93 us
  transfers between devices with their start and end apart: 15, of which 6 were waited for; matrix products, arithmetic and copies ran while one was open for 0% of the time, Pallas kernels for 22%

profile of v5, /device:TPU:1, one launch (start us, length us, event | category | flops | bytes accessed | tf_op | source)
XLA Modules:
  0.0 45.4 jit_solution(895523921840721959)
XLA Ops:
  0.0 0.1 collective-permute-start
  0.1 1.2 %open.1 = (f32[2,32,1536]{2,1,0:T(8,128)S(1)}, f32[2,32,128]{2,1,0:T(8,128)S(1)}) custom-call(f32[2,32,12288]{2,1,0:T(8,128)} %legendre_ref.2, f32[2,32,128]{2,1,0:T(8,128)} %cycles_ref.1, f32[1,32]{1,0:T(1,128)} %bitcast.8, s32[2,64]{1,0:T(2,128)} %hits_ref.1, f32[2,64,128]{2,1,0:T(8,128)} %flux_ref.1), custom_call_target="tpu_custom_call" | custom-call | tf_op jit(solution)/shard_map/open/pallas_call | solution.py:159
  1.3 2.6 %collective-permute-start.4 = (f32[2,32,1536]{2,1,0:T(8,128)S(1)}, f32[2,32,1536]{2,1,0:T(8,128)S(1)}, u32[]{:S(2)}, u32[]{:S(2)}) collective-permute-start(f32[2,32,1536]{2,1,0:T(8,128)S(1)} %get-tuple-element.26), channel_id=1, source_target_pairs={{0,3},{1,2},{2,1},{3,0},{4,7},{5,6},{6,5},{7,4},{8,11},{9,10},{10,... | collective-permute-start | bytes 1179656 | tf_op jit(solution)/shard_map/ppermute | solution.py:481
  3.9 1.8 %cut.1 = (f32[2,32,1408]{2,1,0:T(8,128)S(1)}, f32[2,32,1408]{2,1,0:T(8,128)S(1)}, f32[2,32,1280]{2,1,0:T(8,128)S(1)}, f32[2,32,256]{2,1,0:T(8,128)S(1)}, f32[2,3...) custom-call(f32[2,32,12288]{2,1,0:T(8,128)} %legendre_ref.2, ...), custom_call_target="tpu_custom_call" | custom-call | bytes 85196800 | tf_op jit(solution)/shard_map/cut/pallas_call | solution.py:89
  5.7 0.2 collective-permute-start.10
  5.9 1.3 %collective-permute-start.9 = (f32[2,32,1280]{2,1,0:T(8,128)S(1)}, f32[2,32,1280]{2,1,0:T(8,128)S(1)}, u32[]{:S(2)}, u32[]{:S(2)}) collective-permute-start(f32[2,32,1280]{2,1,0:T(8,128)S(1)} %get-tuple-element.36), channel_id=1, source_target_pairs={{0,2},{1,3},{2,0},{3,1},{4,6},{5,7},{6,4},{7,5},{8,10},{9,11},{10,... | collective-permute-start | bytes 983048 | tf_op jit(solution)/shard_map/ppermute | solution.py:481
  7.2 0.7 %collective-permute-start.6 = (f32[2,32,1408]{2,1,0:T(8,128)S(1)}, f32[2,32,1408]{2,1,0:T(8,128)S(1)}, u32[]{:S(2)}, u32[]{:S(2)}) collective-permute-start(f32[2,32,1408]{2,1,0:T(8,128)S(1)} %get-tuple-element.32), channel_id=1, source_target_pairs={{0,3},{1,2},{2,1},{3,0},{4,7},{5,6},{6,5},{7,4},{8,11},{9,10},{10,... | collective-permute-start | bytes 1081352 | tf_op jit(solution)/shard_map/ppermute | solution.py:481
  8.0 5.6 %collective-permute-done.4.refs_3_ = f32[2,32,1536]{2,1,0:T(8,128)S(1)} collective-permute-done((f32[2,32,1536]{2,1,0:T(8,128)S(1)}, f32[2,32,1536]{2,1,0:T(8,128)S(1)}, u32[]{:S(2)}, u32[]{:S(2)}) %collective-permute-start.4) | collective-permute-done | bytes 393248 | tf_op jit(solution)/shard_map/ppermute | solution.py:481
  13.6 0.3 collective-permute-start.3
  13.9 0.9 %collective-permute-done.3.refs_1_ = f32[2,32,128]{2,1,0:T(8,128)S(1)} collective-permute-done((f32[2,32,128]{2,1,0:T(8,128)S(1)}, f32[2,32,128]{2,1,0:T(8,128)S(1)}, u32[]{:S(2)}, u32[]{:S(2)}) %collective-permute-start.3) | collective-permute-done | bytes 32800 | tf_op jit(solution)/shard_map/ppermute | solution.py:481
  14.8 0.3 collective-permute-start.5
  15.1 13.1 %collective-permute-done.9.refs_2_ = f32[2,32,1280]{2,1,0:T(8,128)S(1)} collective-permute-done((f32[2,32,1280]{2,1,0:T(8,128)S(1)}, f32[2,32,1280]{2,1,0:T(8,128)S(1)}, u32[]{:S(2)}, u32[]{:S(2)}) %collective-permute-start.9) | collective-permute-done | bytes 327712 | tf_op jit(solution)/shard_map/ppermute | solution.py:481
  28.2 0.9 %collective-permute-start.7 = (f32[2,32,256]{2,1,0:T(8,128)S(1)}, f32[2,32,256]{2,1,0:T(8,128)S(1)}, u32[]{:S(2)}, u32[]{:S(2)}) collective-permute-start(f32[2,32,256]{2,1,0:T(8,128)S(1)} %get-tuple-element.34), channel_id=1, source_target_pairs={{0,2},{1,3},{2,0},{3,1},{4,6},{5,7},{6,4},{7,5},{8,10},{9,11},{10,... | collective-permute-start | bytes 196616 | tf_op jit(solution)/shard_map/ppermute | solution.py:481
  29.1 0.0 collective-permute-done.10.refs_2_
  29.1 1.6 %collective-permute-start.8 = (f32[2,32,256]{2,1,0:T(8,128)S(1)}, f32[2,32,256]{2,1,0:T(8,128)S(1)}, u32[]{:S(2)}, u32[]{:S(2)}) collective-permute-start(f32[2,32,256]{2,1,0:T(8,128)S(1)} %get-tuple-element.35), channel_id=1, source_target_pairs={{0,3},{1,2},{2,1},{3,0},{4,7},{5,6},{6,5},{7,4},{8,11},{9,10},{10,... | collective-permute-start | bytes 196616 | tf_op jit(solution)/shard_map/ppermute | solution.py:481
  30.7 1.7 %collective-permute-start.1 = (f32[2,32,256]{2,1,0:T(8,128)S(1)}, f32[2,32,256]{2,1,0:T(8,128)S(1)}, u32[]{:S(2)}, u32[]{:S(2)}) collective-permute-start(f32[2,32,256]{2,1,0:T(8,128)S(1)} %get-tuple-element.29), channel_id=1, source_target_pairs={{0,2},{1,3},{2,0},{3,1},{4,6},{5,7},{6,4},{7,5},{8,10},{9,11},{10,... | collective-permute-start | bytes 196616 | tf_op jit(solution)/shard_map/ppermute | solution.py:481
  32.4 0.0 collective-permute-done.refs_1_
  32.4 0.3 collective-permute-start.2
  32.8 0.9 %response.1 = (f32[8,128]{1,0:T(8,128)S(1)}, s32[8,128]{1,0:T(8,128)S(1)}) custom-call(s32[2]{0:T(128)S(1)} %copy-done.1, f32[8,8,3072]{2,1,0:T(8,128)S(1)} %bitcast.3), custom_call_target="tpu_custom_call" | custom-call | tf_op jit(solution)/shard_map/response/pallas_call | solution.py:210
  33.7 0.1 prepare.1.refs_4_
  33.8 2.5 %chunk.3.refs_6_ = f32[2,128,128]{2,1,0:T(8,128)S(1)} custom-call(s32[8,128]{1,0:T(8,128)S(1)} %get-tuple-element.25.limits_ref, f32[2,32,3072]{2,1,0:T(8,128)S(1)} %get-tuple-element.33.refs_0_, f32[2,32,12288]{2,1,0:T(8,128)S(1)} %collective-permute-done.refs_1_, f32[2,32,1408]{2,1,0:T(8,128)S(1)} %collective-permute-done.10.refs_2_, ...), custom_call_target="tpu_custom_call" | custom-call | tf_op jit(solution)/shard_map/chunk/pallas_call | solution.py:353
  36.4 2.1 %chunk.4.refs_6_ = f32[2,128,128]{2,1,0:T(8,128)S(1)} custom-call(s32[8,128]{1,0:T(8,128)S(1)} %get-tuple-element.25.limits_ref, f32[2,32,3072]{2,1,0:T(8,128)S(1)} %get-tuple-element.33.refs_0_, f32[2,32,12288]{2,1,0:T(8,128)S(1)} %collective-permute-done.refs_1_, f32[2,32,1280]{2,1,0:T(8,128)S(1)} %collective-permute-done.9.refs_2_, ...), custom_call_target="tpu_custom_call" | custom-call | tf_op jit(solution)/shard_map/chunk/pallas_call | solution.py:353
  38.5 0.4 collective-permute-done.8.refs_3_
  38.9 0.6 %chunk.5 = (f32[72,128]{1,0:T(8,128)S(1)}, f32[72,128]{1,0:T(8,128)S(1)}, f32[72,128]{1,0:T(8,128)S(1)}, f32[72,128]{1,0:T(8,128)S(1)}) custom-call(s32[8,128]{1,0:T(8,128)S(1)} %get-tuple-element.25.limits_ref, f32[2,32,3072]{2,1,0:T(8,128)S(1)} %get-tuple-element.33.refs_0_, f32[2,32,12288]{2,1,0:T(8,128)S(1)} %collective-permute-done.refs_1_, ...), custom_call_target="tpu_custom_call" | custom-call | tf_op jit(solution)/shard_map/chunk/pallas_call | solution.py:353
  39.5 1.9 %collective-permute-start.11 = (f32[72,128]{1,0:T(8,128)S(1)}, f32[72,128]{1,0:T(8,128)S(1)}, u32[]{:S(2)}, u32[]{:S(2)}) collective-permute-start(f32[72,128]{1,0:T(8,128)S(1)} %get-tuple-element.41), channel_id=1, source_target_pairs={{0,2},{1,3},{2,0},{3,1},{4,6},{5,7},{6,4},{7,5},{8,10},{9,11},{10,... | collective-permute-start | bytes 110600 | tf_op jit(solution)/shard_map/ppermute | solution.py:481
  41.3 0.1 collective-permute-start.12
  41.5 0.3 collective-permute-start.13
  41.8 0.6 %ends.1 = (f32[72,128]{1,0:T(8,128)S(1)}, f32[64,128]{1,0:T(8,128)S(1)}) custom-call(s32[8,128]{1,0:T(8,128)S(1)} %get-tuple-element.25.limits_ref, f32[2,32,256]{2,1,0:T(8,128)S(1)} %get-tuple-element.28.refs_0_, f32[2,32,12288]{2,1,0:T(8,128)S(1)} %collective-permute-done.refs_1_, f32[2,32,256]{2,1,0:T(8,128)S(1)} %collective-permute-done.1.refs_2_, ...), custom_call_target="tpu_custom_call" | custom-call | tf_op jit(solution)/shard_map/ends/pallas_call | solution.py:414
  42.4 0.2 collective-permute-start.14
  42.6 1.0 %collective-permute-done.14.refs_4_ = f32[64,128]{1,0:T(8,128)S(1)} collective-permute-done((f32[64,128]{1,0:T(8,128)S(1)}, f32[64,128]{1,0:T(8,128)S(1)}, u32[]{:S(2)}, u32[]{:S(2)}) %collective-permute-start.14) | collective-permute-done | bytes 32800 | tf_op jit(solution)/shard_map/ppermute | solution.py:481
  43.7 1.0 %collective-permute-done.12.refs_2_ = f32[72,128]{1,0:T(8,128)S(1)} collective-permute-done((f32[72,128]{1,0:T(8,128)S(1)}, f32[72,128]{1,0:T(8,128)S(1)}, u32[]{:S(2)}, u32[]{:S(2)}) %collective-permute-start.12) | collective-permute-done | bytes 36896 | tf_op jit(solution)/shard_map/ppermute | solution.py:481
  44.7 0.6 %finish.1 = f32[2,32,128]{2,1,0:T(8,128)} custom-call(f32[72,128]{1,0:T(8,128)S(1)} %get-tuple-element.40.refs_0_, f32[72,128]{1,0:T(8,128)S(1)} %collective-permute-done.11.refs_1_, f32[72,128]{1,0:T(8,128)S(1)} %collective-permute-done.12.refs_2_, f32[72,128]{1,0:T(8,128)S(1)} %collective-permute-done.13.refs_3_, f32[64,128]{1,0:T(8,128)S(1)} %collective-permute-done.14.refs_4_), custom_call_target="tpu_custom_call" | custom-call | tf_op jit(solution)/shard_map/finish/pallas_call | solution.py:440
  (12 shorter events, 0.0 us)
Async XLA Ops:
  0.0 32.4 %collective-permute-start = (f32[2,32,12288]{2,1,0:T(8,128)}, f32[2,32,12288]{2,1,0:T(8,128)S(1)}, u32[]{:S(2)}, u32[]{:S(2)}) collective-permute-start(f32[2,32,12288]{2,1,0:T(8,128)} %legendre_ref.2), channel_id=1, source_target_pairs={{0,1},{1,0},{2,3},{3,2},{4,5},{5,4},{6,7},{7,6},{8,9},{9,8},{10,11... | collective-permute-start | bytes 9437192 | tf_op jit(solution)/shard_map/ppermute | solution.py:481
  0.1 32.7 %copy-start = (f32[3072,8,8]{0,2,1:T(8,128)S(1)}, f32[3072,8,8]{0,2,1:T(8,128)}, u32[]{:S(2)}) copy-start(f32[3072,8,8]{0,2,1:T(8,128)} %param.10) | copy-start | bytes 2359300
  0.1 32.7 %copy-start.1 = (s32[2]{0:T(128)S(1)}, s32[2]{0:T(128)}, u32[]{:S(2)}) copy-start(s32[2]{0:T(128)} %order_ref.1) | copy-start | bytes 28
  1.3 12.3 %collective-permute-start.4 = (f32[2,32,1536]{2,1,0:T(8,128)S(1)}, f32[2,32,1536]{2,1,0:T(8,128)S(1)}, u32[]{:S(2)}, u32[]{:S(2)}) collective-permute-start(f32[2,32,1536]{2,1,0:T(8,128)S(1)} %get-tuple-element.26), channel_id=1, source_target_pairs={{0,3},{1,2},{2,1},{3,0},{4,7},{5,6},{6,5},{7,4},{8,11},{9,10},{10,... | collective-permute-start | bytes 1179656 | tf_op jit(solution)/shard_map/ppermute | solution.py:481
  5.7 23.4 %collective-permute-start.10 = (f32[2,32,1408]{2,1,0:T(8,128)S(1)}, f32[2,32,1408]{2,1,0:T(8,128)S(1)}, u32[]{:S(2)}, u32[]{:S(2)}) collective-permute-start(f32[2,32,1408]{2,1,0:T(8,128)S(1)} %get-tuple-element.37), channel_id=1, source_target_pairs={{0,2},{1,3},{2,0},{3,1},{4,6},{5,7},{6,4},{7,5},{8,10},{9,11},{10,... | collective-permute-start | bytes 1081352 | tf_op jit(solution)/shard_map/ppermute | solution.py:481
  5.9 22.3 %collective-permute-start.9 = (f32[2,32,1280]{2,1,0:T(8,128)S(1)}, f32[2,32,1280]{2,1,0:T(8,128)S(1)}, u32[]{:S(2)}, u32[]{:S(2)}) collective-permute-start(f32[2,32,1280]{2,1,0:T(8,128)S(1)} %get-tuple-element.36), channel_id=1, source_target_pairs={{0,2},{1,3},{2,0},{3,1},{4,6},{5,7},{6,4},{7,5},{8,10},{9,11},{10,... | collective-permute-start | bytes 983048 | tf_op jit(solution)/shard_map/ppermute | solution.py:481
  7.2 29.1 %collective-permute-start.6 = (f32[2,32,1408]{2,1,0:T(8,128)S(1)}, f32[2,32,1408]{2,1,0:T(8,128)S(1)}, u32[]{:S(2)}, u32[]{:S(2)}) collective-permute-start(f32[2,32,1408]{2,1,0:T(8,128)S(1)} %get-tuple-element.32), channel_id=1, source_target_pairs={{0,3},{1,2},{2,1},{3,0},{4,7},{5,6},{6,5},{7,4},{8,11},{9,10},{10,... | collective-permute-start | bytes 1081352 | tf_op jit(solution)/shard_map/ppermute | solution.py:481
  13.6 1.2 %collective-permute-start.3 = (f32[2,32,128]{2,1,0:T(8,128)S(1)}, f32[2,32,128]{2,1,0:T(8,128)S(1)}, u32[]{:S(2)}, u32[]{:S(2)}) collective-permute-start(f32[2,32,128]{2,1,0:T(8,128)S(1)} %get-tuple-element.31.refs_0_), channel_id=1, source_target_pairs={{0,1},{1,0},{2,3},{3,2},{4,5},{5,4},{6,7},{7,6},{8,9},{9,8},{10,11... | collective-permute-start | bytes 98312 | tf_op jit(solution)/shard_map/ppermute | solution.py:481
  14.8 15.9 %collective-permute-start.5 = (f32[2,32,128]{2,1,0:T(8,128)S(1)}, f32[2,32,128]{2,1,0:T(8,128)S(1)}, u32[]{:S(2)}, u32[]{:S(2)}) collective-permute-start(f32[2,32,128]{2,1,0:T(8,128)S(1)} %slice.4), channel_id=1, source_target_pairs={{0,1},{1,0},{2,3},{3,2},{4,5},{5,4},{6,7},{7,6},{8,9},{9,8},{10,11... | collective-permute-start | bytes 98312 | tf_op jit(solution)/shard_map/ppermute | solution.py:481
  28.2 10.2 %collective-permute-start.7 = (f32[2,32,256]{2,1,0:T(8,128)S(1)}, f32[2,32,256]{2,1,0:T(8,128)S(1)}, u32[]{:S(2)}, u32[]{:S(2)}) collective-permute-start(f32[2,32,256]{2,1,0:T(8,128)S(1)} %get-tuple-element.34), channel_id=1, source_target_pairs={{0,2},{1,3},{2,0},{3,1},{4,6},{5,7},{6,4},{7,5},{8,10},{9,11},{10,... | collective-permute-start | bytes 196616 | tf_op jit(solution)/shard_map/ppermute | solution.py:481
  29.1 9.7 %collective-permute-start.8 = (f32[2,32,256]{2,1,0:T(8,128)S(1)}, f32[2,32,256]{2,1,0:T(8,128)S(1)}, u32[]{:S(2)}, u32[]{:S(2)}) collective-permute-start(f32[2,32,256]{2,1,0:T(8,128)S(1)} %get-tuple-element.35), channel_id=1, source_target_pairs={{0,3},{1,2},{2,1},{3,0},{4,7},{5,6},{6,5},{7,4},{8,11},{9,10},{10,... | collective-permute-start | bytes 196616 | tf_op jit(solution)/shard_map/ppermute | solution.py:481
  30.7 11.1 %collective-permute-start.1 = (f32[2,32,256]{2,1,0:T(8,128)S(1)}, f32[2,32,256]{2,1,0:T(8,128)S(1)}, u32[]{:S(2)}, u32[]{:S(2)}) collective-permute-start(f32[2,32,256]{2,1,0:T(8,128)S(1)} %get-tuple-element.29), channel_id=1, source_target_pairs={{0,2},{1,3},{2,0},{3,1},{4,6},{5,7},{6,4},{7,5},{8,10},{9,11},{10,... | collective-permute-start | bytes 196616 | tf_op jit(solution)/shard_map/ppermute | solution.py:481
  32.4 9.4 %collective-permute-start.2 = (f32[2,32,256]{2,1,0:T(8,128)S(1)}, f32[2,32,256]{2,1,0:T(8,128)S(1)}, u32[]{:S(2)}, u32[]{:S(2)}) collective-permute-start(f32[2,32,256]{2,1,0:T(8,128)S(1)} %get-tuple-element.30), channel_id=1, source_target_pairs={{0,3},{1,2},{2,1},{3,0},{4,7},{5,6},{6,5},{7,4},{8,11},{9,10},{10,... | collective-permute-start | bytes 196616 | tf_op jit(solution)/shard_map/ppermute | solution.py:481
  39.5 4.2 %collective-permute-start.11 = (f32[72,128]{1,0:T(8,128)S(1)}, f32[72,128]{1,0:T(8,128)S(1)}, u32[]{:S(2)}, u32[]{:S(2)}) collective-permute-start(f32[72,128]{1,0:T(8,128)S(1)} %get-tuple-element.41), channel_id=1, source_target_pairs={{0,2},{1,3},{2,0},{3,1},{4,6},{5,7},{6,4},{7,5},{8,10},{9,11},{10,... | collective-permute-start | bytes 110600 | tf_op jit(solution)/shard_map/ppermute | solution.py:481
  41.3 3.4 %collective-permute-start.12 = (f32[72,128]{1,0:T(8,128)S(1)}, f32[72,128]{1,0:T(8,128)S(1)}, u32[]{:S(2)}, u32[]{:S(2)}) collective-permute-start(f32[72,128]{1,0:T(8,128)S(1)} %get-tuple-element.42), channel_id=1, source_target_pairs={{0,3},{1,2},{2,1},{3,0},{4,7},{5,6},{6,5},{7,4},{8,11},{9,10},{10,... | collective-permute-start | bytes 110600 | tf_op jit(solution)/shard_map/ppermute | solution.py:481
  41.5 3.2 %collective-permute-start.13 = (f32[72,128]{1,0:T(8,128)S(1)}, f32[72,128]{1,0:T(8,128)S(1)}, u32[]{:S(2)}, u32[]{:S(2)}) collective-permute-start(f32[72,128]{1,0:T(8,128)S(1)} %get-tuple-element.43), channel_id=1, source_target_pairs={{0,1},{1,0},{2,3},{3,2},{4,5},{5,4},{6,7},{7,6},{8,9},{9,8},{10,11... | collective-permute-start | bytes 110600 | tf_op jit(solution)/shard_map/ppermute | solution.py:481
  42.4 1.3 %collective-permute-start.14 = (f32[64,128]{1,0:T(8,128)S(1)}, f32[64,128]{1,0:T(8,128)S(1)}, u32[]{:S(2)}, u32[]{:S(2)}) collective-permute-start(f32[64,128]{1,0:T(8,128)S(1)} %get-tuple-element.44), channel_id=1, source_target_pairs={{0,1},{1,0},{2,3},{3,2},{4,5},{5,4},{6,7},{7,6},{8,9},{9,8},{10,11... | collective-permute-start | bytes 98312 | tf_op jit(solution)/shard_map/ppermute | solution.py:481

commit v6 on v5

--- a/solution.py
+++ b/solution.py
@@ -247,16 +247,23 @@
     )(*[array for array, _ in pieces])
 
 
-def tile_sum(values, analysis, weights, keep, rows):
+def tile_sum(values, analysis, weights, keep, rows, stacked):
     scales, channels = len(weights), len(weights[0])
     columns = analysis.shape[0]
     skies = columns // (2 * channels)
     high, low = halves(values)
-    harmonics = jnp.dot(
-        analysis,
-        jnp.concatenate([high, high, low], axis=0),
-        preferred_element_type=jnp.float32,
-    )
+    cycles = high.shape[0]
+    if stacked:
+        terms = jnp.concatenate([analysis[:, :cycles], analysis[:, cycles : 2 * cycles]], axis=0)
+        both = jnp.dot(terms, high, preferred_element_type=jnp.float32)
+        rest = jnp.dot(analysis[:, :cycles], low, preferred_element_type=jnp.float32)
+        harmonics = (rest + both[columns:]) + both[:columns]
+    else:
+        harmonics = jnp.dot(
+            analysis,
+            jnp.concatenate([high, high, low], axis=0),
+            preferred_element_type=jnp.float32,
+        )
     harmonics = jnp.where(keep, harmonics, 0.0)
     matched = []
     for p in range(2):
@@ -314,7 +321,7 @@
                 axis=0,
             )
             keep = degree >= limits_ref[k : k + 1, :1]
-            product = tile_sum(values, analysis_ref[k], weights, keep, n * rows)
+            product = tile_sum(values, analysis_ref[k], weights, keep, n * rows, not last)
             totals[k] = product if totals[k] is None else totals[k] + product
         at += tile
 
@@ -401,7 +408,7 @@
         beside = jnp.concatenate([near[k, :, pl.ds(place, size)] for place in places], axis=1)
         values = jnp.concatenate([home[k], beside] + [other[k] for other in others], axis=0)
         keep = degree >= limits_ref[k : k + 1, :1]
-        result = fold(tile_sum(values, analysis_ref[k], weights, keep, 2 * rows))
+        result = fold(tile_sum(values, analysis_ref[k], weights, keep, 2 * rows, False))
         own_out[k * rows : (k + 1) * rows, :] += result[:rows]
         near_out[k * rows : (k + 1) * rows, :] = result[rows:]
 

time: 45.5 us -> 45.5 us (level)
  waiting for transfers between devices: 22.1 us -> 22.7 us
  Pallas kernels: 10.4 us -> 9.87 us
    ppermute x15, waiting for transfers between devices: 22.1 us -> 22.7 us  [send(): return lax.ppermute(value, 'blk', partner(x, n))]
    pallas_call x3, Pallas kernels: 5.21 us -> 4.65 us  [chunk(): pl.pallas_call(functools.partial(chunk_kernel, n, first, last, blocks, of...]
  transfers between devices with their start and end apart: 15 -> 15, of which waited for: 6 -> 7; matrix products, arithmetic and copies ran while one was open for 0% -> 0% of each run, Pallas kernels for 22% -> 20%
where the time goes in v6:
time: 45.5 us; the launch traced here: 45.4 us
  waiting for transfers between devices  22.7 us (50%)
  starting transfers between devices  12.7 us (28%)
  Pallas kernels  9.87 us (22%)
    ppermute x15, waiting for transfers between devices, send(): return lax.ppermute(value, 'blk', partner(x, n))  22.7 us
    ppermute x15, starting transfers between devices, send(): return lax.ppermute(value, 'blk', partner(x, n))  12.7 us
    pallas_call x3, Pallas kernels, chunk(): pl.pallas_call(functools.partial(chunk_kernel, n, first, last, blocks, of...  4.65 us
    pallas_call x1, Pallas kernels, cut(): pl.pallas_call(functools.partial(cut_kernel, pieces, blocks, carry, endin...  1.8 us
    pallas_call x1, Pallas kernels, open_blocks(): pl.pallas_call(functools.partial(open_kernel, pieces, carry, blocks), out...  1.18 us
    pallas_call x1, Pallas kernels, response_rows(): pl.pallas_call(functools.partial(response_kernel, blocks, scales, skies),...  0.93 us
  transfers between devices with their start and end apart: 15, of which 7 were waited for; matrix products, arithmetic and copies ran while one was open for 0% of the time, Pallas kernels for 20%

profile of v6, /device:TPU:1, one launch (start us, length us, event | category | flops | bytes accessed | tf_op | source)
XLA Modules:
  0.0 45.4 jit_solution(14190504858461552438)
XLA Ops:
  0.0 0.1 collective-permute-start
  0.1 1.2 %open.1 = (f32[2,32,1536]{2,1,0:T(8,128)S(1)}, f32[2,32,128]{2,1,0:T(8,128)S(1)}) custom-call(f32[2,32,12288]{2,1,0:T(8,128)} %legendre_ref.2, f32[2,32,128]{2,1,0:T(8,128)} %cycles_ref.1, f32[1,32]{1,0:T(1,128)} %bitcast.8, s32[2,64]{1,0:T(2,128)} %hits_ref.1, f32[2,64,128]{2,1,0:T(8,128)} %flux_ref.1), custom_call_target="tpu_custom_call" | custom-call | tf_op jit(solution)/shard_map/open/pallas_call | solution.py:159
  1.3 2.6 %collective-permute-start.4 = (f32[2,32,1536]{2,1,0:T(8,128)S(1)}, f32[2,32,1536]{2,1,0:T(8,128)S(1)}, u32[]{:S(2)}, u32[]{:S(2)}) collective-permute-start(f32[2,32,1536]{2,1,0:T(8,128)S(1)} %get-tuple-element.26), channel_id=1, source_target_pairs={{0,3},{1,2},{2,1},{3,0},{4,7},{5,6},{6,5},{7,4},{8,11},{9,10},{10,... | collective-permute-start | bytes 1179656 | tf_op jit(solution)/shard_map/ppermute | solution.py:488
  3.9 1.8 %cut.1 = (f32[2,32,1408]{2,1,0:T(8,128)S(1)}, f32[2,32,1408]{2,1,0:T(8,128)S(1)}, f32[2,32,1280]{2,1,0:T(8,128)S(1)}, f32[2,32,256]{2,1,0:T(8,128)S(1)}, f32[2,3...) custom-call(f32[2,32,12288]{2,1,0:T(8,128)} %legendre_ref.2, ...), custom_call_target="tpu_custom_call" | custom-call | bytes 85196800 | tf_op jit(solution)/shard_map/cut/pallas_call | solution.py:89
  5.7 0.2 collective-permute-start.10
  5.9 1.3 %collective-permute-start.9 = (f32[2,32,1280]{2,1,0:T(8,128)S(1)}, f32[2,32,1280]{2,1,0:T(8,128)S(1)}, u32[]{:S(2)}, u32[]{:S(2)}) collective-permute-start(f32[2,32,1280]{2,1,0:T(8,128)S(1)} %get-tuple-element.36), channel_id=1, source_target_pairs={{0,2},{1,3},{2,0},{3,1},{4,6},{5,7},{6,4},{7,5},{8,10},{9,11},{10,... | collective-permute-start | bytes 983048 | tf_op jit(solution)/shard_map/ppermute | solution.py:488
  7.2 0.7 %collective-permute-start.6 = (f32[2,32,1408]{2,1,0:T(8,128)S(1)}, f32[2,32,1408]{2,1,0:T(8,128)S(1)}, u32[]{:S(2)}, u32[]{:S(2)}) collective-permute-start(f32[2,32,1408]{2,1,0:T(8,128)S(1)} %get-tuple-element.32), channel_id=1, source_target_pairs={{0,3},{1,2},{2,1},{3,0},{4,7},{5,6},{6,5},{7,4},{8,11},{9,10},{10,... | collective-permute-start | bytes 1081352 | tf_op jit(solution)/shard_map/ppermute | solution.py:488
  8.0 5.6 %collective-permute-done.4.refs_3_ = f32[2,32,1536]{2,1,0:T(8,128)S(1)} collective-permute-done((f32[2,32,1536]{2,1,0:T(8,128)S(1)}, f32[2,32,1536]{2,1,0:T(8,128)S(1)}, u32[]{:S(2)}, u32[]{:S(2)}) %collective-permute-start.4) | collective-permute-done | bytes 393248 | tf_op jit(solution)/shard_map/ppermute | solution.py:488
  13.6 0.3 collective-permute-start.3
  13.9 0.9 %collective-permute-done.3.refs_1_ = f32[2,32,128]{2,1,0:T(8,128)S(1)} collective-permute-done((f32[2,32,128]{2,1,0:T(8,128)S(1)}, f32[2,32,128]{2,1,0:T(8,128)S(1)}, u32[]{:S(2)}, u32[]{:S(2)}) %collective-permute-start.3) | collective-permute-done | bytes 32800 | tf_op jit(solution)/shard_map/ppermute | solution.py:488
  14.8 0.3 collective-permute-start.5
  15.1 13.1 %collective-permute-done.9.refs_2_ = f32[2,32,1280]{2,1,0:T(8,128)S(1)} collective-permute-done((f32[2,32,1280]{2,1,0:T(8,128)S(1)}, f32[2,32,1280]{2,1,0:T(8,128)S(1)}, u32[]{:S(2)}, u32[]{:S(2)}) %collective-permute-start.9) | collective-permute-done | bytes 327712 | tf_op jit(solution)/shard_map/ppermute | solution.py:488
  28.2 0.9 %collective-permute-start.7 = (f32[2,32,256]{2,1,0:T(8,128)S(1)}, f32[2,32,256]{2,1,0:T(8,128)S(1)}, u32[]{:S(2)}, u32[]{:S(2)}) collective-permute-start(f32[2,32,256]{2,1,0:T(8,128)S(1)} %get-tuple-element.34), channel_id=1, source_target_pairs={{0,2},{1,3},{2,0},{3,1},{4,6},{5,7},{6,4},{7,5},{8,10},{9,11},{10,... | collective-permute-start | bytes 196616 | tf_op jit(solution)/shard_map/ppermute | solution.py:488
  29.1 0.0 collective-permute-done.10.refs_2_
  29.1 1.6 %collective-permute-start.8 = (f32[2,32,256]{2,1,0:T(8,128)S(1)}, f32[2,32,256]{2,1,0:T(8,128)S(1)}, u32[]{:S(2)}, u32[]{:S(2)}) collective-permute-start(f32[2,32,256]{2,1,0:T(8,128)S(1)} %get-tuple-element.35), channel_id=1, source_target_pairs={{0,3},{1,2},{2,1},{3,0},{4,7},{5,6},{6,5},{7,4},{8,11},{9,10},{10,... | collective-permute-start | bytes 196616 | tf_op jit(solution)/shard_map/ppermute | solution.py:488
  30.7 1.7 %collective-permute-start.1 = (f32[2,32,256]{2,1,0:T(8,128)S(1)}, f32[2,32,256]{2,1,0:T(8,128)S(1)}, u32[]{:S(2)}, u32[]{:S(2)}) collective-permute-start(f32[2,32,256]{2,1,0:T(8,128)S(1)} %get-tuple-element.29), channel_id=1, source_target_pairs={{0,2},{1,3},{2,0},{3,1},{4,6},{5,7},{6,4},{7,5},{8,10},{9,11},{10,... | collective-permute-start | bytes 196616 | tf_op jit(solution)/shard_map/ppermute | solution.py:488
  32.4 0.3 collective-permute-start.2
  32.8 0.9 %response.1 = (f32[8,128]{1,0:T(8,128)S(1)}, s32[8,128]{1,0:T(8,128)S(1)}) custom-call(s32[2]{0:T(128)S(1)} %copy-done.1, f32[8,8,3072]{2,1,0:T(8,128)S(1)} %bitcast.3), custom_call_target="tpu_custom_call" | custom-call | tf_op jit(solution)/shard_map/response/pallas_call | solution.py:210
  33.7 0.1 prepare.1.refs_4_
  33.8 2.1 %chunk.3.refs_6_ = f32[2,128,128]{2,1,0:T(8,128)S(1)} custom-call(s32[8,128]{1,0:T(8,128)S(1)} %get-tuple-element.25.limits_ref, f32[2,32,3072]{2,1,0:T(8,128)S(1)} %get-tuple-element.33.refs_0_, f32[2,32,12288]{2,1,0:T(8,128)S(1)} %collective-permute-done.refs_1_, f32[2,32,1408]{2,1,0:T(8,128)S(1)} %collective-permute-done.10.refs_2_, ...), custom_call_target="tpu_custom_call" | custom-call | tf_op jit(solution)/shard_map/chunk/pallas_call | solution.py:360
  35.9 0.1 collective-permute-done.6.refs_3_.refs_6_
  36.0 2.0 %chunk.4.refs_6_ = f32[2,128,128]{2,1,0:T(8,128)S(1)} custom-call(s32[8,128]{1,0:T(8,128)S(1)} %get-tuple-element.25.limits_ref, f32[2,32,3072]{2,1,0:T(8,128)S(1)} %get-tuple-element.33.refs_0_, f32[2,32,12288]{2,1,0:T(8,128)S(1)} %collective-permute-done.refs_1_, f32[2,32,1280]{2,1,0:T(8,128)S(1)} %collective-permute-done.9.refs_2_, ...), custom_call_target="tpu_custom_call" | custom-call | tf_op jit(solution)/shard_map/chunk/pallas_call | solution.py:360
  38.0 0.8 %collective-permute-done.8.refs_3_ = f32[2,32,256]{2,1,0:T(8,128)S(1)} collective-permute-done((f32[2,32,256]{2,1,0:T(8,128)S(1)}, f32[2,32,256]{2,1,0:T(8,128)S(1)}, u32[]{:S(2)}, u32[]{:S(2)}) %collective-permute-start.8) | collective-permute-done | bytes 65568 | tf_op jit(solution)/shard_map/ppermute | solution.py:488
  38.9 0.6 %chunk.5 = (f32[72,128]{1,0:T(8,128)S(1)}, f32[72,128]{1,0:T(8,128)S(1)}, f32[72,128]{1,0:T(8,128)S(1)}, f32[72,128]{1,0:T(8,128)S(1)}) custom-call(s32[8,128]{1,0:T(8,128)S(1)} %get-tuple-element.25.limits_ref, f32[2,32,3072]{2,1,0:T(8,128)S(1)} %get-tuple-element.33.refs_0_, f32[2,32,12288]{2,1,0:T(8,128)S(1)} %collective-permute-done.refs_1_, ...), custom_call_target="tpu_custom_call" | custom-call | tf_op jit(solution)/shard_map/chunk/pallas_call | solution.py:360
  39.5 1.9 %collective-permute-start.11 = (f32[72,128]{1,0:T(8,128)S(1)}, f32[72,128]{1,0:T(8,128)S(1)}, u32[]{:S(2)}, u32[]{:S(2)}) collective-permute-start(f32[72,128]{1,0:T(8,128)S(1)} %get-tuple-element.41), channel_id=1, source_target_pairs={{0,2},{1,3},{2,0},{3,1},{4,6},{5,7},{6,4},{7,5},{8,10},{9,11},{10,... | collective-permute-start | bytes 110600 | tf_op jit(solution)/shard_map/ppermute | solution.py:488
  41.3 0.1 collective-permute-start.12
  41.5 0.3 collective-permute-start.13
  41.8 0.6 %ends.1 = (f32[72,128]{1,0:T(8,128)S(1)}, f32[64,128]{1,0:T(8,128)S(1)}) custom-call(s32[8,128]{1,0:T(8,128)S(1)} %get-tuple-element.25.limits_ref, f32[2,32,256]{2,1,0:T(8,128)S(1)} %get-tuple-element.28.refs_0_, f32[2,32,12288]{2,1,0:T(8,128)S(1)} %collective-permute-done.refs_1_, f32[2,32,256]{2,1,0:T(8,128)S(1)} %collective-permute-done.1.refs_2_, ...), custom_call_target="tpu_custom_call" | custom-call | tf_op jit(solution)/shard_map/ends/pallas_call | solution.py:421
  42.4 0.2 collective-permute-start.14
  42.6 1.0 %collective-permute-done.14.refs_4_ = f32[64,128]{1,0:T(8,128)S(1)} collective-permute-done((f32[64,128]{1,0:T(8,128)S(1)}, f32[64,128]{1,0:T(8,128)S(1)}, u32[]{:S(2)}, u32[]{:S(2)}) %collective-permute-start.14) | collective-permute-done | bytes 32800 | tf_op jit(solution)/shard_map/ppermute | solution.py:488
  43.7 1.0 %collective-permute-done.12.refs_2_ = f32[72,128]{1,0:T(8,128)S(1)} collective-permute-done((f32[72,128]{1,0:T(8,128)S(1)}, f32[72,128]{1,0:T(8,128)S(1)}, u32[]{:S(2)}, u32[]{:S(2)}) %collective-permute-start.12) | collective-permute-done | bytes 36896 | tf_op jit(solution)/shard_map/ppermute | solution.py:488
  44.7 0.6 %finish.1 = f32[2,32,128]{2,1,0:T(8,128)} custom-call(f32[72,128]{1,0:T(8,128)S(1)} %get-tuple-element.40.refs_0_, f32[72,128]{1,0:T(8,128)S(1)} %collective-permute-done.11.refs_1_, f32[72,128]{1,0:T(8,128)S(1)} %collective-permute-done.12.refs_2_, f32[72,128]{1,0:T(8,128)S(1)} %collective-permute-done.13.refs_3_, f32[64,128]{1,0:T(8,128)S(1)} %collective-permute-done.14.refs_4_), custom_call_target="tpu_custom_call" | custom-call | tf_op jit(solution)/shard_map/finish/pallas_call | solution.py:447
  (12 shorter events, 0.0 us)
Async XLA Ops:
  0.0 32.4 %collective-permute-start = (f32[2,32,12288]{2,1,0:T(8,128)}, f32[2,32,12288]{2,1,0:T(8,128)S(1)}, u32[]{:S(2)}, u32[]{:S(2)}) collective-permute-start(f32[2,32,12288]{2,1,0:T(8,128)} %legendre_ref.2), channel_id=1, source_target_pairs={{0,1},{1,0},{2,3},{3,2},{4,5},{5,4},{6,7},{7,6},{8,9},{9,8},{10,11... | collective-permute-start | bytes 9437192 | tf_op jit(solution)/shard_map/ppermute | solution.py:488
  0.1 32.7 %copy-start = (f32[3072,8,8]{0,2,1:T(8,128)S(1)}, f32[3072,8,8]{0,2,1:T(8,128)}, u32[]{:S(2)}) copy-start(f32[3072,8,8]{0,2,1:T(8,128)} %param.10) | copy-start | bytes 2359300
  0.1 32.7 %copy-start.1 = (s32[2]{0:T(128)S(1)}, s32[2]{0:T(128)}, u32[]{:S(2)}) copy-start(s32[2]{0:T(128)} %order_ref.1) | copy-start | bytes 28
  1.3 12.3 %collective-permute-start.4 = (f32[2,32,1536]{2,1,0:T(8,128)S(1)}, f32[2,32,1536]{2,1,0:T(8,128)S(1)}, u32[]{:S(2)}, u32[]{:S(2)}) collective-permute-start(f32[2,32,1536]{2,1,0:T(8,128)S(1)} %get-tuple-element.26), channel_id=1, source_target_pairs={{0,3},{1,2},{2,1},{3,0},{4,7},{5,6},{6,5},{7,4},{8,11},{9,10},{10,... | collective-permute-start | bytes 1179656 | tf_op jit(solution)/shard_map/ppermute | solution.py:488
  5.7 23.4 %collective-permute-start.10 = (f32[2,32,1408]{2,1,0:T(8,128)S(1)}, f32[2,32,1408]{2,1,0:T(8,128)S(1)}, u32[]{:S(2)}, u32[]{:S(2)}) collective-permute-start(f32[2,32,1408]{2,1,0:T(8,128)S(1)} %get-tuple-element.37), channel_id=1, source_target_pairs={{0,2},{1,3},{2,0},{3,1},{4,6},{5,7},{6,4},{7,5},{8,10},{9,11},{10,... | collective-permute-start | bytes 1081352 | tf_op jit(solution)/shard_map/ppermute | solution.py:488
  5.9 22.3 %collective-permute-start.9 = (f32[2,32,1280]{2,1,0:T(8,128)S(1)}, f32[2,32,1280]{2,1,0:T(8,128)S(1)}, u32[]{:S(2)}, u32[]{:S(2)}) collective-permute-start(f32[2,32,1280]{2,1,0:T(8,128)S(1)} %get-tuple-element.36), channel_id=1, source_target_pairs={{0,2},{1,3},{2,0},{3,1},{4,6},{5,7},{6,4},{7,5},{8,10},{9,11},{10,... | collective-permute-start | bytes 983048 | tf_op jit(solution)/shard_map/ppermute | solution.py:488
  7.2 28.8 %collective-permute-start.6 = (f32[2,32,1408]{2,1,0:T(8,128)S(1)}, f32[2,32,1408]{2,1,0:T(8,128)S(1)}, u32[]{:S(2)}, u32[]{:S(2)}) collective-permute-start(f32[2,32,1408]{2,1,0:T(8,128)S(1)} %get-tuple-element.32), channel_id=1, source_target_pairs={{0,3},{1,2},{2,1},{3,0},{4,7},{5,6},{6,5},{7,4},{8,11},{9,10},{10,... | collective-permute-start | bytes 1081352 | tf_op jit(solution)/shard_map/ppermute | solution.py:488
  13.6 1.2 %collective-permute-start.3 = (f32[2,32,128]{2,1,0:T(8,128)S(1)}, f32[2,32,128]{2,1,0:T(8,128)S(1)}, u32[]{:S(2)}, u32[]{:S(2)}) collective-permute-start(f32[2,32,128]{2,1,0:T(8,128)S(1)} %get-tuple-element.31.refs_0_), channel_id=1, source_target_pairs={{0,1},{1,0},{2,3},{3,2},{4,5},{5,4},{6,7},{7,6},{8,9},{9,8},{10,11... | collective-permute-start | bytes 98312 | tf_op jit(solution)/shard_map/ppermute | solution.py:488
  14.8 15.9 %collective-permute-start.5 = (f32[2,32,128]{2,1,0:T(8,128)S(1)}, f32[2,32,128]{2,1,0:T(8,128)S(1)}, u32[]{:S(2)}, u32[]{:S(2)}) collective-permute-start(f32[2,32,128]{2,1,0:T(8,128)S(1)} %slice.4), channel_id=1, source_target_pairs={{0,1},{1,0},{2,3},{3,2},{4,5},{5,4},{6,7},{7,6},{8,9},{9,8},{10,11... | collective-permute-start | bytes 98312 | tf_op jit(solution)/shard_map/ppermute | solution.py:488
  28.2 9.8 %collective-permute-start.7 = (f32[2,32,256]{2,1,0:T(8,128)S(1)}, f32[2,32,256]{2,1,0:T(8,128)S(1)}, u32[]{:S(2)}, u32[]{:S(2)}) collective-permute-start(f32[2,32,256]{2,1,0:T(8,128)S(1)} %get-tuple-element.34), channel_id=1, source_target_pairs={{0,2},{1,3},{2,0},{3,1},{4,6},{5,7},{6,4},{7,5},{8,10},{9,11},{10,... | collective-permute-start | bytes 196616 | tf_op jit(solution)/shard_map/ppermute | solution.py:488
  29.1 9.7 %collective-permute-start.8 = (f32[2,32,256]{2,1,0:T(8,128)S(1)}, f32[2,32,256]{2,1,0:T(8,128)S(1)}, u32[]{:S(2)}, u32[]{:S(2)}) collective-permute-start(f32[2,32,256]{2,1,0:T(8,128)S(1)} %get-tuple-element.35), channel_id=1, source_target_pairs={{0,3},{1,2},{2,1},{3,0},{4,7},{5,6},{6,5},{7,4},{8,11},{9,10},{10,... | collective-permute-start | bytes 196616 | tf_op jit(solution)/shard_map/ppermute | solution.py:488
  30.7 11.1 %collective-permute-start.1 = (f32[2,32,256]{2,1,0:T(8,128)S(1)}, f32[2,32,256]{2,1,0:T(8,128)S(1)}, u32[]{:S(2)}, u32[]{:S(2)}) collective-permute-start(f32[2,32,256]{2,1,0:T(8,128)S(1)} %get-tuple-element.29), channel_id=1, source_target_pairs={{0,2},{1,3},{2,0},{3,1},{4,6},{5,7},{6,4},{7,5},{8,10},{9,11},{10,... | collective-permute-start | bytes 196616 | tf_op jit(solution)/shard_map/ppermute | solution.py:488
  32.4 9.4 %collective-permute-start.2 = (f32[2,32,256]{2,1,0:T(8,128)S(1)}, f32[2,32,256]{2,1,0:T(8,128)S(1)}, u32[]{:S(2)}, u32[]{:S(2)}) collective-permute-start(f32[2,32,256]{2,1,0:T(8,128)S(1)} %get-tuple-element.30), channel_id=1, source_target_pairs={{0,3},{1,2},{2,1},{3,0},{4,7},{5,6},{6,5},{7,4},{8,11},{9,10},{10,... | collective-permute-start | bytes 196616 | tf_op jit(solution)/shard_map/ppermute | solution.py:488
  39.5 4.2 %collective-permute-start.11 = (f32[72,128]{1,0:T(8,128)S(1)}, f32[72,128]{1,0:T(8,128)S(1)}, u32[]{:S(2)}, u32[]{:S(2)}) collective-permute-start(f32[72,128]{1,0:T(8,128)S(1)} %get-tuple-element.41), channel_id=1, source_target_pairs={{0,2},{1,3},{2,0},{3,1},{4,6},{5,7},{6,4},{7,5},{8,10},{9,11},{10,... | collective-permute-start | bytes 110600 | tf_op jit(solution)/shard_map/ppermute | solution.py:488
  41.3 3.4 %collective-permute-start.12 = (f32[72,128]{1,0:T(8,128)S(1)}, f32[72,128]{1,0:T(8,128)S(1)}, u32[]{:S(2)}, u32[]{:S(2)}) collective-permute-start(f32[72,128]{1,0:T(8,128)S(1)} %get-tuple-element.42), channel_id=1, source_target_pairs={{0,3},{1,2},{2,1},{3,0},{4,7},{5,6},{6,5},{7,4},{8,11},{9,10},{10,... | collective-permute-start | bytes 110600 | tf_op jit(solution)/shard_map/ppermute | solution.py:488
  41.5 3.2 %collective-permute-start.13 = (f32[72,128]{1,0:T(8,128)S(1)}, f32[72,128]{1,0:T(8,128)S(1)}, u32[]{:S(2)}, u32[]{:S(2)}) collective-permute-start(f32[72,128]{1,0:T(8,128)S(1)} %get-tuple-element.43), channel_id=1, source_target_pairs={{0,1},{1,0},{2,3},{3,2},{4,5},{5,4},{6,7},{7,6},{8,9},{9,8},{10,11... | collective-permute-start | bytes 110600 | tf_op jit(solution)/shard_map/ppermute | solution.py:488
  42.4 1.3 %collective-permute-start.14 = (f32[64,128]{1,0:T(8,128)S(1)}, f32[64,128]{1,0:T(8,128)S(1)}, u32[]{:S(2)}, u32[]{:S(2)}) collective-permute-start(f32[64,128]{1,0:T(8,128)S(1)} %get-tuple-element.44), channel_id=1, source_target_pairs={{0,1},{1,0},{2,3},{3,2},{4,5},{5,4},{6,7},{7,6},{8,9},{9,8},{10,11... | collective-permute-start | bytes 98312 | tf_op jit(solution)/shard_map/ppermute | solution.py:488

commit v7 on v5

--- a/solution.py
+++ b/solution.py
@@ -269,7 +269,7 @@
             matched.append(value)
     matched_high, matched_low = halves(jnp.concatenate(matched, axis=0))
     return lax.dot_general(
-        jnp.concatenate([high[:rows], low[:rows]], axis=0),
+        jnp.concatenate([high[rows], low[rows]], axis=0),
         jnp.concatenate([matched_high, matched_low], axis=0),
         (((1,), (1,)), ((), ())),
         preferred_element_type=jnp.float32,
@@ -283,7 +283,7 @@
     ) + total[:rows, :columns]
 
 
-def chunk_kernel(n, first, last, blocks, offset, starts, tiles, limits_ref, *refs):
+def chunk_kernel(n, first, last, skip, blocks, offset, starts, tiles, limits_ref, *refs):
     legendre = refs[:n]
     analysis_ref, weights_ref = refs[n : n + 2]
     rest = list(refs[n + 2 :])
@@ -314,14 +314,16 @@
                 axis=0,
             )
             keep = degree >= limits_ref[k : k + 1, :1]
-            product = tile_sum(values, analysis_ref[k], weights, keep, n * rows)
+            product = tile_sum(values, analysis_ref[k], weights, keep, slice(skip * rows, n * rows))
             totals[k] = product if totals[k] is None else totals[k] + product
         at += tile
 
     for k in range(orders):
         result = fold(totals[k])
         if before is not None:
-            result = result + before[k]
+            result = result + before[k, skip * rows :]
+        if skip:
+            result = jnp.concatenate([before[k, : skip * rows], result], axis=0)
         if last:
             for x in range(n):
                 rest[x][k * rows : (k + 1) * rows, :] = result[x * rows : (x + 1) * rows, :]
@@ -332,7 +334,7 @@
             rest[x][orders * rows :, :] = response[...]
 
 
-def chunk(limits, parts, analysis, weights, before, response, blocks, offset, width):
+def chunk(limits, parts, analysis, weights, before, response, blocks, offset, width, skip):
     n = len(parts)
     orders, rows, _ = parts[0][0].shape
     columns = analysis.shape[1]
@@ -356,6 +358,7 @@
             n,
             first,
             last,
+            skip,
             blocks,
             offset,
             [start for _, start in parts],
@@ -370,7 +373,8 @@
     )(limits, *operands)
 
 
-def ends_kernel(n, across, blocks, at, limits_ref, *refs):
+def ends_kernel(n, across, blocks, at, offset, width, starts, limits_ref, *refs):
+    last, refs = refs[:n], refs[n:]
     home, near, *others = refs[:n]
     analysis_ref, weights_ref, across_ref, own_in, own_out, near_out = refs[n:]
     orders, rows, both = home.shape
@@ -396,23 +400,37 @@
         ]
         for s in range(scales)
     ]
+    last_degree = offset + lax.broadcasted_iota(jnp.int32, (1, width), 1)
+    last_weights = [
+        [weights_ref[s, f : f + 1, offset : offset + width] for f in range(channels)]
+        for s in range(scales)
+    ]
+    begins = [pl.multiple_of(me * blocks + offset, LANES) if b is None else b for b in starts]
     own_out[...] = own_in[...]
     for k in range(orders):
         beside = jnp.concatenate([near[k, :, pl.ds(place, size)] for place in places], axis=1)
         values = jnp.concatenate([home[k], beside] + [other[k] for other in others], axis=0)
         keep = degree >= limits_ref[k : k + 1, :1]
-        result = fold(tile_sum(values, analysis_ref[k], weights, keep, 2 * rows))
+        total = tile_sum(values, analysis_ref[k], weights, keep, slice(0, 2 * rows))
+        values = jnp.concatenate(
+            [block[k, :, pl.ds(begin, width)] for block, begin in zip(last, begins)], axis=0
+        )
+        keep = last_degree >= limits_ref[k : k + 1, :1]
+        total += tile_sum(values, analysis_ref[k], last_weights, keep, slice(0, 2 * rows))
+        result = fold(total)
         own_out[k * rows : (k + 1) * rows, :] += result[:rows]
         near_out[k * rows : (k + 1) * rows, :] = result[rows:]
 
 
-def ends(limits, parts, analysis, weights, across_weights, at, own, across, blocks):
+def ends(limits, last, parts, analysis, weights, across_weights, at, own, across, blocks, offset, width):
     n = len(parts)
     orders, rows, _ = parts[0].shape
     vmem = pl.BlockSpec(memory_space=pltpu.VMEM)
-    operands = parts + [analysis, weights, across_weights, own]
-    return pl.pallas_call(
-        functools.partial(ends_kernel, n, across, blocks, at),
+    operands = [array for array, _ in last] + parts + [analysis, weights, across_weights, own]
+    return pl.pallas_call(
+        functools.partial(
+            ends_kernel, n, across, blocks, at, offset, width, [start for _, start in last]
+        ),
         out_shape=[
             jax.ShapeDtypeStruct(own.shape, own.dtype),
             jax.ShapeDtypeStruct((orders * rows, own.shape[1]), own.dtype),
@@ -533,6 +551,7 @@
             blocks,
             offset,
             width,
+            2 if final and ending else 0,
         )
         total = result[0]
     returned = [send(result[x], x) for x in far + [1]]
@@ -541,6 +560,7 @@
         last_parts[1] = near
         own, beside = ends(
             limits,
+            [sent[-1][x] for x in range(n)],
             [last_parts[x] for x in range(n)],
             analysis,
             weights,
@@ -549,6 +569,8 @@
             own,
             across,
             blocks,
+            offsets[-1],
+            widths[-1],
         )
         returned.append(send(beside, 1))
     return finish([own] + returned, fourier_cycles.shape, float(legendre.shape[2]))

time: 45.5 us -> 45.5 us (level)
  Pallas kernels: 10.4 us -> 10.9 us
  waiting for transfers between devices: 22.1 us -> 21.6 us
    ppermute x15, waiting for transfers between devices: 22.1 us -> 21.6 us  [send(): return lax.ppermute(value, 'blk', partner(x, n))]
    pallas_call x4, Pallas kernels: 5.78 us -> 6.27 us  [the longest x3 5.18 us: chunk(): pl.pallas_call(functools.partial(chunk_kernel, n, first, last, skip, bloc...]
  transfers between devices with their start and end apart: 15 -> 15, of which waited for: 6 -> 6; matrix products, arithmetic and copies ran while one was open for 0% -> 0% of each run, Pallas kernels for 22% -> 23%
where the time goes in v7:
time: 45.5 us; the launch traced here: 45.3 us
  waiting for transfers between devices  21.6 us (47%)
  starting transfers between devices  12.8 us (28%)
  Pallas kernels  10.9 us (24%)
    ppermute x15, waiting for transfers between devices, send(): return lax.ppermute(value, 'blk', partner(x, n))  21.6 us
    ppermute x15, starting transfers between devices, send(): return lax.ppermute(value, 'blk', partner(x, n))  12.8 us
    pallas_call x3, Pallas kernels, chunk(): pl.pallas_call(functools.partial(chunk_kernel, n, first, last, skip, bloc...  5.18 us
    pallas_call x1, Pallas kernels, cut(): pl.pallas_call(functools.partial(cut_kernel, pieces, blocks, carry, endin...  1.8 us
    pallas_call x1, Pallas kernels, open_blocks(): pl.pallas_call(functools.partial(open_kernel, pieces, carry, blocks), out...  1.18 us
    pallas_call x1, Pallas kernels, ends(): pl.pallas_call(functools.partial(ends_kernel, n, across, blocks, at, offs...  1.09 us
    pallas_call x1, Pallas kernels, response_rows(): pl.pallas_call(functools.partial(response_kernel, blocks, scales, skies),...  0.93 us
  transfers between devices with their start and end apart: 15, of which 6 were waited for; matrix products, arithmetic and copies ran while one was open for 0% of the time, Pallas kernels for 23%

profile of v7, /device:TPU:1, one launch (start us, length us, event | category | flops | bytes accessed | tf_op | source)
XLA Modules:
  0.0 45.3 jit_solution(10227160525401021832)
XLA Ops:
  0.0 0.1 collective-permute-start
  0.1 1.2 %open.1 = (f32[2,32,1536]{2,1,0:T(8,128)S(1)}, f32[2,32,128]{2,1,0:T(8,128)S(1)}) custom-call(f32[2,32,12288]{2,1,0:T(8,128)} %legendre_ref.2, f32[2,32,128]{2,1,0:T(8,128)} %cycles_ref.1, f32[1,32]{1,0:T(1,128)} %bitcast.8, s32[2,64]{1,0:T(2,128)} %hits_ref.1, f32[2,64,128]{2,1,0:T(8,128)} %flux_ref.1), custom_call_target="tpu_custom_call" | custom-call | tf_op jit(solution)/shard_map/open/pallas_call | solution.py:159
  1.3 2.6 %collective-permute-start.6 = (f32[2,32,1536]{2,1,0:T(8,128)S(1)}, f32[2,32,1536]{2,1,0:T(8,128)S(1)}, u32[]{:S(2)}, u32[]{:S(2)}) collective-permute-start(f32[2,32,1536]{2,1,0:T(8,128)S(1)} %get-tuple-element.26), channel_id=1, source_target_pairs={{0,3},{1,2},{2,1},{3,0},{4,7},{5,6},{6,5},{7,4},{8,11},{9,10},{10,... | collective-permute-start | bytes 1179656 | tf_op jit(solution)/shard_map/ppermute | solution.py:499
  3.9 1.8 %cut.1 = (f32[2,32,1408]{2,1,0:T(8,128)S(1)}, f32[2,32,1408]{2,1,0:T(8,128)S(1)}, f32[2,32,1280]{2,1,0:T(8,128)S(1)}, f32[2,32,256]{2,1,0:T(8,128)S(1)}, f32[2,3...) custom-call(f32[2,32,12288]{2,1,0:T(8,128)} %legendre_ref.2, ...), custom_call_target="tpu_custom_call" | custom-call | bytes 85196800 | tf_op jit(solution)/shard_map/cut/pallas_call | solution.py:89
  5.7 0.2 collective-permute-start.10
  5.9 1.3 %collective-permute-start.9 = (f32[2,32,1280]{2,1,0:T(8,128)S(1)}, f32[2,32,1280]{2,1,0:T(8,128)S(1)}, u32[]{:S(2)}, u32[]{:S(2)}) collective-permute-start(f32[2,32,1280]{2,1,0:T(8,128)S(1)} %get-tuple-element.36), channel_id=1, source_target_pairs={{0,2},{1,3},{2,0},{3,1},{4,6},{5,7},{6,4},{7,5},{8,10},{9,11},{10,... | collective-permute-start | bytes 983048 | tf_op jit(solution)/shard_map/ppermute | solution.py:499
  7.2 0.7 %collective-permute-start.8 = (f32[2,32,1408]{2,1,0:T(8,128)S(1)}, f32[2,32,1408]{2,1,0:T(8,128)S(1)}, u32[]{:S(2)}, u32[]{:S(2)}) collective-permute-start(f32[2,32,1408]{2,1,0:T(8,128)S(1)} %get-tuple-element.35), channel_id=1, source_target_pairs={{0,3},{1,2},{2,1},{3,0},{4,7},{5,6},{6,5},{7,4},{8,11},{9,10},{10,... | collective-permute-start | bytes 1081352 | tf_op jit(solution)/shard_map/ppermute | solution.py:499
  8.0 5.6 %collective-permute-done.6.refs_3_ = f32[2,32,1536]{2,1,0:T(8,128)S(1)} collective-permute-done((f32[2,32,1536]{2,1,0:T(8,128)S(1)}, f32[2,32,1536]{2,1,0:T(8,128)S(1)}, u32[]{:S(2)}, u32[]{:S(2)}) %collective-permute-start.6) | collective-permute-done | bytes 393248 | tf_op jit(solution)/shard_map/ppermute | solution.py:499
  13.6 0.3 collective-permute-start.5
  13.9 0.9 %collective-permute-done.5.refs_1_ = f32[2,32,128]{2,1,0:T(8,128)S(1)} collective-permute-done((f32[2,32,128]{2,1,0:T(8,128)S(1)}, f32[2,32,128]{2,1,0:T(8,128)S(1)}, u32[]{:S(2)}, u32[]{:S(2)}) %collective-permute-start.5) | collective-permute-done | bytes 32800 | tf_op jit(solution)/shard_map/ppermute | solution.py:499
  14.8 0.3 collective-permute-start.7
  15.1 13.1 %collective-permute-done.9.refs_2_ = f32[2,32,1280]{2,1,0:T(8,128)S(1)} collective-permute-done((f32[2,32,1280]{2,1,0:T(8,128)S(1)}, f32[2,32,1280]{2,1,0:T(8,128)S(1)}, u32[]{:S(2)}, u32[]{:S(2)}) %collective-permute-start.9) | collective-permute-done | bytes 327712 | tf_op jit(solution)/shard_map/ppermute | solution.py:499
  28.2 0.9 %collective-permute-start.1 = (f32[2,32,256]{2,1,0:T(8,128)S(1)}, f32[2,32,256]{2,1,0:T(8,128)S(1)}, u32[]{:S(2)}, u32[]{:S(2)}) collective-permute-start(f32[2,32,256]{2,1,0:T(8,128)S(1)} %get-tuple-element.29), channel_id=1, source_target_pairs={{0,2},{1,3},{2,0},{3,1},{4,6},{5,7},{6,4},{7,5},{8,10},{9,11},{10,... | collective-permute-start | bytes 196616 | tf_op jit(solution)/shard_map/ppermute | solution.py:499
  29.1 1.6 %collective-permute-start.2 = (f32[2,32,256]{2,1,0:T(8,128)S(1)}, f32[2,32,256]{2,1,0:T(8,128)S(1)}, u32[]{:S(2)}, u32[]{:S(2)}) collective-permute-start(f32[2,32,256]{2,1,0:T(8,128)S(1)} %get-tuple-element.30), channel_id=1, source_target_pairs={{0,3},{1,2},{2,1},{3,0},{4,7},{5,6},{6,5},{7,4},{8,11},{9,10},{10,... | collective-permute-start | bytes 196616 | tf_op jit(solution)/shard_map/ppermute | solution.py:499
  30.7 0.0 collective-permute-done.7.refs_2_
  30.7 1.7 %collective-permute-start.3 = (f32[2,32,256]{2,1,0:T(8,128)S(1)}, f32[2,32,256]{2,1,0:T(8,128)S(1)}, u32[]{:S(2)}, u32[]{:S(2)}) collective-permute-start(f32[2,32,256]{2,1,0:T(8,128)S(1)} %get-tuple-element.32), channel_id=1, source_target_pairs={{0,2},{1,3},{2,0},{3,1},{4,6},{5,7},{6,4},{7,5},{8,10},{9,11},{10,... | collective-permute-start | bytes 196616 | tf_op jit(solution)/shard_map/ppermute | solution.py:499
  32.4 0.3 collective-permute-start.4
  32.8 0.9 %response.1 = (f32[8,128]{1,0:T(8,128)S(1)}, s32[8,128]{1,0:T(8,128)S(1)}) custom-call(s32[2]{0:T(128)S(1)} %copy-done.1, f32[8,8,3072]{2,1,0:T(8,128)S(1)} %bitcast.3), custom_call_target="tpu_custom_call" | custom-call | tf_op jit(solution)/shard_map/response/pallas_call | solution.py:210
  33.7 0.1 prepare.1.refs_4_.refs_8_
  33.8 2.5 %chunk.3.refs_6_ = f32[2,128,128]{2,1,0:T(8,128)S(1)} custom-call(s32[8,128]{1,0:T(8,128)S(1)} %get-tuple-element.25.limits_ref, f32[2,32,3072]{2,1,0:T(8,128)S(1)} %get-tuple-element.28.refs_0_, f32[2,32,12288]{2,1,0:T(8,128)S(1)} %collective-permute-done.refs_1_.refs_5_, f32[2,32,1408]{2,1,0:T(8,128)S(1)} %collective-permute-done.10.refs_2_, ...), custom_call_target="tpu_custom_call" | custom-call | tf_op jit(solution)/shard_map/chunk/pallas_call | solution.py:355
  36.4 2.1 %chunk.4.refs_6_ = f32[2,128,128]{2,1,0:T(8,128)S(1)} custom-call(s32[8,128]{1,0:T(8,128)S(1)} %get-tuple-element.25.limits_ref, f32[2,32,3072]{2,1,0:T(8,128)S(1)} %get-tuple-element.28.refs_0_, f32[2,32,12288]{2,1,0:T(8,128)S(1)} %collective-permute-done.refs_1_.refs_5_, f32[2,32,1280]{2,1,0:T(8,128)S(1)} %collective-permute-done.9.refs_2_, ...), custom_call_target="tpu_custom_call" | custom-call | tf_op jit(solution)/shard_map/chunk/pallas_call | solution.py:355
  38.5 0.4 collective-permute-done.2.refs_3_
  38.9 0.6 %chunk.5 = (f32[72,128]{1,0:T(8,128)S(1)}, f32[72,128]{1,0:T(8,128)S(1)}, f32[72,128]{1,0:T(8,128)S(1)}, f32[72,128]{1,0:T(8,128)S(1)}) custom-call(s32[8,128]{1,0:T(8,128)S(1)} %get-tuple-element.25.limits_ref, f32[2,32,3072]{2,1,0:T(8,128)S(1)} %get-tuple-element.28.refs_0_, f32[2,32,12288]{2,1,0:T(8,128)S(1)} %collective-permute-done.refs_1_.refs_5_, ...), custom_call_target="tpu_custom_call" | custom-call | tf_op jit(solution)/shard_map/chunk/pallas_call | solution.py:355
  39.4 1.9 %collective-permute-start.11 = (f32[72,128]{1,0:T(8,128)S(1)}, f32[72,128]{1,0:T(8,128)S(1)}, u32[]{:S(2)}, u32[]{:S(2)}) collective-permute-start(f32[72,128]{1,0:T(8,128)S(1)} %get-tuple-element.41), channel_id=1, source_target_pairs={{0,2},{1,3},{2,0},{3,1},{4,6},{5,7},{6,4},{7,5},{8,10},{9,11},{10,... | collective-permute-start | bytes 110600 | tf_op jit(solution)/shard_map/ppermute | solution.py:499
  41.3 0.1 collective-permute-start.12
  41.4 0.3 collective-permute-start.13
  41.8 1.1 %ends.1 = (f32[72,128]{1,0:T(8,128)S(1)}, f32[64,128]{1,0:T(8,128)S(1)}) custom-call(s32[8,128]{1,0:T(8,128)S(1)} %get-tuple-element.25.limits_ref, f32[2,32,3072]{2,1,0:T(8,128)S(1)} %get-tuple-element.28.refs_0_, f32[2,32,12288]{2,1,0:T(8,128)S(1)} %collective-permute-done.refs_1_.refs_5_, f32[2,32,256]{2,1,0:T(8,128)S(1)} %collective-permute-done.1.refs_2_, ...), custom_call_target="tpu_custom_call" | custom-call | tf_op jit(solution)/shard_map/ends/pallas_call | solution.py:430
  42.9 0.3 collective-permute-start.14
  43.1 1.0 %collective-permute-done.14.refs_4_ = f32[64,128]{1,0:T(8,128)S(1)} collective-permute-done((f32[64,128]{1,0:T(8,128)S(1)}, f32[64,128]{1,0:T(8,128)S(1)}, u32[]{:S(2)}, u32[]{:S(2)}) %collective-permute-start.14) | collective-permute-done | bytes 32800 | tf_op jit(solution)/shard_map/ppermute | solution.py:499
  44.1 0.0 collective-permute-done.11.refs_1_
  44.1 0.5 %collective-permute-done.12.refs_2_ = f32[72,128]{1,0:T(8,128)S(1)} collective-permute-done((f32[72,128]{1,0:T(8,128)S(1)}, f32[72,128]{1,0:T(8,128)S(1)}, u32[]{:S(2)}, u32[]{:S(2)}) %collective-permute-start.12) | collective-permute-done | bytes 36896 | tf_op jit(solution)/shard_map/ppermute | solution.py:499
  44.7 0.6 %finish.1 = f32[2,32,128]{2,1,0:T(8,128)} custom-call(f32[72,128]{1,0:T(8,128)S(1)} %get-tuple-element.40.refs_0_, f32[72,128]{1,0:T(8,128)S(1)} %collective-permute-done.11.refs_1_, f32[72,128]{1,0:T(8,128)S(1)} %collective-permute-done.12.refs_2_, f32[72,128]{1,0:T(8,128)S(1)} %collective-permute-done.13.refs_3_, f32[64,128]{1,0:T(8,128)S(1)} %collective-permute-done.14.refs_4_), custom_call_target="tpu_custom_call" | custom-call | tf_op jit(solution)/shard_map/finish/pallas_call | solution.py:458
  (12 shorter events, 0.0 us)
Async XLA Ops:
  0.0 32.4 %collective-permute-start = (f32[2,32,12288]{2,1,0:T(8,128)}, f32[2,32,12288]{2,1,0:T(8,128)S(1)}, u32[]{:S(2)}, u32[]{:S(2)}) collective-permute-start(f32[2,32,12288]{2,1,0:T(8,128)} %legendre_ref.2), channel_id=1, source_target_pairs={{0,1},{1,0},{2,3},{3,2},{4,5},{5,4},{6,7},{7,6},{8,9},{9,8},{10,11... | collective-permute-start | bytes 9437192 | tf_op jit(solution)/shard_map/ppermute | solution.py:499
  0.1 32.7 %copy-start = (f32[3072,8,8]{0,2,1:T(8,128)S(1)}, f32[3072,8,8]{0,2,1:T(8,128)}, u32[]{:S(2)}) copy-start(f32[3072,8,8]{0,2,1:T(8,128)} %param.10) | copy-start | bytes 2359300
  0.1 32.7 %copy-start.1 = (s32[2]{0:T(128)S(1)}, s32[2]{0:T(128)}, u32[]{:S(2)}) copy-start(s32[2]{0:T(128)} %order_ref.1) | copy-start | bytes 28
  1.3 12.3 %collective-permute-start.6 = (f32[2,32,1536]{2,1,0:T(8,128)S(1)}, f32[2,32,1536]{2,1,0:T(8,128)S(1)}, u32[]{:S(2)}, u32[]{:S(2)}) collective-permute-start(f32[2,32,1536]{2,1,0:T(8,128)S(1)} %get-tuple-element.26), channel_id=1, source_target_pairs={{0,3},{1,2},{2,1},{3,0},{4,7},{5,6},{6,5},{7,4},{8,11},{9,10},{10,... | collective-permute-start | bytes 1179656 | tf_op jit(solution)/shard_map/ppermute | solution.py:499
  5.7 23.4 %collective-permute-start.10 = (f32[2,32,1408]{2,1,0:T(8,128)S(1)}, f32[2,32,1408]{2,1,0:T(8,128)S(1)}, u32[]{:S(2)}, u32[]{:S(2)}) collective-permute-start(f32[2,32,1408]{2,1,0:T(8,128)S(1)} %get-tuple-element.37), channel_id=1, source_target_pairs={{0,2},{1,3},{2,0},{3,1},{4,6},{5,7},{6,4},{7,5},{8,10},{9,11},{10,... | collective-permute-start | bytes 1081352 | tf_op jit(solution)/shard_map/ppermute | solution.py:499
  5.9 22.3 %collective-permute-start.9 = (f32[2,32,1280]{2,1,0:T(8,128)S(1)}, f32[2,32,1280]{2,1,0:T(8,128)S(1)}, u32[]{:S(2)}, u32[]{:S(2)}) collective-permute-start(f32[2,32,1280]{2,1,0:T(8,128)S(1)} %get-tuple-element.36), channel_id=1, source_target_pairs={{0,2},{1,3},{2,0},{3,1},{4,6},{5,7},{6,4},{7,5},{8,10},{9,11},{10,... | collective-permute-start | bytes 983048 | tf_op jit(solution)/shard_map/ppermute | solution.py:499
  7.2 29.1 %collective-permute-start.8 = (f32[2,32,1408]{2,1,0:T(8,128)S(1)}, f32[2,32,1408]{2,1,0:T(8,128)S(1)}, u32[]{:S(2)}, u32[]{:S(2)}) collective-permute-start(f32[2,32,1408]{2,1,0:T(8,128)S(1)} %get-tuple-element.35), channel_id=1, source_target_pairs={{0,3},{1,2},{2,1},{3,0},{4,7},{5,6},{6,5},{7,4},{8,11},{9,10},{10,... | collective-permute-start | bytes 1081352 | tf_op jit(solution)/shard_map/ppermute | solution.py:499
  13.6 1.2 %collective-permute-start.5 = (f32[2,32,128]{2,1,0:T(8,128)S(1)}, f32[2,32,128]{2,1,0:T(8,128)S(1)}, u32[]{:S(2)}, u32[]{:S(2)}) collective-permute-start(f32[2,32,128]{2,1,0:T(8,128)S(1)} %get-tuple-element.34.refs_0_), channel_id=1, source_target_pairs={{0,1},{1,0},{2,3},{3,2},{4,5},{5,4},{6,7},{7,6},{8,9},{9,8},{10,11... | collective-permute-start | bytes 98312 | tf_op jit(solution)/shard_map/ppermute | solution.py:499
  14.8 15.9 %collective-permute-start.7 = (f32[2,32,128]{2,1,0:T(8,128)S(1)}, f32[2,32,128]{2,1,0:T(8,128)S(1)}, u32[]{:S(2)}, u32[]{:S(2)}) collective-permute-start(f32[2,32,128]{2,1,0:T(8,128)S(1)} %slice.4), channel_id=1, source_target_pairs={{0,1},{1,0},{2,3},{3,2},{4,5},{5,4},{6,7},{7,6},{8,9},{9,8},{10,11... | collective-permute-start | bytes 98312 | tf_op jit(solution)/shard_map/ppermute | solution.py:499
  28.2 10.2 %collective-permute-start.1 = (f32[2,32,256]{2,1,0:T(8,128)S(1)}, f32[2,32,256]{2,1,0:T(8,128)S(1)}, u32[]{:S(2)}, u32[]{:S(2)}) collective-permute-start(f32[2,32,256]{2,1,0:T(8,128)S(1)} %get-tuple-element.29), channel_id=1, source_target_pairs={{0,2},{1,3},{2,0},{3,1},{4,6},{5,7},{6,4},{7,5},{8,10},{9,11},{10,... | collective-permute-start | bytes 196616 | tf_op jit(solution)/shard_map/ppermute | solution.py:499
  29.1 9.7 %collective-permute-start.2 = (f32[2,32,256]{2,1,0:T(8,128)S(1)}, f32[2,32,256]{2,1,0:T(8,128)S(1)}, u32[]{:S(2)}, u32[]{:S(2)}) collective-permute-start(f32[2,32,256]{2,1,0:T(8,128)S(1)} %get-tuple-element.30), channel_id=1, source_target_pairs={{0,3},{1,2},{2,1},{3,0},{4,7},{5,6},{6,5},{7,4},{8,11},{9,10},{10,... | collective-permute-start | bytes 196616 | tf_op jit(solution)/shard_map/ppermute | solution.py:499
  30.7 11.0 %collective-permute-start.3 = (f32[2,32,256]{2,1,0:T(8,128)S(1)}, f32[2,32,256]{2,1,0:T(8,128)S(1)}, u32[]{:S(2)}, u32[]{:S(2)}) collective-permute-start(f32[2,32,256]{2,1,0:T(8,128)S(1)} %get-tuple-element.32), channel_id=1, source_target_pairs={{0,2},{1,3},{2,0},{3,1},{4,6},{5,7},{6,4},{7,5},{8,10},{9,11},{10,... | collective-permute-start | bytes 196616 | tf_op jit(solution)/shard_map/ppermute | solution.py:499
  32.4 9.3 %collective-permute-start.4 = (f32[2,32,256]{2,1,0:T(8,128)S(1)}, f32[2,32,256]{2,1,0:T(8,128)S(1)}, u32[]{:S(2)}, u32[]{:S(2)}) collective-permute-start(f32[2,32,256]{2,1,0:T(8,128)S(1)} %get-tuple-element.33), channel_id=1, source_target_pairs={{0,3},{1,2},{2,1},{3,0},{4,7},{5,6},{6,5},{7,4},{8,11},{9,10},{10,... | collective-permute-start | bytes 196616 | tf_op jit(solution)/shard_map/ppermute | solution.py:499
  39.4 4.7 %collective-permute-start.11 = (f32[72,128]{1,0:T(8,128)S(1)}, f32[72,128]{1,0:T(8,128)S(1)}, u32[]{:S(2)}, u32[]{:S(2)}) collective-permute-start(f32[72,128]{1,0:T(8,128)S(1)} %get-tuple-element.41), channel_id=1, source_target_pairs={{0,2},{1,3},{2,0},{3,1},{4,6},{5,7},{6,4},{7,5},{8,10},{9,11},{10,... | collective-permute-start | bytes 110600 | tf_op jit(solution)/shard_map/ppermute | solution.py:499
  41.3 3.4 %collective-permute-start.12 = (f32[72,128]{1,0:T(8,128)S(1)}, f32[72,128]{1,0:T(8,128)S(1)}, u32[]{:S(2)}, u32[]{:S(2)}) collective-permute-start(f32[72,128]{1,0:T(8,128)S(1)} %get-tuple-element.42), channel_id=1, source_target_pairs={{0,3},{1,2},{2,1},{3,0},{4,7},{5,6},{6,5},{7,4},{8,11},{9,10},{10,... | collective-permute-start | bytes 110600 | tf_op jit(solution)/shard_map/ppermute | solution.py:499
  41.4 3.2 %collective-permute-start.13 = (f32[72,128]{1,0:T(8,128)S(1)}, f32[72,128]{1,0:T(8,128)S(1)}, u32[]{:S(2)}, u32[]{:S(2)}) collective-permute-start(f32[72,128]{1,0:T(8,128)S(1)} %get-tuple-element.43), channel_id=1, source_target_pairs={{0,1},{1,0},{2,3},{3,2},{4,5},{5,4},{6,7},{7,6},{8,9},{9,8},{10,11... | collective-permute-start | bytes 110600 | tf_op jit(solution)/shard_map/ppermute | solution.py:499
  42.9 1.3 %collective-permute-start.14 = (f32[64,128]{1,0:T(8,128)S(1)}, f32[64,128]{1,0:T(8,128)S(1)}, u32[]{:S(2)}, u32[]{:S(2)}) collective-permute-start(f32[64,128]{1,0:T(8,128)S(1)} %get-tuple-element.44), channel_id=1, source_target_pairs={{0,1},{1,0},{2,3},{3,2},{4,5},{5,4},{6,7},{7,6},{8,9},{9,8},{10,11... | collective-permute-start | bytes 98312 | tf_op jit(solution)/shard_map/ppermute | solution.py:499

commit v8 on v7

--- a/solution.py
+++ b/solution.py
@@ -247,16 +247,23 @@
     )(*[array for array, _ in pieces])
 
 
-def tile_sum(values, analysis, weights, keep, rows):
+def tile_sum(values, analysis, weights, keep, rows, stacked=False):
     scales, channels = len(weights), len(weights[0])
     columns = analysis.shape[0]
     skies = columns // (2 * channels)
     high, low = halves(values)
-    harmonics = jnp.dot(
-        analysis,
-        jnp.concatenate([high, high, low], axis=0),
-        preferred_element_type=jnp.float32,
-    )
+    cycles = high.shape[0]
+    if stacked:
+        terms = jnp.concatenate([analysis[:, :cycles], analysis[:, cycles : 2 * cycles]], axis=0)
+        both = jnp.dot(terms, high, preferred_element_type=jnp.float32)
+        rest = jnp.dot(analysis[:, :cycles], low, preferred_element_type=jnp.float32)
+        harmonics = (rest + both[columns:]) + both[:columns]
+    else:
+        harmonics = jnp.dot(
+            analysis,
+            jnp.concatenate([high, high, low], axis=0),
+            preferred_element_type=jnp.float32,
+        )
     harmonics = jnp.where(keep, harmonics, 0.0)
     matched = []
     for p in range(2):
@@ -314,7 +321,7 @@
                 axis=0,
             )
             keep = degree >= limits_ref[k : k + 1, :1]
-            product = tile_sum(values, analysis_ref[k], weights, keep, slice(skip * rows, n * rows))
+            product = tile_sum(values, analysis_ref[k], weights, keep, slice(skip * rows, n * rows), not last)
             totals[k] = product if totals[k] is None else totals[k] + product
         at += tile
 
@@ -444,13 +451,18 @@
 
 
 def finish_kernel(degrees, *refs):
-    parts, out_ref = refs[:-1], refs[-1]
+    *parts, out_ref, done, sems = refs
     orders, rows, _ = out_ref.shape
+    copies = []
     for k in range(orders):
         total = sum(part[k * rows : (k + 1) * rows, :] for part in parts)
         at = orders * rows + k
         response = sum(part[at : at + 1, :] for part in parts if part.shape[0] > orders * rows)
-        out_ref[k] = total * (degrees / jnp.sqrt(response))
+        done[k] = total * (degrees / jnp.sqrt(response))
+        copies.append(pltpu.make_async_copy(done.at[k], out_ref.at[k], sems.at[k]))
+        copies[-1].start()
+    for copy in copies:
+        copy.wait()
 
 
 def finish(parts, shape, degrees):
@@ -459,7 +471,8 @@
         functools.partial(finish_kernel, degrees),
         out_shape=jax.ShapeDtypeStruct(shape, jnp.float32),
         in_specs=[vmem] * len(parts),
-        out_specs=vmem,
+        out_specs=pl.BlockSpec(memory_space=pltpu.HBM),
+        scratch_shapes=[pltpu.VMEM(shape, jnp.float32), pltpu.SemaphoreType.DMA((shape[0],))],
         compiler_params=compiler_params(),
         cost_estimate=FREE,
         name="finish",

time: 45.5 us -> 45.5 us (level)
  Pallas kernels: 10.9 us -> 10.4 us
  waiting for transfers between devices: 21.6 us -> 22.1 us
    ppermute x15, waiting for transfers between devices: 21.6 us -> 22.1 us  [send(): return lax.ppermute(value, 'blk', partner(x, n))]
    pallas_call x3, Pallas kernels: 5.18 us -> 4.62 us  [chunk(): pl.pallas_call(functools.partial(chunk_kernel, n, first, last, skip, bloc...]
  transfers between devices with their start and end apart: 15 -> 15, of which waited for: 6 -> 7; matrix products, arithmetic and copies ran while one was open for 0% -> 0% of each run, Pallas kernels for 23% -> 21%
where the time goes in v8:
time: 45.5 us; the launch traced here: 45.3 us
  waiting for transfers between devices  22.1 us (49%)
  starting transfers between devices  12.8 us (28%)
  Pallas kernels  10.4 us (23%)
    ppermute x15, waiting for transfers between devices, send(): return lax.ppermute(value, 'blk', partner(x, n))  22.1 us
    ppermute x15, starting transfers between devices, send(): return lax.ppermute(value, 'blk', partner(x, n))  12.8 us
    pallas_call x3, Pallas kernels, chunk(): pl.pallas_call(functools.partial(chunk_kernel, n, first, last, skip, bloc...  4.62 us
    pallas_call x1, Pallas kernels, cut(): pl.pallas_call(functools.partial(cut_kernel, pieces, blocks, carry, endin...  1.8 us
    pallas_call x1, Pallas kernels, open_blocks(): pl.pallas_call(functools.partial(open_kernel, pieces, carry, blocks), out...  1.18 us
    pallas_call x1, Pallas kernels, ends(): pl.pallas_call(functools.partial(ends_kernel, n, across, blocks, at, offs...  1.09 us
    pallas_call x1, Pallas kernels, response_rows(): pl.pallas_call(functools.partial(response_kernel, blocks, scales, skies),...  0.93 us
  transfers between devices with their start and end apart: 15, of which 7 were waited for; matrix products, arithmetic and copies ran while one was open for 0% of the time, Pallas kernels for 21%

profile of v8, /device:TPU:1, one launch (start us, length us, event | category | flops | bytes accessed | tf_op | source)
XLA Modules:
  0.0 45.3 jit_solution(1231535052257848903)
XLA Ops:
  0.0 0.1 collective-permute-start
  0.1 1.2 %open.1 = (f32[2,32,1536]{2,1,0:T(8,128)S(1)}, f32[2,32,128]{2,1,0:T(8,128)S(1)}) custom-call(f32[2,32,12288]{2,1,0:T(8,128)} %legendre_ref.2, f32[2,32,128]{2,1,0:T(8,128)} %cycles_ref.1, f32[1,32]{1,0:T(1,128)} %bitcast.8, s32[2,64]{1,0:T(2,128)} %hits_ref.1, f32[2,64,128]{2,1,0:T(8,128)} %flux_ref.1), custom_call_target="tpu_custom_call" | custom-call | tf_op jit(solution)/shard_map/open/pallas_call | solution.py:159
  1.3 2.6 %collective-permute-start.6 = (f32[2,32,1536]{2,1,0:T(8,128)S(1)}, f32[2,32,1536]{2,1,0:T(8,128)S(1)}, u32[]{:S(2)}, u32[]{:S(2)}) collective-permute-start(f32[2,32,1536]{2,1,0:T(8,128)S(1)} %get-tuple-element.26), channel_id=1, source_target_pairs={{0,3},{1,2},{2,1},{3,0},{4,7},{5,6},{6,5},{7,4},{8,11},{9,10},{10,... | collective-permute-start | bytes 1179656 | tf_op jit(solution)/shard_map/ppermute | solution.py:512
  3.9 1.8 %cut.1 = (f32[2,32,1408]{2,1,0:T(8,128)S(1)}, f32[2,32,1408]{2,1,0:T(8,128)S(1)}, f32[2,32,1280]{2,1,0:T(8,128)S(1)}, f32[2,32,256]{2,1,0:T(8,128)S(1)}, f32[2,3...) custom-call(f32[2,32,12288]{2,1,0:T(8,128)} %legendre_ref.2, ...), custom_call_target="tpu_custom_call" | custom-call | bytes 85196800 | tf_op jit(solution)/shard_map/cut/pallas_call | solution.py:89
  5.7 0.2 collective-permute-start.10
  5.9 1.3 %collective-permute-start.9 = (f32[2,32,1280]{2,1,0:T(8,128)S(1)}, f32[2,32,1280]{2,1,0:T(8,128)S(1)}, u32[]{:S(2)}, u32[]{:S(2)}) collective-permute-start(f32[2,32,1280]{2,1,0:T(8,128)S(1)} %get-tuple-element.36), channel_id=1, source_target_pairs={{0,2},{1,3},{2,0},{3,1},{4,6},{5,7},{6,4},{7,5},{8,10},{9,11},{10,... | collective-permute-start | bytes 983048 | tf_op jit(solution)/shard_map/ppermute | solution.py:512
  7.2 0.7 %collective-permute-start.8 = (f32[2,32,1408]{2,1,0:T(8,128)S(1)}, f32[2,32,1408]{2,1,0:T(8,128)S(1)}, u32[]{:S(2)}, u32[]{:S(2)}) collective-permute-start(f32[2,32,1408]{2,1,0:T(8,128)S(1)} %get-tuple-element.35), channel_id=1, source_target_pairs={{0,3},{1,2},{2,1},{3,0},{4,7},{5,6},{6,5},{7,4},{8,11},{9,10},{10,... | collective-permute-start | bytes 1081352 | tf_op jit(solution)/shard_map/ppermute | solution.py:512
  8.0 5.6 %collective-permute-done.6.refs_3_ = f32[2,32,1536]{2,1,0:T(8,128)S(1)} collective-permute-done((f32[2,32,1536]{2,1,0:T(8,128)S(1)}, f32[2,32,1536]{2,1,0:T(8,128)S(1)}, u32[]{:S(2)}, u32[]{:S(2)}) %collective-permute-start.6) | collective-permute-done | bytes 393248 | tf_op jit(solution)/shard_map/ppermute | solution.py:512
  13.6 0.3 collective-permute-start.5
  13.9 0.9 %collective-permute-done.5.refs_1_ = f32[2,32,128]{2,1,0:T(8,128)S(1)} collective-permute-done((f32[2,32,128]{2,1,0:T(8,128)S(1)}, f32[2,32,128]{2,1,0:T(8,128)S(1)}, u32[]{:S(2)}, u32[]{:S(2)}) %collective-permute-start.5) | collective-permute-done | bytes 32800 | tf_op jit(solution)/shard_map/ppermute | solution.py:512
  14.8 0.3 collective-permute-start.7
  15.1 13.1 %collective-permute-done.9.refs_2_ = f32[2,32,1280]{2,1,0:T(8,128)S(1)} collective-permute-done((f32[2,32,1280]{2,1,0:T(8,128)S(1)}, f32[2,32,1280]{2,1,0:T(8,128)S(1)}, u32[]{:S(2)}, u32[]{:S(2)}) %collective-permute-start.9) | collective-permute-done | bytes 327712 | tf_op jit(solution)/shard_map/ppermute | solution.py:512
  28.2 0.9 %collective-permute-start.1 = (f32[2,32,256]{2,1,0:T(8,128)S(1)}, f32[2,32,256]{2,1,0:T(8,128)S(1)}, u32[]{:S(2)}, u32[]{:S(2)}) collective-permute-start(f32[2,32,256]{2,1,0:T(8,128)S(1)} %get-tuple-element.29), channel_id=1, source_target_pairs={{0,2},{1,3},{2,0},{3,1},{4,6},{5,7},{6,4},{7,5},{8,10},{9,11},{10,... | collective-permute-start | bytes 196616 | tf_op jit(solution)/shard_map/ppermute | solution.py:512
  29.1 0.0 collective-permute-done.10.refs_2_
  29.1 1.6 %collective-permute-start.2 = (f32[2,32,256]{2,1,0:T(8,128)S(1)}, f32[2,32,256]{2,1,0:T(8,128)S(1)}, u32[]{:S(2)}, u32[]{:S(2)}) collective-permute-start(f32[2,32,256]{2,1,0:T(8,128)S(1)} %get-tuple-element.30), channel_id=1, source_target_pairs={{0,3},{1,2},{2,1},{3,0},{4,7},{5,6},{6,5},{7,4},{8,11},{9,10},{10,... | collective-permute-start | bytes 196616 | tf_op jit(solution)/shard_map/ppermute | solution.py:512
  30.7 1.7 %collective-permute-start.3 = (f32[2,32,256]{2,1,0:T(8,128)S(1)}, f32[2,32,256]{2,1,0:T(8,128)S(1)}, u32[]{:S(2)}, u32[]{:S(2)}) collective-permute-start(f32[2,32,256]{2,1,0:T(8,128)S(1)} %get-tuple-element.32), channel_id=1, source_target_pairs={{0,2},{1,3},{2,0},{3,1},{4,6},{5,7},{6,4},{7,5},{8,10},{9,11},{10,... | collective-permute-start | bytes 196616 | tf_op jit(solution)/shard_map/ppermute | solution.py:512
  32.4 0.3 collective-permute-start.4
  32.8 0.9 %response.1 = (f32[8,128]{1,0:T(8,128)S(1)}, s32[8,128]{1,0:T(8,128)S(1)}) custom-call(s32[2]{0:T(128)S(1)} %copy-done.1, f32[8,8,3072]{2,1,0:T(8,128)S(1)} %bitcast.3), custom_call_target="tpu_custom_call" | custom-call | tf_op jit(solution)/shard_map/response/pallas_call | solution.py:210
  33.7 0.1 prepare.1.refs_4_.refs_8_
  33.8 2.1 %chunk.3.refs_6_ = f32[2,128,128]{2,1,0:T(8,128)S(1)} custom-call(s32[8,128]{1,0:T(8,128)S(1)} %get-tuple-element.25.limits_ref, f32[2,32,3072]{2,1,0:T(8,128)S(1)} %get-tuple-element.28.refs_0_, f32[2,32,12288]{2,1,0:T(8,128)S(1)} %collective-permute-done.refs_1_.refs_5_, f32[2,32,1408]{2,1,0:T(8,128)S(1)} %collective-permute-done.10.refs_2_, ...), custom_call_target="tpu_custom_call" | custom-call | tf_op jit(solution)/shard_map/chunk/pallas_call | solution.py:362
  35.9 0.1 collective-permute-done.8.refs_3_.refs_10_
  36.0 2.0 %chunk.4.refs_6_ = f32[2,128,128]{2,1,0:T(8,128)S(1)} custom-call(s32[8,128]{1,0:T(8,128)S(1)} %get-tuple-element.25.limits_ref, f32[2,32,3072]{2,1,0:T(8,128)S(1)} %get-tuple-element.28.refs_0_, f32[2,32,12288]{2,1,0:T(8,128)S(1)} %collective-permute-done.refs_1_.refs_5_, f32[2,32,1280]{2,1,0:T(8,128)S(1)} %collective-permute-done.9.refs_2_, ...), custom_call_target="tpu_custom_call" | custom-call | tf_op jit(solution)/shard_map/chunk/pallas_call | solution.py:362
  38.0 0.8 %collective-permute-done.2.refs_3_ = f32[2,32,256]{2,1,0:T(8,128)S(1)} collective-permute-done((f32[2,32,256]{2,1,0:T(8,128)S(1)}, f32[2,32,256]{2,1,0:T(8,128)S(1)}, u32[]{:S(2)}, u32[]{:S(2)}) %collective-permute-start.2) | collective-permute-done | bytes 65568 | tf_op jit(solution)/shard_map/ppermute | solution.py:512
  38.9 0.6 %chunk.5 = (f32[72,128]{1,0:T(8,128)S(1)}, f32[72,128]{1,0:T(8,128)S(1)}, f32[72,128]{1,0:T(8,128)S(1)}, f32[72,128]{1,0:T(8,128)S(1)}) custom-call(s32[8,128]{1,0:T(8,128)S(1)} %get-tuple-element.25.limits_ref, f32[2,32,3072]{2,1,0:T(8,128)S(1)} %get-tuple-element.28.refs_0_, f32[2,32,12288]{2,1,0:T(8,128)S(1)} %collective-permute-done.refs_1_.refs_5_, ...), custom_call_target="tpu_custom_call" | custom-call | tf_op jit(solution)/shard_map/chunk/pallas_call | solution.py:362
  39.4 1.9 %collective-permute-start.11 = (f32[72,128]{1,0:T(8,128)S(1)}, f32[72,128]{1,0:T(8,128)S(1)}, u32[]{:S(2)}, u32[]{:S(2)}) collective-permute-start(f32[72,128]{1,0:T(8,128)S(1)} %get-tuple-element.41), channel_id=1, source_target_pairs={{0,2},{1,3},{2,0},{3,1},{4,6},{5,7},{6,4},{7,5},{8,10},{9,11},{10,... | collective-permute-start | bytes 110600 | tf_op jit(solution)/shard_map/ppermute | solution.py:512
  41.3 0.1 collective-permute-start.12
  41.4 0.3 collective-permute-start.13
  41.8 1.1 %ends.1 = (f32[72,128]{1,0:T(8,128)S(1)}, f32[64,128]{1,0:T(8,128)S(1)}) custom-call(s32[8,128]{1,0:T(8,128)S(1)} %get-tuple-element.25.limits_ref, f32[2,32,3072]{2,1,0:T(8,128)S(1)} %get-tuple-element.28.refs_0_, f32[2,32,12288]{2,1,0:T(8,128)S(1)} %collective-permute-done.refs_1_.refs_5_, f32[2,32,256]{2,1,0:T(8,128)S(1)} %collective-permute-done.1.refs_2_, ...), custom_call_target="tpu_custom_call" | custom-call | tf_op jit(solution)/shard_map/ends/pallas_call | solution.py:437
  42.9 0.3 collective-permute-start.14
  43.1 1.0 %collective-permute-done.14.refs_4_ = f32[64,128]{1,0:T(8,128)S(1)} collective-permute-done((f32[64,128]{1,0:T(8,128)S(1)}, f32[64,128]{1,0:T(8,128)S(1)}, u32[]{:S(2)}, u32[]{:S(2)}) %collective-permute-start.14) | collective-permute-done | bytes 32800 | tf_op jit(solution)/shard_map/ppermute | solution.py:512
  44.1 0.5 %collective-permute-done.12.refs_2_ = f32[72,128]{1,0:T(8,128)S(1)} collective-permute-done((f32[72,128]{1,0:T(8,128)S(1)}, f32[72,128]{1,0:T(8,128)S(1)}, u32[]{:S(2)}, u32[]{:S(2)}) %collective-permute-start.12) | collective-permute-done | bytes 36896 | tf_op jit(solution)/shard_map/ppermute | solution.py:512
  44.7 0.7 %finish.1 = f32[2,32,128]{2,1,0:T(8,128)} custom-call(f32[72,128]{1,0:T(8,128)S(1)} %get-tuple-element.40.refs_0_, f32[72,128]{1,0:T(8,128)S(1)} %collective-permute-done.11.refs_1_, f32[72,128]{1,0:T(8,128)S(1)} %collective-permute-done.12.refs_2_, f32[72,128]{1,0:T(8,128)S(1)} %collective-permute-done.13.refs_3_, f32[64,128]{1,0:T(8,128)S(1)} %collective-permute-done.14.refs_4_), custom_call_target="tpu_custom_call" | custom-call | tf_op jit(solution)/shard_map/finish/pallas_call | solution.py:470
  (12 shorter events, 0.0 us)
Async XLA Ops:
  0.0 32.4 %collective-permute-start = (f32[2,32,12288]{2,1,0:T(8,128)}, f32[2,32,12288]{2,1,0:T(8,128)S(1)}, u32[]{:S(2)}, u32[]{:S(2)}) collective-permute-start(f32[2,32,12288]{2,1,0:T(8,128)} %legendre_ref.2), channel_id=1, source_target_pairs={{0,1},{1,0},{2,3},{3,2},{4,5},{5,4},{6,7},{7,6},{8,9},{9,8},{10,11... | collective-permute-start | bytes 9437192 | tf_op jit(solution)/shard_map/ppermute | solution.py:512
  0.1 32.7 %copy-start = (f32[3072,8,8]{0,2,1:T(8,128)S(1)}, f32[3072,8,8]{0,2,1:T(8,128)}, u32[]{:S(2)}) copy-start(f32[3072,8,8]{0,2,1:T(8,128)} %param.10) | copy-start | bytes 2359300
  0.1 32.7 %copy-start.1 = (s32[2]{0:T(128)S(1)}, s32[2]{0:T(128)}, u32[]{:S(2)}) copy-start(s32[2]{0:T(128)} %order_ref.1) | copy-start | bytes 28
  1.3 12.3 %collective-permute-start.6 = (f32[2,32,1536]{2,1,0:T(8,128)S(1)}, f32[2,32,1536]{2,1,0:T(8,128)S(1)}, u32[]{:S(2)}, u32[]{:S(2)}) collective-permute-start(f32[2,32,1536]{2,1,0:T(8,128)S(1)} %get-tuple-element.26), channel_id=1, source_target_pairs={{0,3},{1,2},{2,1},{3,0},{4,7},{5,6},{6,5},{7,4},{8,11},{9,10},{10,... | collective-permute-start | bytes 1179656 | tf_op jit(solution)/shard_map/ppermute | solution.py:512
  5.7 23.4 %collective-permute-start.10 = (f32[2,32,1408]{2,1,0:T(8,128)S(1)}, f32[2,32,1408]{2,1,0:T(8,128)S(1)}, u32[]{:S(2)}, u32[]{:S(2)}) collective-permute-start(f32[2,32,1408]{2,1,0:T(8,128)S(1)} %get-tuple-element.37), channel_id=1, source_target_pairs={{0,2},{1,3},{2,0},{3,1},{4,6},{5,7},{6,4},{7,5},{8,10},{9,11},{10,... | collective-permute-start | bytes 1081352 | tf_op jit(solution)/shard_map/ppermute | solution.py:512
  5.9 22.3 %collective-permute-start.9 = (f32[2,32,1280]{2,1,0:T(8,128)S(1)}, f32[2,32,1280]{2,1,0:T(8,128)S(1)}, u32[]{:S(2)}, u32[]{:S(2)}) collective-permute-start(f32[2,32,1280]{2,1,0:T(8,128)S(1)} %get-tuple-element.36), channel_id=1, source_target_pairs={{0,2},{1,3},{2,0},{3,1},{4,6},{5,7},{6,4},{7,5},{8,10},{9,11},{10,... | collective-permute-start | bytes 983048 | tf_op jit(solution)/shard_map/ppermute | solution.py:512
  7.2 28.8 %collective-permute-start.8 = (f32[2,32,1408]{2,1,0:T(8,128)S(1)}, f32[2,32,1408]{2,1,0:T(8,128)S(1)}, u32[]{:S(2)}, u32[]{:S(2)}) collective-permute-start(f32[2,32,1408]{2,1,0:T(8,128)S(1)} %get-tuple-element.35), channel_id=1, source_target_pairs={{0,3},{1,2},{2,1},{3,0},{4,7},{5,6},{6,5},{7,4},{8,11},{9,10},{10,... | collective-permute-start | bytes 1081352 | tf_op jit(solution)/shard_map/ppermute | solution.py:512
  13.6 1.2 %collective-permute-start.5 = (f32[2,32,128]{2,1,0:T(8,128)S(1)}, f32[2,32,128]{2,1,0:T(8,128)S(1)}, u32[]{:S(2)}, u32[]{:S(2)}) collective-permute-start(f32[2,32,128]{2,1,0:T(8,128)S(1)} %get-tuple-element.34.refs_0_), channel_id=1, source_target_pairs={{0,1},{1,0},{2,3},{3,2},{4,5},{5,4},{6,7},{7,6},{8,9},{9,8},{10,11... | collective-permute-start | bytes 98312 | tf_op jit(solution)/shard_map/ppermute | solution.py:512
  14.8 15.9 %collective-permute-start.7 = (f32[2,32,128]{2,1,0:T(8,128)S(1)}, f32[2,32,128]{2,1,0:T(8,128)S(1)}, u32[]{:S(2)}, u32[]{:S(2)}) collective-permute-start(f32[2,32,128]{2,1,0:T(8,128)S(1)} %slice.4), channel_id=1, source_target_pairs={{0,1},{1,0},{2,3},{3,2},{4,5},{5,4},{6,7},{7,6},{8,9},{9,8},{10,11... | collective-permute-start | bytes 98312 | tf_op jit(solution)/shard_map/ppermute | solution.py:512
  28.2 9.8 %collective-permute-start.1 = (f32[2,32,256]{2,1,0:T(8,128)S(1)}, f32[2,32,256]{2,1,0:T(8,128)S(1)}, u32[]{:S(2)}, u32[]{:S(2)}) collective-permute-start(f32[2,32,256]{2,1,0:T(8,128)S(1)} %get-tuple-element.29), channel_id=1, source_target_pairs={{0,2},{1,3},{2,0},{3,1},{4,6},{5,7},{6,4},{7,5},{8,10},{9,11},{10,... | collective-permute-start | bytes 196616 | tf_op jit(solution)/shard_map/ppermute | solution.py:512
  29.1 9.7 %collective-permute-start.2 = (f32[2,32,256]{2,1,0:T(8,128)S(1)}, f32[2,32,256]{2,1,0:T(8,128)S(1)}, u32[]{:S(2)}, u32[]{:S(2)}) collective-permute-start(f32[2,32,256]{2,1,0:T(8,128)S(1)} %get-tuple-element.30), channel_id=1, source_target_pairs={{0,3},{1,2},{2,1},{3,0},{4,7},{5,6},{6,5},{7,4},{8,11},{9,10},{10,... | collective-permute-start | bytes 196616 | tf_op jit(solution)/shard_map/ppermute | solution.py:512
  30.7 11.0 %collective-permute-start.3 = (f32[2,32,256]{2,1,0:T(8,128)S(1)}, f32[2,32,256]{2,1,0:T(8,128)S(1)}, u32[]{:S(2)}, u32[]{:S(2)}) collective-permute-start(f32[2,32,256]{2,1,0:T(8,128)S(1)} %get-tuple-element.32), channel_id=1, source_target_pairs={{0,2},{1,3},{2,0},{3,1},{4,6},{5,7},{6,4},{7,5},{8,10},{9,11},{10,... | collective-permute-start | bytes 196616 | tf_op jit(solution)/shard_map/ppermute | solution.py:512
  32.4 9.3 %collective-permute-start.4 = (f32[2,32,256]{2,1,0:T(8,128)S(1)}, f32[2,32,256]{2,1,0:T(8,128)S(1)}, u32[]{:S(2)}, u32[]{:S(2)}) collective-permute-start(f32[2,32,256]{2,1,0:T(8,128)S(1)} %get-tuple-element.33), channel_id=1, source_target_pairs={{0,3},{1,2},{2,1},{3,0},{4,7},{5,6},{6,5},{7,4},{8,11},{9,10},{10,... | collective-permute-start | bytes 196616 | tf_op jit(solution)/shard_map/ppermute | solution.py:512
  39.4 4.7 %collective-permute-start.11 = (f32[72,128]{1,0:T(8,128)S(1)}, f32[72,128]{1,0:T(8,128)S(1)}, u32[]{:S(2)}, u32[]{:S(2)}) collective-permute-start(f32[72,128]{1,0:T(8,128)S(1)} %get-tuple-element.41), channel_id=1, source_target_pairs={{0,2},{1,3},{2,0},{3,1},{4,6},{5,7},{6,4},{7,5},{8,10},{9,11},{10,... | collective-permute-start | bytes 110600 | tf_op jit(solution)/shard_map/ppermute | solution.py:512
  41.3 3.4 %collective-permute-start.12 = (f32[72,128]{1,0:T(8,128)S(1)}, f32[72,128]{1,0:T(8,128)S(1)}, u32[]{:S(2)}, u32[]{:S(2)}) collective-permute-start(f32[72,128]{1,0:T(8,128)S(1)} %get-tuple-element.42), channel_id=1, source_target_pairs={{0,3},{1,2},{2,1},{3,0},{4,7},{5,6},{6,5},{7,4},{8,11},{9,10},{10,... | collective-permute-start | bytes 110600 | tf_op jit(solution)/shard_map/ppermute | solution.py:512
  41.4 3.2 %collective-permute-start.13 = (f32[72,128]{1,0:T(8,128)S(1)}, f32[72,128]{1,0:T(8,128)S(1)}, u32[]{:S(2)}, u32[]{:S(2)}) collective-permute-start(f32[72,128]{1,0:T(8,128)S(1)} %get-tuple-element.43), channel_id=1, source_target_pairs={{0,1},{1,0},{2,3},{3,2},{4,5},{5,4},{6,7},{7,6},{8,9},{9,8},{10,11... | collective-permute-start | bytes 110600 | tf_op jit(solution)/shard_map/ppermute | solution.py:512
  42.9 1.3 %collective-permute-start.14 = (f32[64,128]{1,0:T(8,128)S(1)}, f32[64,128]{1,0:T(8,128)S(1)}, u32[]{:S(2)}, u32[]{:S(2)}) collective-permute-start(f32[64,128]{1,0:T(8,128)S(1)} %get-tuple-element.44), channel_id=1, source_target_pairs={{0,1},{1,0},{2,3},{3,2},{4,5},{5,4},{6,7},{7,6},{8,9},{9,8},{10,11... | collective-permute-start | bytes 98312 | tf_op jit(solution)/shard_map/ppermute | solution.py:512
